TPU v7x, 128 devices: a whole 4x4x4 slice. The times are simulated.
128 devices in a mesh: node: 8 (over y, core), cores: 16 (over z, x).
Axes of the slice: x: 4, y: 4, z: 4, core: 2. Of those that a mesh axis runs over, the one named last changes fastest.
Arguments:
- adjoint: bfloat16 [1024, 2, 128, 128], P(('node', 'cores')), may hold values from -6 to 6
- saved: bfloat16 [2, 4, 1024, 2, 128, 128], P(None, None, ('node', 'cores')), may hold values from -0.046875 to 0.046875
- propagators: bfloat16 [2, 4, 2, 128, 128], replicated, may hold values from -3 to 3, as said below
- coupling: bfloat16 [128, 128], replicated, may hold values from -0.5 to 0.5
- higher: int32 [1024, 4], replicated, may hold values from 0 to 1023, as said below
- lower: int32 [1024, 4], replicated, may hold values from 0 to 1023, as said below
- ladder: int32 [2, 1024, 4], P(None, ('node', 'cores')), may hold values from 0 to 3
- rates: float32 [2, 4], replicated, may hold values from 0.1 to 0.4
- decay: float32 [1024], P(('node', 'cores')), may hold values from 0.4 to 1
Outputs:
- adjoint_out: bfloat16 [1024, 2, 128, 128], P(('node', 'cores'))
- gradient: float32 [128, 8, 2, 128], P(('node', 'cores'))
Inputs may be any that keep to these rules, and one draw needn't show every extreme that they name: Density j lives on owner j // 8. Taken in the order of density then mode, the 32 higher-tier partners of one owner's densities lie on distinct owners when 8 * 4 <= 128, and else exactly 1 of them lie on each owner. The same holds for the lower-tier partners. `propagators`: A propagator substep is close to unitary.
All inputs are finite; a program needn't handle non-finite values.
Results may differ from a plain program's by a relative error of at most 0.024.
Values may be sent and summed in bfloat16 or wider, within the bound.
No kernel may reach another device: no remote copies, remote signals or barrier semaphores. Data moves between devices by JAX's collectives and lax.ppermute only.
A program may use at most 128 MiB of HBM per device.

v0:
```python
import jax
import jax.numpy as jnp
from jax import lax
from jax.sharding import Mesh
from jax.sharding import PartitionSpec as P

NODE_CORES = ("node_0", "node_1", "cores_0", "cores_1")


def cut_along(x, dim, length):
    dims = x.shape
    tiles = x.reshape(*dims[:dim], length, dims[dim] // length, *dims[dim + 1 :])
    return jnp.moveaxis(tiles, dim, 0)


def sent_and_summed(x, axis, dim):
    length = lax.axis_size(axis)
    tiles = lax.all_to_all(cut_along(x, dim, length), axis, 0, 0, tiled=True)
    return jnp.sum(tiles, axis=0)


def sum_in_two_steps(x, axes, dim):
    far, near = axes
    tiles = cut_along(x, dim, lax.axis_size(far))
    nearer = sent_and_summed(tiles, near, dim + 1)
    arrived = lax.all_to_all(nearer, far, split_axis=0, concat_axis=0, tiled=True)
    return arrived.sum(axis=0)


def send_slots(link_table, owners, own_index, own_count, links, capacity):
    flattened = link_table.reshape(owners, links)
    source = flattened // own_count
    local = flattened % own_count
    mine = (source == own_index).astype(jnp.int32)
    before = jnp.cumsum(mine, axis=1) - mine
    picked = [jnp.sum(jnp.where((mine == 1) & (before == 0), local, 0), axis=1)]
    return jnp.stack(picked, axis=1).reshape(owners * capacity)


def receive_slots(link_table, own_index, own_count, links, capacity):
    own_rows = lax.dynamic_slice_in_dim(link_table, own_index * own_count, own_count, 0).reshape(
        links
    )
    source = own_rows // own_count
    positions = jnp.arange(links)
    earlier = (source[:, None] == source[None, :]) & (positions[None, :] < positions[:, None])
    before = jnp.sum(earlier.astype(jnp.int32), axis=1)
    return source * capacity + before


def linked_sum(received, picks, weights, strengths, own_count, modes):
    chosen = received[picks].reshape((own_count, modes) + received.shape[1:])
    factors = weights.astype(jnp.float32) * strengths[None, :]
    total = factors[:, 0, None, None, None] * chosen[:, 0].astype(jnp.float32)
    for mode_index in range(1, modes):
        total = total + factors[:, mode_index, None, None, None] * chosen[:, mode_index].astype(
            jnp.float32
        )
    return total


def couple_step(state, up_sum, down_sum, coupling, decay):
    plus = (up_sum + down_sum).astype(jnp.bfloat16)
    minus = (up_sum - down_sum).astype(jnp.bfloat16)
    left = jnp.einsum("ab,jxbc->jxac", coupling, plus, preferred_element_type=jnp.float32)
    right = jnp.einsum("jxab,bc->jxac", minus, coupling, preferred_element_type=jnp.float32)
    kept = decay[:, None, None, None] * state.astype(jnp.float32)
    real_part = kept[:, 0] + left[:, 1] - right[:, 1]
    imag_part = kept[:, 1] - left[:, 0] + right[:, 0]
    return jnp.stack([real_part, imag_part], axis=1).astype(jnp.bfloat16)


def rotate_step(state, prop_re, prop_im):
    times_re = jnp.einsum("jxab,bc->jxac", state, prop_re, preferred_element_type=jnp.float32)
    times_im = jnp.einsum("jxab,bc->jxac", state, prop_im, preferred_element_type=jnp.float32)
    middle = jnp.stack(
        [times_re[:, 0] - times_im[:, 1], times_im[:, 0] + times_re[:, 1]], axis=1
    ).astype(jnp.bfloat16)
    left_re = jnp.einsum("ba,jxbc->jxac", prop_re, middle, preferred_element_type=jnp.float32)
    left_im = jnp.einsum("ba,jxbc->jxac", prop_im, middle, preferred_element_type=jnp.float32)
    result = jnp.stack([left_re[:, 0] + left_im[:, 1], left_re[:, 1] - left_im[:, 0]], axis=1)
    return result.astype(jnp.bfloat16)


def projection(saved_block, state):
    swapped = jnp.stack([state[:, 1], -state[:, 0]], axis=1)
    real_part = jnp.einsum("jxba,jxbc->ac", saved_block, state, preferred_element_type=jnp.float32)
    imag_part = jnp.einsum(
        "jxba,jxbc->ac", saved_block, swapped, preferred_element_type=jnp.float32
    )
    return jnp.stack([real_part, imag_part], axis=1)


def body(adjoint, saved, propagators, coupling, higher, lower, ladder, rates, decay):
    owners = lax.axis_size(NODE_CORES)
    own_index = lax.axis_index(NODE_CORES)
    own_count = adjoint.shape[0]
    modes = higher.shape[1]
    links = own_count * modes
    capacity = max(1, links // owners)
    step_count = propagators.shape[0]
    sub_count = propagators.shape[1]
    up_send = send_slots(higher, owners, own_index, own_count, links, capacity)
    down_send = send_slots(lower, owners, own_index, own_count, links, capacity)
    up_take = receive_slots(higher, own_index, own_count, links, capacity)
    down_take = receive_slots(lower, own_index, own_count, links, capacity)
    state = adjoint
    all_terms = []
    for step_index in range(step_count):
        up_out = state[up_send]
        down_out = state[down_send]
        up_in, down_in = (
            lax.all_to_all(up_out, NODE_CORES, split_axis=0, concat_axis=0, tiled=True),
            lax.all_to_all(down_out, NODE_CORES, split_axis=0, concat_axis=0, tiled=True),
        )
        up_sum = linked_sum(up_in, up_take, ladder[0], rates[0], own_count, modes)
        down_sum = linked_sum(down_in, down_take, ladder[1], rates[1], own_count, modes)
        state = couple_step(state, up_sum, down_sum, coupling, decay)
        step_terms = []
        for substep in range(sub_count):
            state = rotate_step(
                state, propagators[step_index, substep, 0], propagators[step_index, substep, 1]
            )
            step_terms.append(projection(saved[step_index, substep], state))
        terms = jnp.stack(step_terms, axis=1)
        all_terms.append(terms)
    combined = jnp.concatenate(all_terms, axis=1)
    gradient = sum_in_two_steps(combined, (("node_0", "node_1", "cores_0"), "cores_1"), 0)
    return (state, gradient)


def solution(mesh):
    finer = Mesh(mesh.devices.reshape(4, 2, 4, 4), ("node_0", "node_1", "cores_0", "cores_1"))
    placed = (
        P(NODE_CORES, None, None, None),
        P(None, None, NODE_CORES, None, None, None),
        P(),
        P(),
        P(),
        P(),
        P(None, NODE_CORES, None),
        P(),
        P(NODE_CORES),
    )
    return jax.shard_map(
        body,
        mesh=finer,
        in_specs=placed,
        out_specs=(P(NODE_CORES, None, None, None), P(NODE_CORES, None, None, None)),
        check_vma=False,
    )
```

profile of v0, /device:TPU:1, one launch (start us, length us, event | category | flops | bytes accessed | tf_op | source)
XLA Modules:
  0.0 581.4 jit_solution(13768292560024137467)
XLA Ops:
  7.5 6.4 %gather_fusion.2 = bf16[128,2,128,128]{3,2,1,0:T(8,128)(2,1)} fusion(bf16[8,2,128,128]{3,2,1,0:T(8,128)(2,1)S(1)} %copy-done.1, s32[1024]{0:T(1024)S(1)} %pad_clamp_fusion.1), kind=kCustom, calls=%fused_computation.2 | custom fusion | bytes 16777728 | tf_op jit(solution)/shard_map/gather | solution.py:111
  13.9 11.9 %all-to-all-start.1 = ((bf16[128,2,128,128]{3,2,1,0:T(8,128)(2,1)}), bf16[128,2,128,128]{3,2,1,0:T(8,128)(2,1)}, u32[]{:S(2)}, u32[]{:S(2)}) async-start(bf16[128,2,128,128]{3,2,1,0:T(8,128)(2,1)} %gather_fusion.2), calls=%async_computation.1 | async-start | bytes 16777216 | tf_op jit(solution)/shard_map/all_to_all | solution.py:114
  26.0 6.4 %gather_fusion = bf16[128,2,128,128]{3,2,1,0:T(8,128)(2,1)} fusion(bf16[8,2,128,128]{3,2,1,0:T(8,128)(2,1)S(1)} %copy-done.1, s32[1024]{0:T(1024)S(1)} %pad_clamp_fusion.3), kind=kCustom, calls=%fused_computation | custom fusion | bytes 16777728 | tf_op jit(solution)/shard_map/gather | solution.py:110
  32.5 93.1 %all-to-all-done.1 = bf16[128,2,128,128]{3,2,1,0:T(8,128)(2,1)} async-done(((bf16[128,2,128,128]{3,2,1,0:T(8,128)(2,1)}), bf16[128,2,128,128]{3,2,1,0:T(8,128)(2,1)}, u32[]{:S(2)}, u32[]{:S(2)}) %all-to-all-start.1) | async-done | bytes 8388640 | tf_op jit(solution)/shard_map/all_to_all | solution.py:114
  125.5 19.4 %all-to-all-start = ((bf16[128,2,128,128]{3,2,1,0:T(8,128)(2,1)}), bf16[128,2,128,128]{3,2,1,0:T(8,128)(2,1)}, u32[]{:S(2)}, u32[]{:S(2)}) async-start(bf16[128,2,128,128]{3,2,1,0:T(8,128)(2,1)} %gather_fusion), calls=%async_computation | async-start | bytes 16777216 | tf_op jit(solution)/shard_map/all_to_all | solution.py:113
  148.0 4.3 gather_fusion.3
  152.3 92.5 %all-to-all-done = bf16[128,2,128,128]{3,2,1,0:T(8,128)(2,1)} async-done(((bf16[128,2,128,128]{3,2,1,0:T(8,128)(2,1)}), bf16[128,2,128,128]{3,2,1,0:T(8,128)(2,1)}, u32[]{:S(2)}, u32[]{:S(2)}) %all-to-all-start) | async-done | bytes 8388640 | tf_op jit(solution)/shard_map/all_to_all | solution.py:113
  244.8 5.6 gather_fusion.1
  250.4 2.6 fusion.20
  253.0 2.7 convolution_bitcast_fusion.17
  263.2 6.4 %gather_fusion.4 = bf16[128,2,128,128]{2,3,1,0:T(8,128)(2,1)} fusion(bf16[8,2,128,128]{2,3,1,0:T(8,128)(2,1)S(1)} %pad_maximum_fusion.8, s32[1024]{0:T(1024)S(1)} %pad_clamp_fusion.3), kind=kCustom, calls=%fused_computation.4 | custom fusion | bytes 16777728 | tf_op jit(solution)/shard_map/gather | solution.py:110
  269.6 17.6 %all-to-all-start.2 = ((bf16[128,2,128,128]{2,3,1,0:T(8,128)(2,1)}), bf16[128,2,128,128]{2,3,1,0:T(8,128)(2,1)}, u32[]{:S(2)}, u32[]{:S(2)}) async-start(bf16[128,2,128,128]{2,3,1,0:T(8,128)(2,1)} %gather_fusion.4), calls=%async_computation.2 | async-start | bytes 16777216 | tf_op jit(solution)/shard_map/all_to_all | solution.py:113
  287.2 6.4 %gather_fusion.6 = bf16[128,2,128,128]{2,3,1,0:T(8,128)(2,1)} fusion(bf16[8,2,128,128]{2,3,1,0:T(8,128)(2,1)S(1)} %pad_maximum_fusion.8, s32[1024]{0:T(1024)S(1)} %pad_clamp_fusion.1), kind=kCustom, calls=%fused_computation.6 | custom fusion | bytes 16777728 | tf_op jit(solution)/shard_map/gather | solution.py:111
  293.6 93.3 %all-to-all-done.2 = bf16[128,2,128,128]{2,3,1,0:T(8,128)(2,1)} async-done(((bf16[128,2,128,128]{2,3,1,0:T(8,128)(2,1)}), bf16[128,2,128,128]{2,3,1,0:T(8,128)(2,1)}, u32[]{:S(2)}, u32[]{:S(2)}) %all-to-all-start.2) | async-done | bytes 8388640 | tf_op jit(solution)/shard_map/all_to_all | solution.py:113
  386.9 19.2 %all-to-all-start.3 = ((bf16[128,2,128,128]{2,3,1,0:T(8,128)(2,1)}), bf16[128,2,128,128]{2,3,1,0:T(8,128)(2,1)}, u32[]{:S(2)}, u32[]{:S(2)}) async-start(bf16[128,2,128,128]{2,3,1,0:T(8,128)(2,1)} %gather_fusion.6), calls=%async_computation.3 | async-start | bytes 16777216 | tf_op jit(solution)/shard_map/all_to_all | solution.py:114
  406.2 1.5 fusion.58
  407.8 1.4 fusion.112
  416.3 4.3 gather_fusion.5
  422.0 2.1 copy.669
  424.1 2.1 copy.671
  426.1 2.0 copy.670
  428.2 2.0 copy.672
  430.2 75.5 %all-to-all-done.3 = bf16[128,2,128,128]{2,3,1,0:T(8,128)(2,1)} async-done(((bf16[128,2,128,128]{2,3,1,0:T(8,128)(2,1)}), bf16[128,2,128,128]{2,3,1,0:T(8,128)(2,1)}, u32[]{:S(2)}, u32[]{:S(2)}) %all-to-all-start.3) | async-done | bytes 8388640 | tf_op jit(solution)/shard_map/all_to_all | solution.py:114
  505.7 4.3 gather_fusion.7
  511.4 2.2 copy.673
  513.6 2.0 copy.675
  515.6 2.0 copy.674
  517.7 2.0 copy.676
  519.8 2.7 fusion.21
  537.5 24.6 %all_to_all.30 = f32[4,32,1,8,2,128]{5,1,4,3,2,0:T(8,128)S(1)} all-to-all(f32[4,32,1,8,2,128]{5,1,4,3,2,0:T(8,128)} %bitcast.197), channel_id=1, replica_groups=mesh['node_0'=4,'node_1'=2,'cores_0'=4,'cores_1'=4] {'cores_1'}, dimensions={0} | all-to-all | bytes 2097152 | tf_op jit(solution)/shard_map/all_to_all | solution.py:18
  563.2 8.3 %all-to-all-start.5 = ((f32[32,1,8,2,128]{4,3,2,1,0:T(2,128)}), f32[32,1,8,2,128]{4,3,2,1,0:T(2,128)S(1)}, u32[]{:S(2)}, u32[]{:S(2)}) async-start(f32[32,1,8,2,128]{4,3,2,1,0:T(2,128)} %copy.569), calls=%async_computation.5 | async-start | bytes 524288 | tf_op jit(solution)/shard_map/all_to_all | solution.py:26
  572.5 7.7 %all-to-all-done.5 = f32[32,1,8,2,128]{4,3,2,1,0:T(2,128)S(1)} async-done(((f32[32,1,8,2,128]{4,3,2,1,0:T(2,128)}), f32[32,1,8,2,128]{4,3,2,1,0:T(2,128)S(1)}, u32[]{:S(2)}, u32[]{:S(2)}) %all-to-all-start.5) | async-done | bytes 262176 | tf_op jit(solution)/shard_map/all_to_all | solution.py:26
  (191 shorter events, 44.5 us)
Async XLA Ops:
  0.6 249.8 %copy-start = (bf16[128,128]{1,0:T(8,128)(2,1)S(1)}, bf16[128,128]{1,0:T(8,128)(2,1)}, u32[]{:S(2)}) copy-start(bf16[128,128]{1,0:T(8,128)(2,1)} %param.12) | copy-start | bytes 98308
  0.6 6.8 %copy-start.1 = (bf16[8,2,128,128]{3,2,1,0:T(8,128)(2,1)S(1)}, bf16[8,2,128,128]{3,2,1,0:T(8,128)(2,1)}, u32[]{:S(2)}) copy-start(bf16[8,2,128,128]{3,2,1,0:T(8,128)(2,1)} %param.9) | copy-start | bytes 1572868
  13.9 111.6 %all-to-all-start.1 = ((bf16[128,2,128,128]{3,2,1,0:T(8,128)(2,1)}), bf16[128,2,128,128]{3,2,1,0:T(8,128)(2,1)}, u32[]{:S(2)}, u32[]{:S(2)}) async-start(bf16[128,2,128,128]{3,2,1,0:T(8,128)(2,1)} %gather_fusion.2), calls=%async_computation.1 | async-start | bytes 16777216 | tf_op jit(solution)/shard_map/all_to_all | solution.py:114
  32.4 115.2 %copy-start.16 = (f32[2,4]{1,0:T(2,128)S(1)}, f32[2,4]{1,0:T(2,128)}, u32[]{:S(2)}) copy-start(f32[2,4]{1,0:T(2,128)} %param.16) | copy-start | bytes 100
  32.4 115.2 %copy-start.14 = (s32[2,8,4]{1,2,0:T(4,128)S(1)}, s32[2,8,4]{1,2,0:T(4,128)}, u32[]{:S(2)}) copy-start(s32[2,8,4]{1,2,0:T(4,128)} %param.15) | copy-start | bytes 772
  32.4 115.3 %copy-start.15 = (f32[8]{0:T(128)S(1)}, f32[8]{0:T(128)}, u32[]{:S(2)}) copy-start(f32[8]{0:T(128)} %param.17) | copy-start | bytes 100
  125.5 119.3 %all-to-all-start = ((bf16[128,2,128,128]{3,2,1,0:T(8,128)(2,1)}), bf16[128,2,128,128]{3,2,1,0:T(8,128)(2,1)}, u32[]{:S(2)}, u32[]{:S(2)}) async-start(bf16[128,2,128,128]{3,2,1,0:T(8,128)(2,1)} %gather_fusion), calls=%async_computation | async-start | bytes 16777216 | tf_op jit(solution)/shard_map/all_to_all | solution.py:113
  253.0 2.9 copy-start.3
  263.2 148.9 %copy-start.2 = (bf16[8,1,128,128]{2,3,1,0:T(8,128)(2,1)}, bf16[8,1,128,128]{2,3,1,0:T(8,128)(2,1)S(1)}, u32[]{:S(2)}) copy-start(bf16[8,1,128,128]{2,3,1,0:T(8,128)(2,1)S(1)} %get-tuple-element.21) | copy-start | bytes 786436
  269.6 117.3 %all-to-all-start.2 = ((bf16[128,2,128,128]{2,3,1,0:T(8,128)(2,1)}), bf16[128,2,128,128]{2,3,1,0:T(8,128)(2,1)}, u32[]{:S(2)}, u32[]{:S(2)}) async-start(bf16[128,2,128,128]{2,3,1,0:T(8,128)(2,1)} %gather_fusion.4), calls=%async_computation.2 | async-start | bytes 16777216 | tf_op jit(solution)/shard_map/all_to_all | solution.py:113
  386.9 118.8 %all-to-all-start.3 = ((bf16[128,2,128,128]{2,3,1,0:T(8,128)(2,1)}), bf16[128,2,128,128]{2,3,1,0:T(8,128)(2,1)}, u32[]{:S(2)}, u32[]{:S(2)}) async-start(bf16[128,2,128,128]{2,3,1,0:T(8,128)(2,1)} %gather_fusion.6), calls=%async_computation.3 | async-start | bytes 16777216 | tf_op jit(solution)/shard_map/all_to_all | solution.py:114
  406.2 4.4 copy-start.17
  407.7 4.0 copy-start.13
  511.4 8.3 %copy-start.5 = (bf16[8,1,2,128,128]{4,3,2,0,1:T(8,128)(2,1)S(1)}, bf16[8,1,2,128,128]{4,3,2,0,1:T(8,128)(2,1)}, u32[]{:S(2)}) copy-start(bf16[8,1,2,128,128]{4,3,2,0,1:T(8,128)(2,1)} %copy.669) | copy-start | bytes 1572868
  511.4 8.3 %copy-start.6 = (bf16[8,1,2,128,128]{4,3,2,0,1:T(8,128)(2,1)S(1)}, bf16[8,1,2,128,128]{4,3,2,0,1:T(8,128)(2,1)}, u32[]{:S(2)}) copy-start(bf16[8,1,2,128,128]{4,3,2,0,1:T(8,128)(2,1)} %copy.671) | copy-start | bytes 1572868
  511.4 8.3 %copy-start.7 = (bf16[8,1,2,128,128]{4,3,2,0,1:T(8,128)(2,1)S(1)}, bf16[8,1,2,128,128]{4,3,2,0,1:T(8,128)(2,1)}, u32[]{:S(2)}) copy-start(bf16[8,1,2,128,128]{4,3,2,0,1:T(8,128)(2,1)} %copy.670) | copy-start | bytes 1572868
  511.4 8.3 %copy-start.8 = (bf16[8,1,2,128,128]{4,3,2,0,1:T(8,128)(2,1)S(1)}, bf16[8,1,2,128,128]{4,3,2,0,1:T(8,128)(2,1)}, u32[]{:S(2)}) copy-start(bf16[8,1,2,128,128]{4,3,2,0,1:T(8,128)(2,1)} %copy.672) | copy-start | bytes 1572868
  519.7 2.8 copy-start.9
  519.7 2.8 copy-start.10
  519.7 2.8 copy-start.11
  519.8 2.8 copy-start.12
  522.5 1.3 copy-start.4
  524.5 2.2 copy-start.18
  563.2 17.1 %all-to-all-start.5 = ((f32[32,1,8,2,128]{4,3,2,1,0:T(2,128)}), f32[32,1,8,2,128]{4,3,2,1,0:T(2,128)S(1)}, u32[]{:S(2)}, u32[]{:S(2)}) async-start(f32[32,1,8,2,128]{4,3,2,1,0:T(2,128)} %copy.569), calls=%async_computation.5 | async-start | bytes 524288 | tf_op jit(solution)/shard_map/all_to_all | solution.py:26
where the time goes:
time: 588 us; the launch traced here: 581 us
  waiting for transfers between devices  362 us (62%)
  starting transfers between devices  76.4 us (13%)
  local copies, waits for them, and re-layouts  72.7 us (12%)
  matrix products  28.7 us (5%)
  blocking collectives  24.6 us (4%)
  other arithmetic  14.7 us (2%)
    all_to_all x2, waiting for transfers between devices, body(): lax.all_to_all(up_out, NODE_CORES, split_axis=0, concat_axis=0, tiled=True)  186 us
    all_to_all x2, waiting for transfers between devices, body(): lax.all_to_all(down_out, NODE_CORES, split_axis=0, concat_axis=0, tiled=T...  169 us
    all_to_all x2, starting transfers between devices, body(): lax.all_to_all(up_out, NODE_CORES, split_axis=0, concat_axis=0, tiled=True)  37 us
    all_to_all x2, starting transfers between devices, body(): lax.all_to_all(down_out, NODE_CORES, split_axis=0, concat_axis=0, tiled=T...  31.2 us
    all_to_all x1, blocking collectives, sent_and_summed(): tiles = lax.all_to_all(cut_along(x, dim, length), axis, 0, 0, tiled=True)  24.6 us
    unnamed x50, local copies, waits for them, and re-layouts  21 us
    gather x4, local copies, waits for them, and re-layouts, linked_sum(): chosen = received[picks].reshape((own_count, modes) + received.shape[1:])  18.6 us
    gather x2, local copies, waits for them, and re-layouts, body(): down_out = state[down_send]  12.9 us
  transfers between devices with their start and end apart: 5, of which 5 were waited for; matrix products, arithmetic and copies ran while one was open for 8% of the time, Pallas kernels for 0%

commit v1 on v0

v1 whole, which is shorter than its diff:
```python
import jax
import jax.numpy as jnp
from jax import lax
from jax.experimental import pallas as pl
from jax.experimental.pallas import tpu as pltpu
from jax.sharding import Mesh
from jax.sharding import PartitionSpec as P

AXES = ("y", "c", "z", "x")
BF = jnp.bfloat16
F32 = jnp.float32
OWN = 8
MODES = 4
DIM = 128
ROWS = 2 * DIM
BLOCK = OWN * ROWS


def pairs(move):
    out = []
    for y in range(4):
        for c in range(2):
            for z in range(4):
                for x in range(4):
                    ny, nc, nz, nx = move(y, c, z, x)
                    here = ((y * 2 + c) * 4 + z) * 4 + x
                    there = ((ny * 2 + nc) * 4 + nz) * 4 + nx
                    out.append((here, there))
    return out


def first(s):
    return pairs(lambda y, c, z, x: (y, c, z, (x + s) % 4) if c == 0 else (y, c, (z + s) % 4, x))


def second(s):
    return pairs(lambda y, c, z, x: (y, c, (z + s) % 4, x) if c == 0 else (y, c, z, (x + s) % 4))


def along_y(s):
    return pairs(lambda y, c, z, x: ((y + s) % 4, c, z, x))


def along_z(s):
    return pairs(lambda y, c, z, x: (y, c, (z + s) % 4, x))


def along_x(s):
    return pairs(lambda y, c, z, x: (y, c, z, (x + s) % 4))


SIBLING = pairs(lambda y, c, z, x: (y, 1 - c, z, x))


def send(a, route):
    return lax.ppermute(a, AXES, route)


def gather_layer(block):
    near = {0: block}
    for s in (1, 3, 2):
        near[s] = send(block, first(s))
    held = {}
    for s in (0, 1, 3, 2):
        held[s, 0] = near[s]
        held[s, 1] = send(near[s], second(1))
        held[s, 3] = send(near[s], second(3))
        if s in (0, 3):
            held[s, 2] = send(held[s, 1], second(1))
        else:
            held[s, 2] = send(held[s, 3], second(3))
    mine = [held[s, t] for s in range(4) for t in range(4)]
    return mine + [send(b, SIBLING) for b in mine]


def gather_meta(meta):
    by_y = jnp.stack([meta] + [send(meta, along_y(s)) for s in (1, 2, 3)])
    part = by_y.reshape(32, 16)
    part = jnp.concatenate([part, send(part, SIBLING)])
    part = jnp.concatenate([part] + [send(part, along_z(s)) for s in (1, 2, 3)])
    part = jnp.concatenate([part] + [send(part, along_x(s)) for s in (1, 2, 3)])
    return by_y, part


def slot_of(q, at):
    y, c, z, x = at
    owner = q >> 3
    oy, oc, oz, ox = owner >> 5, (owner >> 4) & 1, (owner >> 2) & 3, owner & 3
    dx, dz = (x - ox) & 3, (z - oz) & 3
    s = jnp.where(oc == 0, dx, dz)
    t = jnp.where(oc == 0, dz, dx)
    other = (oc != c).astype(jnp.int32)
    slot = ((other * 16 + s * 4 + t) << 3) + (q & 7)
    return jnp.where(oy == y, slot, -1)


def meta_row(q, at):
    y, c, z, x = at
    owner = q >> 3
    oy, oc, oz, ox = owner >> 5, (owner >> 4) & 1, (owner >> 2) & 3, owner & 3
    other = (oc != c).astype(jnp.int32)
    relative = ((((x - ox) & 3) * 4 + ((z - oz) & 3)) * 2 + other) * 4 + ((y - oy) & 3)
    return (relative << 3) + (q & 7)


def compact(slot, values):
    count = slot.shape[-1]
    keep = (slot >= 0) & (values[0] != 0)
    before = jnp.arange(count)[:, None] < jnp.arange(count)[None, :]
    at = jnp.sum((keep[..., :, None] & before).astype(jnp.int32), axis=-2)
    moved = keep[..., :, None] & (at[..., :, None] == jnp.arange(count))
    lists = [jnp.sum(jnp.where(moved, v[..., :, None], 0), axis=-2).reshape(-1) for v in [slot, *values]]
    return [jnp.sum(keep.astype(jnp.int32), axis=-1).reshape(-1), *lists]


def pick(rows, table):
    hot = (rows.reshape(-1)[:, None] == jnp.arange(table.shape[0])[None, :]).astype(F32)
    return jnp.dot(hot, table, precision=lax.Precision.HIGHEST, preferred_element_type=F32)


def own_links(higher, lower, at):
    y, c, z, x = at
    rows = []
    for dy in range(4):
        start = ((((y + dy) & 3) * 2 + c) * 16 + z * 4 + x) * OWN
        both = [lax.dynamic_slice_in_dim(t, start, OWN, 0) for t in (higher, lower)]
        rows.append(jnp.concatenate(both, axis=1))
    return jnp.concatenate(rows)


def link_lists(higher, lower, by_y, meta, rates, at):
    strengths = rates.reshape(1, 8)
    partner = own_links(higher, lower, at)
    weights = jnp.concatenate([by_y[0], by_y[3], by_y[2], by_y[1]])[:, :8] * strengths
    near_slot = slot_of(partner, at)
    wanted = pick(meta_row(partner, at), meta)
    decay = wanted[:, 8].reshape(32, 8)
    near = compact(near_slot.reshape(32, 2, 4), [v.reshape(32, 2, 4) for v in (weights, weights * decay)])
    far = jnp.concatenate([slot_of(higher, at), slot_of(lower, at)], axis=1).astype(F32)
    far_slot = pick(partner, far).astype(jnp.int32)
    far_weight = wanted[:, :8] * strengths * weights.reshape(256, 1)
    spread = lambda v: v.reshape(32, 2, 4, 2, 4).transpose(0, 1, 3, 2, 4).reshape(32, 4, 16)
    return near, compact(spread(far_slot), [spread(far_weight)])


def fetch(blocks, held, sems):
    copies = [
        pltpu.make_async_copy(b, held.at[pl.ds(k * BLOCK, BLOCK), :], sems.at[k])
        for k, b in enumerate(blocks)
    ]
    for copy in copies:
        copy.start()
    for copy in copies:
        copy.wait()


def link_sum(held, slots, weights, base, count):
    def add(k, total):
        start = pl.multiple_of(slots[base + k] * ROWS, ROWS)
        return total + weights[base + k] * held[pl.ds(start, ROWS), :].astype(F32)

    return lax.fori_loop(0, count, add, jnp.zeros((ROWS, DIM), F32))


def mm(a, b):
    return jnp.dot(a, b, preferred_element_type=F32)


def commute(c, plus, minus):
    left = mm(c, jnp.concatenate([plus[DIM:], -plus[:DIM]], axis=1))
    right = mm(minus, c)
    return left[:, :DIM] - right[DIM:], left[:, DIM:] + right[:DIM]


def near_kernel(count, slots, weights, c_ref, *refs):
    blocks, outs = refs[:32], refs[32:36]
    held, sems = refs[36:]
    fetch(blocks, held, sems)
    c = c_ref[...]
    for dy in range(4):
        out = outs[dy]

        def one(i, _):
            d = (dy * OWN + i) * 2
            up = link_sum(held, slots, weights, d * 4, count[d])
            down = link_sum(held, slots, weights, d * 4 + 4, count[d + 1])
            re, im = commute(c, (up + down).astype(BF), (up - down).astype(BF))
            at = pl.multiple_of(i * ROWS, ROWS)
            out[pl.ds(at, DIM), :] = re.astype(out.dtype)
            out[pl.ds(at + DIM, DIM), :] = im.astype(out.dtype)
            return 0

        lax.fori_loop(0, OWN, one, 0)


def far_kernel(n1, s1, w1, n2, s2, w2, c_ref, right_ref, left_ref, *refs):
    blocks, outs = refs[:32], refs[32:36]
    held, sems, acc = refs[36:]
    fetch(blocks, held, sems)
    c = c_ref[...]
    for dy in range(4):
        out = outs[dy]

        def one(i, _):
            d = dy * OWN + i
            for k in range(4):
                acc[k] = link_sum(held, s2, w2, d * 64 + k * 16, n2[d * 4 + k])
            for k in range(2):
                acc[4 + k] = link_sum(held, s1, w1, d * 8 + k * 4, n1[d * 2 + k])
            pu, mu = acc[0] + acc[1], acc[0] - acc[1]
            pd, md = acc[2] + acc[3], acc[2] - acc[3]
            halves = []
            for sign in (1, -1):
                re, im = commute(c, (pu + sign * pd).astype(BF), (mu + sign * md).astype(BF))
                kept = acc[4] + sign * acc[5]
                halves.append(jnp.concatenate([kept[:DIM] + re, kept[DIM:] + im], axis=1))
            y = jnp.concatenate(halves).astype(BF)
            mid = mm(y, right_ref[...]).astype(BF)
            stacked = jnp.concatenate(
                [
                    jnp.concatenate([mid[:DIM, :DIM], mid[DIM:, :DIM]], axis=1),
                    jnp.concatenate([mid[:DIM, DIM:], mid[DIM:, DIM:]], axis=1),
                ]
            )
            turned = mm(left_ref[...], stacked).astype(BF)
            re, im = commute(c, turned[:, :DIM], turned[:, DIM:])
            at = pl.multiple_of(i * ROWS, ROWS)
            out[pl.ds(at, DIM), :] = re.astype(out.dtype)
            out[pl.ds(at + DIM, DIM), :] = im.astype(out.dtype)
            return 0

        lax.fori_loop(0, OWN, one, 0)


SM = pl.BlockSpec(memory_space=pltpu.SMEM)
VM = pl.BlockSpec(memory_space=pltpu.VMEM)
ANY = pl.BlockSpec(memory_space=pl.ANY)


def parts_of(kernel, scalars, arrays, blocks, scratch, flops):
    shapes = [jax.ShapeDtypeStruct((BLOCK, DIM), F32)] + [jax.ShapeDtypeStruct((BLOCK, DIM), BF)] * 3
    return pl.pallas_call(
        kernel,
        out_shape=shapes,
        in_specs=[SM] * len(scalars) + [VM] * len(arrays) + [ANY] * 32,
        out_specs=[VM] * 4,
        scratch_shapes=[pltpu.VMEM((32 * BLOCK, DIM), BF), pltpu.SemaphoreType.DMA((32,))] + scratch,
        compiler_params=pltpu.CompilerParams(vmem_limit_bytes=32 << 20),
        cost_estimate=pl.CostEstimate(flops=flops, bytes_accessed=20 << 20, transcendentals=0),
    )(*scalars, *arrays, *blocks)


def chain_kernel(decay, lam_ref, own_ref, a_ref, b_ref, d_ref, right_ref, left_ref, saved_ref, out_ref, grad_ref, wide, tall):
    for j in range(OWN):
        rows = pl.ds(j * ROWS, ROWS)
        mixed = decay[j] * lam_ref[rows, :].astype(F32) + own_ref[rows, :]
        mixed = mixed + a_ref[rows, :].astype(F32) + b_ref[rows, :].astype(F32) + d_ref[rows, :].astype(F32)
        mixed = mixed.astype(BF)
        wide[pl.ds(j * DIM, DIM), 0:DIM] = mixed[:DIM]
        wide[pl.ds(j * DIM, DIM), DIM:ROWS] = mixed[DIM:]

    def substep(u, _):
        right, left = right_ref[u], left_ref[u]
        for h in range(OWN // 2):
            mid = mm(wide[pl.ds(h * ROWS, ROWS), :], right).astype(BF)
            stacked = jnp.concatenate(
                [
                    jnp.concatenate([mid[:DIM, :DIM], mid[DIM:, :DIM]], axis=1),
                    jnp.concatenate([mid[:DIM, DIM:], mid[DIM:, DIM:]], axis=1),
                ]
            )
            turned = mm(left, stacked).astype(BF)
            for k in range(2):
                re, im = turned[:DIM, k * DIM : (k + 1) * DIM], turned[DIM:, k * DIM : (k + 1) * DIM]
                j = 2 * h + k
                wide[pl.ds(j * DIM, DIM), 0:DIM] = re
                wide[pl.ds(j * DIM, DIM), DIM:ROWS] = im
                tall[pl.ds(j * ROWS, DIM), 0:DIM] = re
                tall[pl.ds(j * ROWS, DIM), DIM:ROWS] = im
                tall[pl.ds(j * ROWS + DIM, DIM), 0:DIM] = im
                tall[pl.ds(j * ROWS + DIM, DIM), DIM:ROWS] = -re
        terms = lax.dot_general(
            saved_ref[u], tall[...], (((0,), (0,)), ((), ())), preferred_element_type=F32
        )
        grad_ref[u, 0] = terms[:, :DIM]
        grad_ref[u, 1] = terms[:, DIM:]
        return 0

    lax.fori_loop(0, 4, substep, 0)
    for j in range(OWN):
        out_ref[pl.ds(j * ROWS, DIM), :] = wide[pl.ds(j * DIM, DIM), 0:DIM]
        out_ref[pl.ds(j * ROWS + DIM, DIM), :] = wide[pl.ds(j * DIM, DIM), DIM:ROWS]


def chain(decay, lam, parts, right, left, saved):
    return pl.pallas_call(
        chain_kernel,
        out_shape=[
            jax.ShapeDtypeStruct((BLOCK, DIM), BF),
            jax.ShapeDtypeStruct((4, 2, DIM, DIM), F32),
        ],
        in_specs=[SM] + [VM] * 8,
        out_specs=[VM] * 2,
        scratch_shapes=[pltpu.VMEM((OWN * DIM, ROWS), BF), pltpu.VMEM((BLOCK, ROWS), BF)],
        compiler_params=pltpu.CompilerParams(vmem_limit_bytes=24 << 20),
        cost_estimate=pl.CostEstimate(flops=2 * 10**9, bytes_accessed=6 << 20, transcendentals=0),
    )(decay, lam, *parts, right, left, saved)


def compose_kernel(prop_ref, right_ref, left_ref):
    hi = lambda v: v.astype(BF)
    re, im = prop_ref[0, 0].astype(F32), prop_ref[0, 1].astype(F32)
    for u in range(1, 4):
        ur, ui = prop_ref[u, 0], prop_ref[u, 1]
        mul = lambda v, m: mm(hi(v), m) + mm(hi(v - hi(v).astype(F32)), m)
        re, im = mul(re, ur) - mul(im, ui), mul(re, ui) + mul(im, ur)
    turned_re, turned_im = re.T.astype(BF), im.T.astype(BF)
    re, im = re.astype(BF), im.astype(BF)
    right_ref[0:DIM, 0:DIM] = re
    right_ref[0:DIM, DIM:ROWS] = im
    right_ref[DIM:ROWS, 0:DIM] = -im
    right_ref[DIM:ROWS, DIM:ROWS] = re
    left_ref[0:DIM, 0:DIM] = turned_re
    left_ref[0:DIM, DIM:ROWS] = turned_im
    left_ref[DIM:ROWS, 0:DIM] = -turned_im
    left_ref[DIM:ROWS, DIM:ROWS] = turned_re


def compose(props):
    return pl.pallas_call(
        compose_kernel,
        out_shape=[jax.ShapeDtypeStruct((ROWS, ROWS), BF)] * 2,
        in_specs=[VM],
        out_specs=[VM] * 2,
    )(props)


def body(adjoint, saved, propagators, coupling, higher, lower, ladder, rates, decay):
    at = tuple(lax.axis_index(a) for a in AXES)
    lam = adjoint.reshape(BLOCK, DIM)
    meta = jnp.concatenate(
        [ladder[0].astype(F32), ladder[1].astype(F32), decay[:, None], jnp.zeros((OWN, 7), F32)], axis=1
    )
    blocks = gather_layer(lam)
    by_y, meta = gather_meta(meta)
    near, far = link_lists(higher, lower, by_y, meta, rates, at)
    count, slots, weights, damped = near
    re, im = propagators[:, :, 0], propagators[:, :, 1]
    right = jnp.concatenate(
        [jnp.concatenate([re, im], axis=3), jnp.concatenate([-im, re], axis=3)], axis=2
    )
    turn = lambda v: jnp.swapaxes(v, 2, 3)
    left = jnp.concatenate(
        [jnp.concatenate([turn(re), turn(im)], axis=3), jnp.concatenate([-turn(im), turn(re)], axis=3)], axis=2
    )
    whole_right, whole_left = compose(propagators[0])
    one = parts_of(near_kernel, [count, slots, weights], [coupling], blocks, [], 10**9)
    got_one = [one[0]] + [send(one[dy], along_y(dy)) for dy in (1, 2, 3)]
    two = parts_of(
        far_kernel,
        [count, slots, damped, *far],
        [coupling, whole_right, whole_left],
        blocks,
        [pltpu.VMEM((6, ROWS, DIM), F32)],
        16 * 10**9,
    )
    got_two = [two[0]] + [send(two[dy], along_y(dy)) for dy in (1, 2, 3)]
    saved = saved.reshape(2, 4, BLOCK, DIM)
    lam, grad_one = chain(decay, lam, got_one, right[0], left[0], saved[0])
    lam, grad_two = chain(decay, lam, got_two, right[1], left[1], saved[1])
    grad = jnp.concatenate([grad_one, grad_two]).astype(BF)
    grad = jnp.moveaxis(grad, 2, 0)
    grad = lax.all_to_all(grad, AXES, 0, 0, tiled=True)
    grad = jnp.sum(grad.astype(F32), axis=0, keepdims=True)
    return lam.reshape(OWN, 2, DIM, DIM), grad


def solution(mesh):
    finer = Mesh(mesh.devices.reshape(4, 2, 4, 4), AXES)
    rows = P(AXES)
    return jax.shard_map(
        body,
        mesh=finer,
        in_specs=(rows, P(None, None, AXES), P(), P(), P(), P(), P(None, AXES), P(), rows),
        out_specs=(rows, rows),
        check_vma=False,
    )
```

time: 588 us -> 224 us (0.38); the launches traced: 581 us -> 223 us
  waiting for transfers between devices: 362 us -> 44.1 us
  Pallas kernels: 0 us -> 66.8 us
  local copies, waits for them, and re-layouts: 72.7 us -> 20.7 us
  matrix products: 28.7 us -> 1.26 us
  starting transfers between devices: 76.4 us -> 60.2 us
  other arithmetic: 14.7 us -> 8.49 us
    all_to_all x5 -> x0, waiting for transfers between devices: 362 us -> none  [the longest x2 186 us: body(): lax.all_to_all(up_out, NODE_CORES, split_axis=0, concat_axis=0, tiled=True)]
    all_to_all x5 -> x0, starting transfers between devices: 76.4 us -> none  [the longest x2 37 us: body(): lax.all_to_all(up_out, NODE_CORES, split_axis=0, concat_axis=0, tiled=True)]
    pallas_call x0 -> x5, Pallas kernels: none -> 66.8 us  [the longest x2 53 us: parts_of(): pl.pallas_call(kernel, out_shape=shapes, in_specs=[SM] * len(scalars) + [...]
    ppermute x0 -> x47, starting transfers between devices: none -> 60.2 us  [send(): return lax.ppermute(a, AXES, route)]
    gather x8 -> x0, local copies, waits for them, and re-layouts: 44.2 us -> none  [the longest x4 18.6 us: linked_sum(): chosen = received[picks].reshape((own_count, modes) + received.shape[1:])]
    ppermute x0 -> x47, waiting for transfers between devices: none -> 44.1 us  [send(): return lax.ppermute(a, AXES, route)]
    dot_general x52 -> x2, matrix products: 28.7 us -> 1.26 us  [pick(): jnp.dot(hot, table, precision=lax.Precision.HIGHEST, preferred_element_ty...]
    unnamed x50 -> x62, local copies, waits for them, and re-layouts: 21 us -> 9.75 us
  transfers between devices with their start and end apart: 5 -> 47, of which waited for: 5 -> 19; matrix products, arithmetic and copies ran while one was open for 8% -> 8% of each run, Pallas kernels for 0% -> 21%
where the time goes in v1:
time: 224 us; the launch traced here: 223 us
  Pallas kernels  66.8 us (30%)
  starting transfers between devices  60.2 us (27%)
  waiting for transfers between devices  44.1 us (20%)
  local copies, waits for them, and re-layouts  20.7 us (9%)
  blocking collectives  20.7 us (9%)
  other arithmetic  8.49 us (4%)
    ppermute x47, starting transfers between devices, send(): return lax.ppermute(a, AXES, route)  60.2 us
    pallas_call x2, Pallas kernels, parts_of(): pl.pallas_call(kernel, out_shape=shapes, in_specs=[SM] * len(scalars) + [...  53 us
    ppermute x47, waiting for transfers between devices, send(): return lax.ppermute(a, AXES, route)  44.1 us
    all_to_all x1, blocking collectives, body(): grad = lax.all_to_all(grad, AXES, 0, 0, tiled=True)  20.7 us
    pallas_call x2, Pallas kernels, chain(): pl.pallas_call(chain_kernel, out_shape=[jax.ShapeDtypeStruct((BLOCK, DIM)...  11.4 us
    unnamed x62, local copies, waits for them, and re-layouts  9.75 us
  transfers between devices with their start and end apart: 47, of which 19 were waited for; matrix products, arithmetic and copies ran while one was open for 8% of the time, Pallas kernels for 21%

profile of v1, /device:TPU:1, one launch (start us, length us, event | category | flops | bytes accessed | tf_op | source)
XLA Modules:
  0.0 223.4 jit_solution(17136803827709783144)
XLA Ops:
  2.3 2.1 collective-permute-start.2
  4.5 2.6 %collective-permute-start.1 = (f32[8,16]{1,0:T(8,128)S(1)}, f32[8,16]{1,0:T(8,128)S(1)}, u32[]{:S(2)}, u32[]{:S(2)}) collective-permute-start(f32[8,16]{1,0:T(8,128)S(1)} %pad_maximum_fusion.7), channel_id=1, source_target_pairs={{0,64},{1,65},{2,66},{3,67},{4,68},{5,69},{6,70},{7,71},{8,72},{9,... | collective-permute-start | bytes 1544 | tf_op jit(solution)/shard_map/ppermute | solution.py:56
  8.2 1.6 collective-permute-start.6
  9.8 3.3 %collective-permute-start.10 = (bf16[2048,128]{1,0:T(8,128)(2,1)}, bf16[2048,128]{1,0:T(8,128)(2,1)}, u32[]{:S(2)}, u32[]{:S(2)}) collective-permute-start(bf16[2048,128]{1,0:T(8,128)(2,1)} %bitcast.66), channel_id=1, source_target_pairs={{0,2},{1,3},{2,0},{3,1},{4,6},{5,7},{6,4},{7,5},{8,10},{9,11},{10,... | collective-permute-start | bytes 1572872 | tf_op jit(solution)/shard_map/ppermute | solution.py:56
  19.9 1.7 collective-permute-start.38
  21.6 3.3 %collective-permute-start.39 = (f32[64,16]{0,1:T(8,128)S(1)}, f32[64,16]{0,1:T(8,128)S(1)}, u32[]{:S(2)}, u32[]{:S(2)}) collective-permute-start(f32[64,16]{0,1:T(8,128)S(1)} %pad_maximum_fusion.6), channel_id=1, source_target_pairs={{0,8},{1,9},{2,10},{3,11},{4,12},{5,13},{6,14},{7,15},{8,0},{9,1},... | collective-permute-start | bytes 12296 | tf_op jit(solution)/shard_map/ppermute | solution.py:56
  27.5 2.3 %collective-permute-start.42 = (f32[256,16]{0,1:T(8,128)S(1)}, f32[256,16]{0,1:T(8,128)S(1)}, u32[]{:S(2)}, u32[]{:S(2)}) collective-permute-start(f32[256,16]{0,1:T(8,128)S(1)} %concatenate.102), channel_id=1, source_target_pairs={{0,2},{1,3},{2,0},{3,1},{4,6},{5,7},{6,4},{7,5},{8,10},{9,11},{10,... | collective-permute-start | bytes 49160 | tf_op jit(solution)/shard_map/ppermute | solution.py:56
  31.3 2.3 %collective-permute-start.14 = (bf16[2048,128]{1,0:T(8,128)(2,1)S(1)}, bf16[2048,128]{1,0:T(8,128)(2,1)}, u32[]{:S(2)}, u32[]{:S(2)}) collective-permute-start(bf16[2048,128]{1,0:T(8,128)(2,1)S(1)} %bitcast.67), channel_id=1, source_target_pairs={{0,3},{1,0},{2,1},{3,2},{4,7},{5,4},{6,5},{7,6},{8,11},{9,8},{10,9... | collective-permute-start | bytes 1572872 | tf_op jit(solution)/shard_map/ppermute | solution.py:56
  33.6 2.7 %collective-permute-start.5 = (bf16[2048,128]{1,0:T(8,128)(2,1)S(1)}, bf16[2048,128]{1,0:T(8,128)(2,1)S(1)}, u32[]{:S(2)}, u32[]{:S(2)}) collective-permute-start(bf16[2048,128]{1,0:T(8,128)(2,1)S(1)} %bitcast.69), channel_id=1, source_target_pairs={{0,12},{1,13},{2,14},{3,15},{4,0},{5,1},{6,2},{7,3},{8,4},{9,5},{1... | collective-permute-start | bytes 1572872 | tf_op jit(solution)/shard_map/ppermute | solution.py:56
  36.3 2.2 collective-permute-start.18
  39.2 2.6 %collective-permute-start.8 = (bf16[2048,128]{1,0:T(8,128)(2,1)S(1)}, bf16[2048,128]{1,0:T(8,128)(2,1)S(1)}, u32[]{:S(2)}, u32[]{:S(2)}) collective-permute-start(bf16[2048,128]{1,0:T(8,128)(2,1)S(1)} %collective-permute-done.6.refs_4_), channel_id=1, source_target_pairs={{0,12},{1,13},{2,14},{3,15},{4,0},{5,1},{6,2},{7,3},{8,4},{9,5},{1... | collective-permute-start | bytes 1572872 | tf_op jit(solution)/shard_map/ppermute | solution.py:56
  41.9 1.4 collective-permute-done.3.refs_1_
  44.5 2.1 collective-permute-done.5.refs_3_
  46.6 2.0 collective-permute-start.11
  53.3 2.4 %collective-permute-start.17 = (bf16[2048,128]{1,0:T(8,128)(2,1)}, bf16[2048,128]{1,0:T(8,128)(2,1)}, u32[]{:S(2)}, u32[]{:S(2)}) collective-permute-start(bf16[2048,128]{1,0:T(8,128)(2,1)} %collective-permute-done.14.refs_12_), channel_id=1, source_target_pairs={{0,12},{1,13},{2,14},{3,15},{4,0},{5,1},{6,2},{7,3},{8,4},{9,5},{1... | collective-permute-start | bytes 1572872 | tf_op jit(solution)/shard_map/ppermute | solution.py:56
  55.7 3.2 %collective-permute-done.12.refs_11_ = bf16[2048,128]{1,0:T(8,128)(2,1)S(1)} collective-permute-done((bf16[2048,128]{1,0:T(8,128)(2,1)}, bf16[2048,128]{1,0:T(8,128)(2,1)S(1)}, u32[]{:S(2)}, u32[]{:S(2)}) %collective-permute-start.12) | collective-permute-done | bytes 524320 | tf_op jit(solution)/shard_map/ppermute | solution.py:56
  59.7 2.9 %collective-permute-done.15.refs_13_ = bf16[2048,128]{1,0:T(8,128)(2,1)S(1)} collective-permute-done((bf16[2048,128]{1,0:T(8,128)(2,1)}, bf16[2048,128]{1,0:T(8,128)(2,1)S(1)}, u32[]{:S(2)}, u32[]{:S(2)}) %collective-permute-start.15) | collective-permute-done | bytes 524320 | tf_op jit(solution)/shard_map/ppermute | solution.py:56
  62.6 8.4 %collective-permute-start.26 = (bf16[2048,128]{1,0:T(8,128)(2,1)}, bf16[2048,128]{1,0:T(8,128)(2,1)}, u32[]{:S(2)}, u32[]{:S(2)}) collective-permute-start(bf16[2048,128]{1,0:T(8,128)(2,1)} %collective-permute-done.10.refs_8_), channel_id=1, source_target_pairs={{0,16},{1,17},{2,18},{3,19},{4,20},{5,21},{6,22},{7,23},{8,24},{9,... | collective-permute-start | bytes 1572872 | tf_op jit(solution)/shard_map/ppermute | solution.py:56
  73.9 2.3 %shard_map.106 = (bf16[256,256]{1,0:T(8,128)(2,1)}, bf16[256,256]{1,0:T(8,128)(2,1)}) custom-call(bf16[4,2,128,128]{3,2,1,0:T(8,128)(2,1)} %slice_bitcast_fusion.4.prop_ref), custom_call_target="tpu_custom_call" | custom-call | tf_op jit(solution)/shard_map/pallas_call | solution.py:330
  77.7 1.3 slice_bitcast_fusion
  79.8 2.1 collective-permute-done.4.refs_2_
  86.4 5.1 %collective-permute-done.9.refs_6_ = bf16[2048,128]{1,0:T(8,128)(2,1)} collective-permute-done((bf16[2048,128]{1,0:T(8,128)(2,1)}, bf16[2048,128]{1,0:T(8,128)(2,1)}, u32[]{:S(2)}, u32[]{:S(2)}) %collective-permute-start.9) | collective-permute-done | bytes 524320 | tf_op jit(solution)/shard_map/ppermute | solution.py:56
  92.4 4.8 %collective-permute-done.13.refs_10_ = bf16[2048,128]{1,0:T(8,128)(2,1)} collective-permute-done((bf16[2048,128]{1,0:T(8,128)(2,1)}, bf16[2048,128]{1,0:T(8,128)(2,1)}, u32[]{:S(2)}, u32[]{:S(2)}) %collective-permute-start.13) | collective-permute-done | bytes 524320 | tf_op jit(solution)/shard_map/ppermute | solution.py:56
  112.6 13.0 %shard_map.104 = (f32[2048,128]{1,0:T(8,128)S(1)}, bf16[2048,128]{1,0:T(8,128)(2,1)S(1)}, bf16[2048,128]{1,0:T(8,128)(2,1)S(1)}, bf16[2048,128]{1,0:T(8,128)(2,1)S(1)}) custom-call(s32[64]{0:T(128)S(1)} %reshape.265.count.n1, s32[256]{0:T(256)S(1)} %reshape.266.slots.s1, f32[256]{0:T(256)S(1)} %reshape.267.weights, bf16[128,128]{1,0:T(8,128)(2,1)S(1)} %copy-done.15, ...), custom_call_target="tpu_custom_call" | custom-call | flops 1000000000 | bytes 20971520 | tf_op jit(solution)/shard_map/pallas_call | solution.py:242
  126.7 2.1 collective-permute-start.36
  128.9 40.0 %shard_map.107 = (f32[2048,128]{1,0:T(8,128)S(1)}, bf16[2048,128]{1,0:T(8,128)(2,1)S(1)}, bf16[2048,128]{1,0:T(8,128)(2,1)S(1)}, bf16[2048,128]{1,0:T(8,128)(2,1)S(1)}) custom-call(s32[64]{0:T(128)S(1)} %reshape.265.count.n1, s32[256]{0:T(256)S(1)} %reshape.266.slots.s1, f32[256]{0:T(256)S(1)} %reshape.269.w1, s32[128]{0:T(128)S(1)} %reshape.272.n2, ...), custom_call_target="tpu_custom_call" | custom-call | flops 16000000000 | bytes 20971520 | tf_op jit(solution)/shard_map/pallas_call | solution.py:242
  169.0 2.6 %collective-permute-start.45 = (bf16[2048,128]{1,0:T(8,128)(2,1)S(1)}, bf16[2048,128]{1,0:T(8,128)(2,1)S(1)}, u32[]{:S(2)}, u32[]{:S(2)}) collective-permute-start(bf16[2048,128]{1,0:T(8,128)(2,1)S(1)} %get-tuple-element.25), channel_id=1, source_target_pairs={{0,64},{1,65},{2,66},{3,67},{4,68},{5,69},{6,70},{7,71},{8,72},{9,... | collective-permute-start | bytes 1572872 | tf_op jit(solution)/shard_map/ppermute | solution.py:56
  172.8 5.3 %shard_map.105 = (bf16[2048,128]{1,0:T(8,128)(2,1)S(1)}, f32[4,2,128,128]{3,2,1,0:T(8,128)S(1)}) custom-call(f32[8]{0:T(128)S(1)} %copy-done.16, bf16[2048,128]{1,0:T(8,128)(2,1)S(1)} %bitcast.73, f32[2048,128]{1,0:T(8,128)S(1)} %get-tuple-element.16.own_ref, bf16[2048,128]{1,0:T(8,128)(2,1)S(1)} %collective-permute-done.34.a_ref, ...), custom_call_target="tpu_custom_call" | custom-call | flops 2000000000 | bytes 6291456 | tf_op jit(solution)/shard_map/pallas_call | solution.py:296
  178.2 5.1 %collective-permute-done.44.a_ref = bf16[2048,128]{1,0:T(8,128)(2,1)S(1)} collective-permute-done((bf16[2048,128]{1,0:T(8,128)(2,1)S(1)}, bf16[2048,128]{1,0:T(8,128)(2,1)S(1)}, u32[]{:S(2)}, u32[]{:S(2)}) %collective-permute-start.44) | collective-permute-done | bytes 524320 | tf_op jit(solution)/shard_map/ppermute | solution.py:56
  183.2 10.4 %collective-permute-done.45.b_ref = bf16[2048,128]{1,0:T(8,128)(2,1)S(1)} collective-permute-done((bf16[2048,128]{1,0:T(8,128)(2,1)S(1)}, bf16[2048,128]{1,0:T(8,128)(2,1)S(1)}, u32[]{:S(2)}, u32[]{:S(2)}) %collective-permute-start.45) | collective-permute-done | bytes 524320 | tf_op jit(solution)/shard_map/ppermute | solution.py:56
  194.8 6.1 %shard_map.108 = (bf16[2048,128]{1,0:T(8,128)(2,1)}, f32[4,2,128,128]{3,2,1,0:T(8,128)S(1)}) custom-call(f32[8]{0:T(128)S(1)} %copy-done.16, bf16[2048,128]{1,0:T(8,128)(2,1)S(1)} %get-tuple-element.20.lam_ref, f32[2048,128]{1,0:T(8,128)S(1)} %get-tuple-element.23.own_ref, bf16[2048,128]{1,0:T(8,128)(2,1)S(1)} %collective-permute-done.44.a_ref, ...), custom_call_target="tpu_custom_call" | custom-call | flops 2000000000 | bytes 6291456 | tf_op jit(solution)/shard_map/pallas_call | solution.py:296
  201.6 20.7 %all_to_all.5 = bf16[128,8,2,128]{3,2,1,0:T(2,128)(2,1)S(1)} all-to-all(bf16[128,8,2,128]{3,2,1,0:T(2,128)(2,1)S(1)} %copy.115), channel_id=1, replica_groups=mesh['y'=4,'c'=2,'z'=4,'x'=4] {'y','c','z','x'}, dimensions={0} | all-to-all | bytes 1048576 | tf_op jit(solution)/shard_map/all_to_all | solution.py:373
  (206 shorter events, 52.2 us)
Async XLA Ops:
  2.3 15.7 %collective-permute-start.2 = (f32[8,16]{1,0:T(8,128)S(1)}, f32[8,16]{1,0:T(8,128)S(1)}, u32[]{:S(2)}, u32[]{:S(2)}) collective-permute-start(f32[8,16]{1,0:T(8,128)S(1)} %pad_maximum_fusion.7), channel_id=1, source_target_pairs={{0,32},{1,33},{2,34},{3,35},{4,36},{5,37},{6,38},{7,39},{8,40},{9,... | collective-permute-start | bytes 1544 | tf_op jit(solution)/shard_map/ppermute | solution.py:56
  4.5 13.6 %collective-permute-start.1 = (f32[8,16]{1,0:T(8,128)S(1)}, f32[8,16]{1,0:T(8,128)S(1)}, u32[]{:S(2)}, u32[]{:S(2)}) collective-permute-start(f32[8,16]{1,0:T(8,128)S(1)} %pad_maximum_fusion.7), channel_id=1, source_target_pairs={{0,64},{1,65},{2,66},{3,67},{4,68},{5,69},{6,70},{7,71},{8,72},{9,... | collective-permute-start | bytes 1544 | tf_op jit(solution)/shard_map/ppermute | solution.py:56
  7.1 11.0 %collective-permute-start = (f32[8,16]{1,0:T(8,128)S(1)}, f32[8,16]{1,0:T(8,128)S(1)}, u32[]{:S(2)}, u32[]{:S(2)}) collective-permute-start(f32[8,16]{1,0:T(8,128)S(1)} %pad_maximum_fusion.7), channel_id=1, source_target_pairs={{0,96},{1,97},{2,98},{3,99},{4,100},{5,101},{6,102},{7,103},{8,104... | collective-permute-start | bytes 1544 | tf_op jit(solution)/shard_map/ppermute | solution.py:56
  8.2 28.2 %collective-permute-start.6 = (bf16[2048,128]{1,0:T(8,128)(2,1)}, bf16[2048,128]{1,0:T(8,128)(2,1)S(1)}, u32[]{:S(2)}, u32[]{:S(2)}) collective-permute-start(bf16[2048,128]{1,0:T(8,128)(2,1)} %bitcast.65), channel_id=1, source_target_pairs={{0,1},{1,2},{2,3},{3,0},{4,5},{5,6},{6,7},{7,4},{8,9},{9,10},{10,1... | collective-permute-start | bytes 1572872 | tf_op jit(solution)/shard_map/ppermute | solution.py:56
  9.8 29.4 %collective-permute-start.10 = (bf16[2048,128]{1,0:T(8,128)(2,1)}, bf16[2048,128]{1,0:T(8,128)(2,1)}, u32[]{:S(2)}, u32[]{:S(2)}) collective-permute-start(bf16[2048,128]{1,0:T(8,128)(2,1)} %bitcast.66), channel_id=1, source_target_pairs={{0,2},{1,3},{2,0},{3,1},{4,6},{5,7},{6,4},{7,5},{8,10},{9,11},{10,... | collective-permute-start | bytes 1572872 | tf_op jit(solution)/shard_map/ppermute | solution.py:56
  19.9 6.1 %collective-permute-start.38 = (f32[64,16]{0,1:T(8,128)S(1)}, f32[64,16]{0,1:T(8,128)S(1)}, u32[]{:S(2)}, u32[]{:S(2)}) collective-permute-start(f32[64,16]{0,1:T(8,128)S(1)} %pad_maximum_fusion.6), channel_id=1, source_target_pairs={{0,4},{1,5},{2,6},{3,7},{4,8},{5,9},{6,10},{7,11},{8,12},{9,13},{1... | collective-permute-start | bytes 12296 | tf_op jit(solution)/shard_map/ppermute | solution.py:56
  31.3 10.6 %collective-permute-start.14 = (bf16[2048,128]{1,0:T(8,128)(2,1)S(1)}, bf16[2048,128]{1,0:T(8,128)(2,1)}, u32[]{:S(2)}, u32[]{:S(2)}) collective-permute-start(bf16[2048,128]{1,0:T(8,128)(2,1)S(1)} %bitcast.67), channel_id=1, source_target_pairs={{0,3},{1,0},{2,1},{3,2},{4,7},{5,4},{6,5},{7,6},{8,11},{9,8},{10,9... | collective-permute-start | bytes 1572872 | tf_op jit(solution)/shard_map/ppermute | solution.py:56
  33.6 9.6 %collective-permute-start.3 = (bf16[2048,128]{1,0:T(8,128)(2,1)S(1)}, bf16[2048,128]{1,0:T(8,128)(2,1)}, u32[]{:S(2)}, u32[]{:S(2)}) collective-permute-start(bf16[2048,128]{1,0:T(8,128)(2,1)S(1)} %bitcast.68), channel_id=1, source_target_pairs={{0,4},{1,5},{2,6},{3,7},{4,8},{5,9},{6,10},{7,11},{8,12},{9,13},{1... | collective-permute-start | bytes 1572872 | tf_op jit(solution)/shard_map/ppermute | solution.py:56
  33.6 13.0 %collective-permute-start.5 = (bf16[2048,128]{1,0:T(8,128)(2,1)S(1)}, bf16[2048,128]{1,0:T(8,128)(2,1)S(1)}, u32[]{:S(2)}, u32[]{:S(2)}) collective-permute-start(bf16[2048,128]{1,0:T(8,128)(2,1)S(1)} %bitcast.69), channel_id=1, source_target_pairs={{0,12},{1,13},{2,14},{3,15},{4,0},{5,1},{6,2},{7,3},{8,4},{9,5},{1... | collective-permute-start | bytes 1572872 | tf_op jit(solution)/shard_map/ppermute | solution.py:56
  36.3 12.3 %collective-permute-start.18 = (bf16[2048,128]{1,0:T(8,128)(2,1)S(1)}, bf16[2048,128]{1,0:T(8,128)(2,1)S(1)}, u32[]{:S(2)}, u32[]{:S(2)}) collective-permute-start(bf16[2048,128]{1,0:T(8,128)(2,1)S(1)} %bitcast.70), channel_id=1, source_target_pairs={{0,16},{1,17},{2,18},{3,19},{4,20},{5,21},{6,22},{7,23},{8,24},{9,... | collective-permute-start | bytes 1572872 | tf_op jit(solution)/shard_map/ppermute | solution.py:56
  39.2 14.0 %collective-permute-start.8 = (bf16[2048,128]{1,0:T(8,128)(2,1)S(1)}, bf16[2048,128]{1,0:T(8,128)(2,1)S(1)}, u32[]{:S(2)}, u32[]{:S(2)}) collective-permute-start(bf16[2048,128]{1,0:T(8,128)(2,1)S(1)} %collective-permute-done.6.refs_4_), channel_id=1, source_target_pairs={{0,12},{1,13},{2,14},{3,15},{4,0},{5,1},{6,2},{7,3},{8,4},{9,5},{1... | collective-permute-start | bytes 1572872 | tf_op jit(solution)/shard_map/ppermute | solution.py:56
  41.9 29.2 %collective-permute-start.7 = (bf16[2048,128]{1,0:T(8,128)(2,1)S(1)}, bf16[2048,128]{1,0:T(8,128)(2,1)S(1)}, u32[]{:S(2)}, u32[]{:S(2)}) collective-permute-start(bf16[2048,128]{1,0:T(8,128)(2,1)S(1)} %collective-permute-done.6.refs_4_), channel_id=1, source_target_pairs={{0,4},{1,5},{2,6},{3,7},{4,8},{5,9},{6,10},{7,11},{8,12},{9,13},{1... | collective-permute-start | bytes 1572872 | tf_op jit(solution)/shard_map/ppermute | solution.py:56
  43.3 15.6 %collective-permute-start.12 = (bf16[2048,128]{1,0:T(8,128)(2,1)}, bf16[2048,128]{1,0:T(8,128)(2,1)S(1)}, u32[]{:S(2)}, u32[]{:S(2)}) collective-permute-start(bf16[2048,128]{1,0:T(8,128)(2,1)} %collective-permute-done.10.refs_8_), channel_id=1, source_target_pairs={{0,12},{1,13},{2,14},{3,15},{4,0},{5,1},{6,2},{7,3},{8,4},{9,5},{1... | collective-permute-start | bytes 1572872 | tf_op jit(solution)/shard_map/ppermute | solution.py:56
  46.6 25.2 %collective-permute-start.11 = (bf16[2048,128]{1,0:T(8,128)(2,1)}, bf16[2048,128]{1,0:T(8,128)(2,1)S(1)}, u32[]{:S(2)}, u32[]{:S(2)}) collective-permute-start(bf16[2048,128]{1,0:T(8,128)(2,1)} %collective-permute-done.10.refs_8_), channel_id=1, source_target_pairs={{0,4},{1,5},{2,6},{3,7},{4,8},{5,9},{6,10},{7,11},{8,12},{9,13},{1... | collective-permute-start | bytes 1572872 | tf_op jit(solution)/shard_map/ppermute | solution.py:56
  49.4 13.2 %collective-permute-start.15 = (bf16[2048,128]{1,0:T(8,128)(2,1)}, bf16[2048,128]{1,0:T(8,128)(2,1)S(1)}, u32[]{:S(2)}, u32[]{:S(2)}) collective-permute-start(bf16[2048,128]{1,0:T(8,128)(2,1)} %collective-permute-done.14.refs_12_), channel_id=1, source_target_pairs={{0,4},{1,5},{2,6},{3,7},{4,8},{5,9},{6,10},{7,11},{8,12},{9,13},{1... | collective-permute-start | bytes 1572872 | tf_op jit(solution)/shard_map/ppermute | solution.py:56
  53.3 26.4 %collective-permute-start.17 = (bf16[2048,128]{1,0:T(8,128)(2,1)}, bf16[2048,128]{1,0:T(8,128)(2,1)}, u32[]{:S(2)}, u32[]{:S(2)}) collective-permute-start(bf16[2048,128]{1,0:T(8,128)(2,1)} %collective-permute-done.14.refs_12_), channel_id=1, source_target_pairs={{0,12},{1,13},{2,14},{3,15},{4,0},{5,1},{6,2},{7,3},{8,4},{9,5},{1... | collective-permute-start | bytes 1572872 | tf_op jit(solution)/shard_map/ppermute | solution.py:56
  58.9 24.0 %collective-permute-start.22 = (bf16[2048,128]{1,0:T(8,128)(2,1)S(1)}, bf16[2048,128]{1,0:T(8,128)(2,1)}, u32[]{:S(2)}, u32[]{:S(2)}) collective-permute-start(bf16[2048,128]{1,0:T(8,128)(2,1)S(1)} %collective-permute-done.6.refs_4_), channel_id=1, source_target_pairs={{0,16},{1,17},{2,18},{3,19},{4,20},{5,21},{6,22},{7,23},{8,24},{9,... | collective-permute-start | bytes 1572872 | tf_op jit(solution)/shard_map/ppermute | solution.py:56
  62.6 20.3 %collective-permute-start.26 = (bf16[2048,128]{1,0:T(8,128)(2,1)}, bf16[2048,128]{1,0:T(8,128)(2,1)}, u32[]{:S(2)}, u32[]{:S(2)}) collective-permute-start(bf16[2048,128]{1,0:T(8,128)(2,1)} %collective-permute-done.10.refs_8_), channel_id=1, source_target_pairs={{0,16},{1,17},{2,18},{3,19},{4,20},{5,21},{6,22},{7,23},{8,24},{9,... | collective-permute-start | bytes 1572872 | tf_op jit(solution)/shard_map/ppermute | solution.py:56
  71.1 13.0 %collective-permute-start.30 = (bf16[2048,128]{1,0:T(8,128)(2,1)}, bf16[2048,128]{1,0:T(8,128)(2,1)}, u32[]{:S(2)}, u32[]{:S(2)}) collective-permute-start(bf16[2048,128]{1,0:T(8,128)(2,1)} %collective-permute-done.14.refs_12_), channel_id=1, source_target_pairs={{0,16},{1,17},{2,18},{3,19},{4,20},{5,21},{6,22},{7,23},{8,24},{9,... | collective-permute-start | bytes 1572872 | tf_op jit(solution)/shard_map/ppermute | solution.py:56
  71.9 10.1 %collective-permute-start.4 = (bf16[2048,128]{1,0:T(8,128)(2,1)}, bf16[2048,128]{1,0:T(8,128)(2,1)}, u32[]{:S(2)}, u32[]{:S(2)}) collective-permute-start(bf16[2048,128]{1,0:T(8,128)(2,1)} %collective-permute-done.3.refs_1_), channel_id=1, source_target_pairs={{0,4},{1,5},{2,6},{3,7},{4,8},{5,9},{6,10},{7,11},{8,12},{9,13},{1... | collective-permute-start | bytes 1572872 | tf_op jit(solution)/shard_map/ppermute | solution.py:56
  82.9 8.6 %collective-permute-start.9 = (bf16[2048,128]{1,0:T(8,128)(2,1)}, bf16[2048,128]{1,0:T(8,128)(2,1)}, u32[]{:S(2)}, u32[]{:S(2)}) collective-permute-start(bf16[2048,128]{1,0:T(8,128)(2,1)} %copy-done.5), channel_id=1, source_target_pairs={{0,12},{1,13},{2,14},{3,15},{4,0},{5,1},{6,2},{7,3},{8,4},{9,5},{1... | collective-permute-start | bytes 1572872 | tf_op jit(solution)/shard_map/ppermute | solution.py:56
  83.0 14.2 %collective-permute-start.13 = (bf16[2048,128]{1,0:T(8,128)(2,1)}, bf16[2048,128]{1,0:T(8,128)(2,1)}, u32[]{:S(2)}, u32[]{:S(2)}) collective-permute-start(bf16[2048,128]{1,0:T(8,128)(2,1)} %copy-done.9), channel_id=1, source_target_pairs={{0,12},{1,13},{2,14},{3,15},{4,0},{5,1},{6,2},{7,3},{8,4},{9,5},{1... | collective-permute-start | bytes 1572872 | tf_op jit(solution)/shard_map/ppermute | solution.py:56
  84.1 13.9 %collective-permute-start.16 = (bf16[2048,128]{1,0:T(8,128)(2,1)}, bf16[2048,128]{1,0:T(8,128)(2,1)}, u32[]{:S(2)}, u32[]{:S(2)}) collective-permute-start(bf16[2048,128]{1,0:T(8,128)(2,1)} %copy-done.13), channel_id=1, source_target_pairs={{0,4},{1,5},{2,6},{3,7},{4,8},{5,9},{6,10},{7,11},{8,12},{9,13},{1... | collective-permute-start | bytes 1572872 | tf_op jit(solution)/shard_map/ppermute | solution.py:56
  85.4 14.5 %collective-permute-start.25 = (bf16[2048,128]{1,0:T(8,128)(2,1)}, bf16[2048,128]{1,0:T(8,128)(2,1)}, u32[]{:S(2)}, u32[]{:S(2)}) collective-permute-start(bf16[2048,128]{1,0:T(8,128)(2,1)} %copy-done.5), channel_id=1, source_target_pairs={{0,16},{1,17},{2,18},{3,19},{4,20},{5,21},{6,22},{7,23},{8,24},{9,... | collective-permute-start | bytes 1572872 | tf_op jit(solution)/shard_map/ppermute | solution.py:56
  86.3 14.1 %collective-permute-start.29 = (bf16[2048,128]{1,0:T(8,128)(2,1)}, bf16[2048,128]{1,0:T(8,128)(2,1)}, u32[]{:S(2)}, u32[]{:S(2)}) collective-permute-start(bf16[2048,128]{1,0:T(8,128)(2,1)} %copy-done.9), channel_id=1, source_target_pairs={{0,16},{1,17},{2,18},{3,19},{4,20},{5,21},{6,22},{7,23},{8,24},{9,... | collective-permute-start | bytes 1572872 | tf_op jit(solution)/shard_map/ppermute | solution.py:56
  91.5 9.0 %collective-permute-start.31 = (bf16[2048,128]{1,0:T(8,128)(2,1)}, bf16[2048,128]{1,0:T(8,128)(2,1)}, u32[]{:S(2)}, u32[]{:S(2)}) collective-permute-start(bf16[2048,128]{1,0:T(8,128)(2,1)} %copy-done.13), channel_id=1, source_target_pairs={{0,16},{1,17},{2,18},{3,19},{4,20},{5,21},{6,22},{7,23},{8,24},{9,... | collective-permute-start | bytes 1572872 | tf_op jit(solution)/shard_map/ppermute | solution.py:56
  125.6 45.9 %collective-permute-start.34 = (bf16[2048,128]{1,0:T(8,128)(2,1)S(1)}, bf16[2048,128]{1,0:T(8,128)(2,1)S(1)}, u32[]{:S(2)}, u32[]{:S(2)}) collective-permute-start(bf16[2048,128]{1,0:T(8,128)(2,1)S(1)} %get-tuple-element.17), channel_id=1, source_target_pairs={{0,32},{1,33},{2,34},{3,35},{4,36},{5,37},{6,38},{7,39},{8,40},{9,... | collective-permute-start | bytes 1572872 | tf_op jit(solution)/shard_map/ppermute | solution.py:56
  126.4 46.4 %collective-permute-start.35 = (bf16[2048,128]{1,0:T(8,128)(2,1)S(1)}, bf16[2048,128]{1,0:T(8,128)(2,1)S(1)}, u32[]{:S(2)}, u32[]{:S(2)}) collective-permute-start(bf16[2048,128]{1,0:T(8,128)(2,1)S(1)} %get-tuple-element.18), channel_id=1, source_target_pairs={{0,64},{1,65},{2,66},{3,67},{4,68},{5,69},{6,70},{7,71},{8,72},{9,... | collective-permute-start | bytes 1572872 | tf_op jit(solution)/shard_map/ppermute | solution.py:56
  126.7 46.1 %collective-permute-start.36 = (bf16[2048,128]{1,0:T(8,128)(2,1)S(1)}, bf16[2048,128]{1,0:T(8,128)(2,1)S(1)}, u32[]{:S(2)}, u32[]{:S(2)}) collective-permute-start(bf16[2048,128]{1,0:T(8,128)(2,1)S(1)} %get-tuple-element.19), channel_id=1, source_target_pairs={{0,96},{1,97},{2,98},{3,99},{4,100},{5,101},{6,102},{7,103},{8,104... | collective-permute-start | bytes 1572872 | tf_op jit(solution)/shard_map/ppermute | solution.py:56
  168.9 14.3 %collective-permute-start.44 = (bf16[2048,128]{1,0:T(8,128)(2,1)S(1)}, bf16[2048,128]{1,0:T(8,128)(2,1)S(1)}, u32[]{:S(2)}, u32[]{:S(2)}) collective-permute-start(bf16[2048,128]{1,0:T(8,128)(2,1)S(1)} %get-tuple-element.24), channel_id=1, source_target_pairs={{0,32},{1,33},{2,34},{3,35},{4,36},{5,37},{6,38},{7,39},{8,40},{9,... | collective-permute-start | bytes 1572872 | tf_op jit(solution)/shard_map/ppermute | solution.py:56
  169.0 24.6 %collective-permute-start.45 = (bf16[2048,128]{1,0:T(8,128)(2,1)S(1)}, bf16[2048,128]{1,0:T(8,128)(2,1)S(1)}, u32[]{:S(2)}, u32[]{:S(2)}) collective-permute-start(bf16[2048,128]{1,0:T(8,128)(2,1)S(1)} %get-tuple-element.25), channel_id=1, source_target_pairs={{0,64},{1,65},{2,66},{3,67},{4,68},{5,69},{6,70},{7,71},{8,72},{9,... | collective-permute-start | bytes 1572872 | tf_op jit(solution)/shard_map/ppermute | solution.py:56
  171.5 23.3 %collective-permute-start.46 = (bf16[2048,128]{1,0:T(8,128)(2,1)S(1)}, bf16[2048,128]{1,0:T(8,128)(2,1)S(1)}, u32[]{:S(2)}, u32[]{:S(2)}) collective-permute-start(bf16[2048,128]{1,0:T(8,128)(2,1)S(1)} %get-tuple-element.26), channel_id=1, source_target_pairs={{0,96},{1,97},{2,98},{3,99},{4,100},{5,101},{6,102},{7,103},{8,104... | collective-permute-start | bytes 1572872 | tf_op jit(solution)/shard_map/ppermute | solution.py:56
  (45 other events, 380.7 us)

commit v2 on v1

v2 whole, which is shorter than its diff:
```python
import functools

import jax
import jax.numpy as jnp
from jax import lax
from jax.experimental import pallas as pl
from jax.experimental.pallas import tpu as pltpu
from jax.sharding import Mesh
from jax.sharding import PartitionSpec as P

AXES = ("y", "c", "z", "x")
BF = jnp.bfloat16
F32 = jnp.float32
OWN = 8
MODES = 4
DIM = 128
ROWS = 2 * DIM
BLOCK = OWN * ROWS
GROUP = 4
EXTRA = 64


def pairs(move):
    out = []
    for y in range(4):
        for c in range(2):
            for z in range(4):
                for x in range(4):
                    ny, nc, nz, nx = move(y, c, z, x)
                    here = ((y * 2 + c) * 4 + z) * 4 + x
                    there = ((ny * 2 + nc) * 4 + nz) * 4 + nx
                    out.append((here, there))
    return out


def first(s):
    return pairs(lambda y, c, z, x: (y, c, z, (x + s) % 4) if c == 0 else (y, c, (z + s) % 4, x))


def second(s):
    return pairs(lambda y, c, z, x: (y, c, (z + s) % 4, x) if c == 0 else (y, c, z, (x + s) % 4))


def along_y(s):
    return pairs(lambda y, c, z, x: ((y + s) % 4, c, z, x))


SIBLING = pairs(lambda y, c, z, x: (y, 1 - c, z, x))


def send(a, route):
    return lax.ppermute(a, AXES, route)


def gather_layer(block, prepare):
    near = {0: block}
    for s in (1, 3, 2):
        near[s] = send(block, first(s))
    made = prepare(near[3])
    near[2], made = lax.optimization_barrier((near[2], made))
    held = {}
    for s in (0, 1, 3, 2):
        held[s, 0] = near[s]
        held[s, 1] = send(near[s], second(1))
        held[s, 3] = send(near[s], second(3))
        if s in (0, 3):
            held[s, 2] = send(held[s, 1], second(1))
        else:
            held[s, 2] = send(held[s, 3], second(3))
    mine = [held[s, t] for s in range(4) for t in range(4)]
    return made, mine + [send(b, SIBLING) for b in mine]


def own_meta(ladder, decay):
    top = lax.reduce_precision(decay, 8, 7)
    mid = lax.reduce_precision(decay - top, 8, 7)
    parts = [ladder[0].astype(F32), ladder[1].astype(F32), jnp.stack([top, mid, decay - top - mid], axis=1)]
    return jnp.concatenate(parts, axis=1)


def place(q, at):
    y, c, z, x = at
    owner = q >> 3
    oy, oc, oz, ox = owner >> 5, (owner >> 4) & 1, (owner >> 2) & 3, owner & 3
    dx, dz = (x - ox) & 3, (z - oz) & 3
    s = jnp.where(oc == 0, dx, dz)
    t = jnp.where(oc == 0, dz, dx)
    other = (oc != c).astype(jnp.int32)
    return (y - oy) & 3, ((other * 16 + s * 4 + t) << 3) + (q & 7)


def slot_of(q, at):
    dy, slot = place(q, at)
    return jnp.where(dy == 0, slot, -1)


def compact(slot, values):
    count = slot.shape[-1]
    keep = (slot >= 0) & (values[0] != 0)
    before = jnp.arange(count)[:, None] < jnp.arange(count)[None, :]
    at = jnp.sum((keep[..., :, None] & before).astype(jnp.int32), axis=-2)
    moved = keep[..., :, None] & (at[..., :, None] == jnp.arange(count))
    lists = [jnp.sum(jnp.where(moved, v[..., :, None], 0), axis=-2).reshape(-1) for v in [slot, *values]]
    return [jnp.sum(keep.astype(jnp.int32), axis=-1).reshape(-1), *lists]


def pick(rows, table):
    hot = (rows.reshape(-1)[:, None] == jnp.arange(table.shape[0])[None, :]).astype(BF)
    return jnp.dot(hot, table.astype(BF), preferred_element_type=F32)


def own_links(higher, lower, at):
    y, c, z, x = at
    rows = []
    for dy in range(4):
        start = ((((y + dy) & 3) * 2 + c) * 16 + z * 4 + x) * OWN
        both = [lax.dynamic_slice_in_dim(t, start, OWN, 0) for t in (higher, lower)]
        rows.append(jnp.concatenate(both, axis=1))
    return jnp.concatenate(rows)


def near_lists(partner, weights, at):
    return compact(slot_of(partner, at).reshape(32, 2, 4), [weights.reshape(32, 2, 4)])


def spread(v):
    return v.reshape(32, 2, 4, 2, 4).transpose(0, 1, 3, 2, 4).reshape(32, 64)


def far_tables(partner, higher, lower, strengths, at):
    dy, slot = place(partner, at)
    near = jnp.where(dy == 0, slot, -1).astype(F32)
    table = jnp.concatenate([slot_of(higher, at), slot_of(lower, at)], axis=1).astype(F32)
    far = spread(pick(partner, table))
    slots = jnp.concatenate([far, near, jnp.full((32, 56), -1, F32)], axis=1)
    up, down = strengths[0, :4], strengths[0, 4:]
    products = [(a[:, None] * b[None, :]).reshape(16) for a in (up, down) for b in (up, down)]
    scale = jnp.concatenate([*products, up, down, jnp.zeros((56,), F32)]).reshape(1, DIM)
    return (slot >> 3) * EXTRA + dy * 16 + (slot & 7), slots, scale


def copies_of(blocks, held, sems, start, rows):
    return [
        pltpu.make_async_copy(b.at[pl.ds(start, rows), :], held.at[pl.ds(k * rows, rows), :], sems.at[k])
        for k, b in enumerate(blocks)
    ]


def link_sum(held, slots, weights, base, count):
    def add(k, total):
        for n in (base + 2 * k, base + 2 * k + 1):
            start = pl.multiple_of(slots[n] * ROWS, ROWS)
            total = total + weights[n] * held[pl.ds(start, ROWS), :].astype(F32)
        return total

    return lax.fori_loop(0, (count + 1) >> 1, add, jnp.zeros((ROWS, DIM), F32))


def mm(a, b):
    return jnp.dot(a, b, preferred_element_type=F32)


def crossed(plus):
    return jnp.concatenate([plus[DIM:], -plus[:DIM]], axis=1)


def near_sums(order, held, count, slots, weights, c_ref, outs, lefts, rights):
    for dy, out in zip(order, outs):

        def links(i, _):
            d = (dy * OWN + i) * 2
            up = link_sum(held, slots, weights, d * 4, count[d])
            down = link_sum(held, slots, weights, d * 4 + 4, count[d + 1])
            lefts[i] = crossed((up + down).astype(BF))
            rights[i] = (up - down).astype(BF)
            return 0

        lax.fori_loop(0, OWN, links, 0)
        c = c_ref[...]
        for i in range(OWN):
            left, right = mm(c, lefts[i]), mm(rights[i], c)
            out[pl.ds(i * ROWS, DIM), :] = (left[:, :DIM] - right[DIM:]).astype(out.dtype)
            out[pl.ds(i * ROWS + DIM, DIM), :] = (left[:, DIM:] + right[:DIM]).astype(out.dtype)


def near_kernel(order, count, slots, weights, c_ref, *refs):
    blocks, outs = refs[:32], refs[32 : 32 + len(order)]
    held, sems, lefts, rights = refs[32 + len(order) :]
    copies = copies_of(blocks, held, sems, 0, BLOCK)
    for copy in copies:
        copy.start()
    for copy in copies:
        copy.wait()
    near_sums(order, held, count, slots, weights, c_ref, outs, lefts, rights)


def make_lists(row_ref, ladder_ref, scale_ref, slot_ref, table, code_v, weight_v):
    lane = lax.broadcasted_iota(jnp.int32, (32, DIM), 1)
    row = lax.broadcasted_iota(jnp.int32, (DIM, DIM), 0)
    col = lax.broadcasted_iota(jnp.int32, (DIM, DIM), 1)
    wide = lax.broadcasted_iota(jnp.int32, (32, 32 * EXTRA), 1)
    total = jnp.zeros((32, DIM), F32)
    for k in range(2 * MODES):
        hot = jnp.where(row_ref[:, k : k + 1] == wide, 1.0, 0.0).astype(BF)
        wanted = mm(hot, table[...])
        mine = ladder_ref[:, k : k + 1]
        target = ((k // 4) * 2 + (row >> 2)) * 16 + (k % 4) * 4 + (row & 3)
        shift = jnp.where((row < 2 * MODES) & (col == target), 1.0, 0.0).astype(BF)
        total = total + mm((wanted * mine).astype(BF), shift)
        decay = wanted[:, 8:9] + wanted[:, 9:10] + wanted[:, 10:11]
        total = jnp.where(lane == 64 + k, decay * mine, total)
    slot = slot_ref[...]
    keep = (slot >= 0) & (total != 0)
    kept = jnp.where(keep, 1.0, 0.0)
    spot = mm(kept.astype(BF), jnp.where(row < col, 1.0, 0.0).astype(BF)).astype(jnp.int32)
    spot = jnp.where(keep, spot, -1)
    kind = jnp.where(lane < 64, lane >> 4, 4 + ((lane - 64) >> 2)).astype(F32)
    code, weight = slot + 256.0 * kind, total * scale_ref[...]
    codes = jnp.where(lane == DIM - 1, jnp.sum(kept, axis=1, keepdims=True), 0.0)
    weights = jnp.zeros((32, DIM), F32)
    for n in range(72):
        here = spot == n
        codes = jnp.where(lane == n, jnp.sum(jnp.where(here, code, 0.0), axis=1, keepdims=True), codes)
        weights = jnp.where(lane == n, jnp.sum(jnp.where(here, weight, 0.0), axis=1, keepdims=True), weights)
    code_v[...] = codes.astype(jnp.int32)
    weight_v[...] = weights


def far_kernel(order, c_ref, right_ref, left_ref, row_ref, ladder_ref, scale_ref, slot_ref, *refs):
    blocks, outs = refs[:32], refs[32 : 32 + len(order)]
    held, extra, main_sems, extra_sems, *rest = refs[32 + len(order) :]
    acc, lefts, rights, kept, double, code_v, weight_v, code_s, weight_s, sems = rest
    tails = copies_of(blocks, extra, extra_sems, BLOCK, EXTRA)
    mains = copies_of(blocks, held, main_sems, 0, BLOCK)
    for copy in tails + mains:
        copy.start()
    for copy in tails:
        copy.wait()
    make_lists(row_ref, ladder_ref, scale_ref, slot_ref, extra, code_v, weight_v)
    codes = pltpu.make_async_copy(code_v, code_s, sems.at[0])
    weights = pltpu.make_async_copy(weight_v, weight_s, sems.at[1])
    codes.start()
    weights.start()
    c = c_ref[...]
    double[0:DIM, 0:DIM] = c
    double[0:DIM, DIM:ROWS] = c
    double[DIM:ROWS, 0:DIM] = c
    double[DIM:ROWS, DIM:ROWS] = -c
    codes.wait()
    weights.wait()
    for copy in mains:
        copy.wait()
    for dy, out in zip(order, outs):

        def group(h, _):
            def links(g, _):
                d = dy * OWN + h * GROUP + g
                for k in range(6):
                    acc[k] = jnp.zeros((ROWS, DIM), F32)

                def add(e, _):
                    for n in (2 * e, 2 * e + 1):
                        code, weight = code_s[d, n], weight_s[d, n]
                        start = pl.multiple_of((code & 255) * ROWS, ROWS)
                        kind = code >> 8
                        acc[kind] = acc[kind] + weight * held[pl.ds(start, ROWS), :].astype(F32)
                    return 0

                lax.fori_loop(0, (code_s[d, DIM - 1] + 1) >> 1, add, 0)
                kept[g, 0] = acc[4] + acc[5]
                kept[g, 1] = acc[4] - acc[5]
                lefts[g, 0:DIM] = crossed((acc[0] + acc[1]).astype(BF))
                lefts[g, DIM:ROWS] = crossed((acc[2] + acc[3]).astype(BF))
                rights[g, :, 0:DIM] = (acc[0] - acc[1]).astype(BF)
                rights[g, :, DIM:ROWS] = (acc[2] - acc[3]).astype(BF)
                return 0

            lax.fori_loop(0, GROUP, links, 0)
            c, cc, w, wh = c_ref[...], double[...], right_ref[...], left_ref[...]
            turned = []
            for g in range(GROUP):
                left, right = mm(cc, lefts[g]), mm(rights[g], cc)
                halves = []
                for k in range(2):
                    side, cols = left[k * DIM : (k + 1) * DIM], right[:, k * DIM : (k + 1) * DIM]
                    re = kept[g, k, 0:DIM] + side[:, :DIM] - cols[DIM:]
                    im = kept[g, k, DIM:ROWS] + side[:, DIM:] + cols[:DIM]
                    halves.append(jnp.concatenate([re, im], axis=1).astype(BF))
                mid = mm(jnp.concatenate(halves), w).astype(BF)
                turned.append(mm(wh, stack_parts(mid)).astype(BF))
            for g in range(GROUP):
                left, right = mm(c, crossed(turned[g][:, :DIM])), mm(turned[g][:, DIM:], c)
                at = pl.multiple_of((h * GROUP + g) * ROWS, ROWS)
                out[pl.ds(at, DIM), :] = (left[:, :DIM] - right[DIM:]).astype(out.dtype)
                out[pl.ds(at + DIM, DIM), :] = (left[:, DIM:] + right[:DIM]).astype(out.dtype)
            return 0

        lax.fori_loop(0, OWN // GROUP, group, 0)


def stack_parts(mid):
    return jnp.concatenate(
        [
            jnp.concatenate([mid[:DIM, :DIM], mid[DIM:, :DIM]], axis=1),
            jnp.concatenate([mid[:DIM, DIM:], mid[DIM:, DIM:]], axis=1),
        ]
    )


SM = pl.BlockSpec(memory_space=pltpu.SMEM)
VM = pl.BlockSpec(memory_space=pltpu.VMEM)
FAR = pl.BlockSpec(memory_space=pltpu.HBM)


def part_shapes(order):
    return [jax.ShapeDtypeStruct((BLOCK, DIM), BF if dy else F32) for dy in order]


def near_scratch():
    return [pltpu.VMEM((OWN, DIM, ROWS), BF), pltpu.VMEM((OWN, ROWS, DIM), BF)]


def near_parts(order, lists, coupling, blocks):
    return pl.pallas_call(
        functools.partial(near_kernel, order),
        out_shape=part_shapes(order),
        in_specs=[SM] * 3 + [VM] + [FAR] * 32,
        out_specs=[VM] * len(order),
        scratch_shapes=[pltpu.VMEM((32 * BLOCK, DIM), BF), pltpu.SemaphoreType.DMA((32,))] + near_scratch(),
        compiler_params=pltpu.CompilerParams(vmem_limit_bytes=26 << 20),
        cost_estimate=pl.CostEstimate(flops=10**8, bytes_accessed=1 << 20, transcendentals=0),
    )(*lists, coupling, *blocks)


def far_parts(order, arrays, blocks):
    return pl.pallas_call(
        functools.partial(far_kernel, order),
        out_shape=part_shapes(order),
        in_specs=[VM] * len(arrays) + [FAR] * 32,
        out_specs=[VM] * len(order),
        scratch_shapes=[
            pltpu.VMEM((32 * BLOCK, DIM), BF),
            pltpu.VMEM((32 * EXTRA, DIM), BF),
            pltpu.SemaphoreType.DMA((32,)),
            pltpu.SemaphoreType.DMA((32,)),
            pltpu.VMEM((6, ROWS, DIM), F32),
            pltpu.VMEM((GROUP, ROWS, ROWS), BF),
            pltpu.VMEM((GROUP, ROWS, ROWS), BF),
            pltpu.VMEM((GROUP, 2, ROWS, DIM), F32),
            pltpu.VMEM((ROWS, ROWS), BF),
            pltpu.VMEM((32, DIM), jnp.int32),
            pltpu.VMEM((32, DIM), F32),
            pltpu.SMEM((32, DIM), jnp.int32),
            pltpu.SMEM((32, DIM), F32),
            pltpu.SemaphoreType.DMA((2,)),
        ],
        compiler_params=pltpu.CompilerParams(vmem_limit_bytes=30 << 20),
        cost_estimate=pl.CostEstimate(flops=10**8, bytes_accessed=1 << 20, transcendentals=0),
    )(*arrays, *blocks)


def chain_kernel(step, decay, lam_ref, own_ref, a_ref, b_ref, d_ref, right_ref, left_ref, saved_hbm, *refs):
    out_ref, grad_ref, wide, tall, saved_ref, sems = refs

    def saved_copy(u):
        return pltpu.make_async_copy(saved_hbm.at[step * 4 + u], saved_ref.at[u], sems.at[u])

    for u in range(4):
        saved_copy(u).start()
    for j in range(OWN):
        rows = pl.ds(j * ROWS, ROWS)
        mixed = decay[j] * lam_ref[rows, :].astype(F32) + own_ref[rows, :]
        mixed = mixed + a_ref[rows, :].astype(F32) + b_ref[rows, :].astype(F32) + d_ref[rows, :].astype(F32)
        mixed = mixed.astype(BF)
        wide[pl.ds(j * DIM, DIM), 0:DIM] = mixed[:DIM]
        wide[pl.ds(j * DIM, DIM), DIM:ROWS] = mixed[DIM:]

    def substep(u, _):
        right, left = right_ref[step * 4 + u], left_ref[step * 4 + u]
        for h in range(OWN // 2):
            mid = mm(wide[pl.ds(h * ROWS, ROWS), :], right).astype(BF)
            turned = mm(left, stack_parts(mid)).astype(BF)
            for k in range(2):
                re, im = turned[:DIM, k * DIM : (k + 1) * DIM], turned[DIM:, k * DIM : (k + 1) * DIM]
                j = 2 * h + k
                wide[pl.ds(j * DIM, DIM), 0:DIM] = re
                wide[pl.ds(j * DIM, DIM), DIM:ROWS] = im
                tall[pl.ds(j * ROWS, DIM), 0:DIM] = re
                tall[pl.ds(j * ROWS, DIM), DIM:ROWS] = im
                tall[pl.ds(j * ROWS + DIM, DIM), 0:DIM] = im
                tall[pl.ds(j * ROWS + DIM, DIM), DIM:ROWS] = -re
        saved_copy(u).wait()
        terms = lax.dot_general(
            saved_ref[u], tall[...], (((0,), (0,)), ((), ())), preferred_element_type=F32
        )
        grad_ref[u, 0] = terms[:, :DIM]
        grad_ref[u, 1] = terms[:, DIM:]
        return 0

    lax.fori_loop(0, 4, substep, 0)
    for j in range(OWN):
        out_ref[pl.ds(j * ROWS, DIM), :] = wide[pl.ds(j * DIM, DIM), 0:DIM]
        out_ref[pl.ds(j * ROWS + DIM, DIM), :] = wide[pl.ds(j * DIM, DIM), DIM:ROWS]


def chain(step, decay, lam, parts, right, left, saved):
    return pl.pallas_call(
        functools.partial(chain_kernel, step),
        out_shape=[
            jax.ShapeDtypeStruct((BLOCK, DIM), BF),
            jax.ShapeDtypeStruct((4, 2, DIM, DIM), F32),
        ],
        in_specs=[SM] + [VM] * 7 + [FAR],
        out_specs=[VM] * 2,
        scratch_shapes=[pltpu.VMEM((OWN * DIM, ROWS), BF), pltpu.VMEM((BLOCK, ROWS), BF), pltpu.VMEM((4, BLOCK, DIM), BF), pltpu.SemaphoreType.DMA((4,))],
        compiler_params=pltpu.CompilerParams(vmem_limit_bytes=8 << 20),
        cost_estimate=pl.CostEstimate(flops=10**8, bytes_accessed=1 << 20, transcendentals=0),
    )(decay, lam, *parts, right, left, saved)


def fill_right(out, re, im):
    out[0:DIM, 0:DIM] = re
    out[0:DIM, DIM:ROWS] = im
    out[DIM:ROWS, 0:DIM] = -im
    out[DIM:ROWS, DIM:ROWS] = re


def sides_kernel(prop_ref, whole_right, whole_left, right_ref, left_ref):
    for n in range(8):
        re, im = prop_ref[n, 0], prop_ref[n, 1]
        fill_right(right_ref.at[n], re, im)
        fill_right(left_ref.at[n], re.T, im.T)
    hi = lambda v: v.astype(BF)
    re, im = prop_ref[0, 0].astype(F32), prop_ref[0, 1].astype(F32)
    for u in range(1, 4):
        ur, ui = prop_ref[u, 0], prop_ref[u, 1]
        mul = lambda v, m: mm(hi(v), m) + mm(hi(v - hi(v).astype(F32)), m)
        re, im = mul(re, ur) - mul(im, ui), mul(re, ui) + mul(im, ur)
    fill_right(whole_right, hi(re), hi(im))
    fill_right(whole_left, hi(re.T), hi(im.T))


def sides(props):
    return pl.pallas_call(
        sides_kernel,
        out_shape=[jax.ShapeDtypeStruct((ROWS, ROWS), BF)] * 2 + [jax.ShapeDtypeStruct((8, ROWS, ROWS), BF)] * 2,
        in_specs=[VM],
        out_specs=[VM] * 4,
        compiler_params=pltpu.CompilerParams(vmem_limit_bytes=8 << 20),
    )(props)


def body(adjoint, saved, propagators, coupling, higher, lower, ladder, rates, decay):
    at = tuple(lax.axis_index(a) for a in AXES)
    lam = adjoint.reshape(BLOCK, DIM)
    meta = jnp.pad(own_meta(ladder, decay), ((0, 0), (0, 5)))
    by_y = [meta] + [send(meta, along_y(s)) for s in (1, 2, 3)]
    ladders = jnp.concatenate([by_y[(4 - dy) % 4][:, :8] for dy in range(4)])
    tail = jnp.pad(jnp.stack(by_y).astype(BF), ((0, 0), (0, 16 - OWN), (0, DIM - 16))).reshape(EXTRA, DIM)
    strengths = rates.reshape(1, 8)

    def prepare(arrived):
        tied = (propagators, higher, lower, ladders, strengths, arrived)
        props, up, down, wanted, factors, _ = lax.optimization_barrier(tied)
        partner = own_links(up, down, at)
        near = near_lists(partner, wanted * factors, at)
        return near, far_tables(partner, up, down, factors, at), sides(props.reshape(8, 2, DIM, DIM))

    made, blocks = gather_layer(jnp.concatenate([lam, tail]), prepare)
    one_list, (rows, slots, scale), (whole_right, whole_left, right, left) = made
    one_2, one_1, one_3, one_0 = near_parts((2, 1, 3, 0), one_list, coupling, blocks)
    got_one = [one_0] + [send(p, along_y(s)) for p, s in ((one_2, 2), (one_1, 1), (one_3, 3))]
    arrays = [coupling, whole_right, whole_left, rows, ladders, scale, slots]
    two_2, two_1, two_3 = far_parts((2, 1, 3), arrays, blocks)
    got_two = [send(p, along_y(s)) for p, s in ((two_2, 2), (two_1, 1), (two_3, 3))]
    [two_0] = far_parts((0,), arrays, blocks)
    got_two = [two_0] + got_two
    saved = saved.reshape(8, BLOCK, DIM)
    lam, grad_one = chain(0, decay, lam, got_one, right, left, saved)
    lam, grad_two = chain(1, decay, lam, got_two, right, left, saved)
    grad = jnp.concatenate([grad_one, grad_two]).astype(BF)
    grad = jnp.moveaxis(grad, 2, 0)
    grad = lax.all_to_all(grad, AXES, 0, 0, tiled=True)
    grad = jnp.sum(grad.astype(F32), axis=0, keepdims=True)
    return lam.reshape(OWN, 2, DIM, DIM), grad


def solution(mesh):
    finer = Mesh(mesh.devices.reshape(4, 2, 4, 4), AXES)
    rows = P(AXES)
    return jax.shard_map(
        body,
        mesh=finer,
        in_specs=(rows, P(None, None, AXES), P(), P(), P(), P(), P(None, AXES), P(), rows),
        out_specs=(rows, rows),
        check_vma=False,
    )
```

time: 224 us -> 203 us (0.906)
  starting transfers between devices: 60.2 us -> 49.8 us
  Pallas kernels: 66.8 us -> 60.4 us
  waiting for transfers between devices: 44.1 us -> 41.8 us
    ppermute x47 -> x40, starting transfers between devices: 60.2 us -> 49.8 us  [send(): return lax.ppermute(a, AXES, route)]
    pallas_call x5 -> x6, Pallas kernels: 66.8 us -> 60.4 us  [the longest x2 39.5 us: far_parts(): pl.pallas_call(functools.partial(far_kernel, order), out_shape=part_shape...]
    mul x4 -> x6, local copies, waits for them, and re-layouts: 0.3 us -> 5.3 us  [the longest x5 5.24 us: far_tables(): a[:, None] * b[None, :]]
    unnamed x62 -> x38, local copies, waits for them, and re-layouts: 9.75 us -> 5.1 us
    squeeze x5 -> x0, local copies, waits for them, and re-layouts: 4.4 us -> none  [the longest x3 2.4 us: body(): lam, grad_two = chain(decay, lam, got_two, right[1], left[1], saved[1])]
    ppermute x47 -> x40, waiting for transfers between devices: 44.1 us -> 41.8 us  [send(): return lax.ppermute(a, AXES, route)]
  transfers between devices with their start and end apart: 47 -> 40, of which waited for: 19 -> 16; matrix products, arithmetic and copies ran while one was open for 8% -> 9% of each run, Pallas kernels for 21% -> 23%
where the time goes in v2:
time: 203 us; the launch traced here: 202 us
  Pallas kernels  60.4 us (30%)
  starting transfers between devices  49.8 us (25%)
  waiting for transfers between devices  41.8 us (21%)
  blocking collectives  22 us (11%)
  local copies, waits for them, and re-layouts  19.9 us (10%)
  other arithmetic  6.38 us (3%)
    ppermute x40, starting transfers between devices, send(): return lax.ppermute(a, AXES, route)  49.8 us
    ppermute x40, waiting for transfers between devices, send(): return lax.ppermute(a, AXES, route)  41.8 us
    pallas_call x2, Pallas kernels, far_parts(): pl.pallas_call(functools.partial(far_kernel, order), out_shape=part_shape...  39.5 us
    all_to_all x1, blocking collectives, body(): grad = lax.all_to_all(grad, AXES, 0, 0, tiled=True)  22 us
    pallas_call x2, Pallas kernels, chain(): pl.pallas_call(functools.partial(chain_kernel, step), out_shape=[jax.Shap...  13.2 us
    pallas_call x1, Pallas kernels, near_parts(): pl.pallas_call(functools.partial(near_kernel, order), out_shape=part_shap...  6.97 us
    mul x5, local copies, waits for them, and re-layouts, far_tables(): a[:, None] * b[None, :]  5.24 us
    unnamed x38, local copies, waits for them, and re-layouts  5.1 us
  transfers between devices with their start and end apart: 40, of which 16 were waited for; matrix products, arithmetic and copies ran while one was open for 9% of the time, Pallas kernels for 23%

profile of v2, /device:TPU:1, one launch (start us, length us, event | category | flops | bytes accessed | tf_op | source)
XLA Modules:
  0.0 202.2 jit_solution(4970267610875129293)
XLA Ops:
  2.5 3.6 %collective-permute-start.2 = (f32[8,16]{1,0:T(8,128)S(1)}, f32[8,16]{1,0:T(8,128)S(1)}, u32[]{:S(2)}, u32[]{:S(2)}) collective-permute-start(f32[8,16]{1,0:T(8,128)S(1)} %pad.8), channel_id=1, source_target_pairs={{0,96},{1,97},{2,98},{3,99},{4,100},{5,101},{6,102},{7,103},{8,104... | collective-permute-start | bytes 1544 | tf_op jit(solution)/shard_map/ppermute | solution.py:52
  7.2 2.9 %collective-permute-done.1 = f32[8,16]{1,0:T(8,128)S(1)} collective-permute-done((f32[8,16]{1,0:T(8,128)S(1)}, f32[8,16]{1,0:T(8,128)S(1)}, u32[]{:S(2)}, u32[]{:S(2)}) %collective-permute-start.1) | collective-permute-done | bytes 544 | tf_op jit(solution)/shard_map/ppermute | solution.py:52
  11.2 3.8 %collective-permute-start.4 = (bf16[2112,128]{1,0:T(8,128)(2,1)S(1)}, bf16[2112,128]{1,0:T(8,128)(2,1)S(1)}, u32[]{:S(2)}, u32[]{:S(2)}) collective-permute-start(bf16[2112,128]{1,0:T(8,128)(2,1)S(1)} %pad_maximum_fusion.refs_0_), channel_id=1, source_target_pairs={{0,3},{1,0},{2,1},{3,2},{4,7},{5,4},{6,5},{7,6},{8,11},{9,8},{10,9... | collective-permute-start | bytes 1622024 | tf_op jit(solution)/shard_map/ppermute | solution.py:52
  15.8 1.3 collective-permute-start.5
  17.0 1.5 collective-permute-start.7
  19.2 9.9 %collective-permute-done.4.refs_12_ = bf16[2112,128]{1,0:T(8,128)(2,1)S(1)} collective-permute-done((bf16[2112,128]{1,0:T(8,128)(2,1)S(1)}, bf16[2112,128]{1,0:T(8,128)(2,1)S(1)}, u32[]{:S(2)}, u32[]{:S(2)}) %collective-permute-start.4) | collective-permute-done | bytes 540704 | tf_op jit(solution)/shard_map/ppermute | solution.py:52
  36.0 1.4 copy.124
  39.9 1.3 mul.195
  41.2 1.3 mul.197
  46.8 1.3 concatenate.79
  52.1 1.6 collective-permute-start.10
  54.4 2.0 collective-permute-start.13
  56.4 4.2 %collective-permute-done.6.refs_2_ = bf16[2112,128]{1,0:T(8,128)(2,1)S(1)} collective-permute-done((bf16[2112,128]{1,0:T(8,128)(2,1)S(1)}, bf16[2112,128]{1,0:T(8,128)(2,1)S(1)}, u32[]{:S(2)}, u32[]{:S(2)}) %collective-permute-start.6) | collective-permute-done | bytes 540704 | tf_op jit(solution)/shard_map/ppermute | solution.py:52
  60.6 5.8 %collective-permute-done.9.refs_5_ = bf16[2112,128]{1,0:T(8,128)(2,1)S(1)} collective-permute-done((bf16[2112,128]{1,0:T(8,128)(2,1)S(1)}, bf16[2112,128]{1,0:T(8,128)(2,1)S(1)}, u32[]{:S(2)}, u32[]{:S(2)}) %collective-permute-start.9) | collective-permute-done | bytes 540704 | tf_op jit(solution)/shard_map/ppermute | solution.py:52
  66.4 1.5 collective-permute-start.17
  67.8 5.3 %collective-permute-start.19 = (bf16[2112,128]{1,0:T(8,128)(2,1)S(1)}, bf16[2112,128]{1,0:T(8,128)(2,1)S(1)}, u32[]{:S(2)}, u32[]{:S(2)}) collective-permute-start(bf16[2112,128]{1,0:T(8,128)(2,1)S(1)} %collective-permute-done.5.refs_1_), channel_id=1, source_target_pairs={{0,16},{1,17},{2,18},{3,19},{4,20},{5,21},{6,22},{7,23},{8,24},{9,... | collective-permute-start | bytes 1622024 | tf_op jit(solution)/shard_map/ppermute | solution.py:52
  73.1 3.8 %collective-permute-start.21 = (bf16[2112,128]{1,0:T(8,128)(2,1)S(1)}, bf16[2112,128]{1,0:T(8,128)(2,1)S(1)}, u32[]{:S(2)}, u32[]{:S(2)}) collective-permute-start(bf16[2112,128]{1,0:T(8,128)(2,1)S(1)} %collective-permute-done.7.refs_3_), channel_id=1, source_target_pairs={{0,16},{1,17},{2,18},{3,19},{4,20},{5,21},{6,22},{7,23},{8,24},{9,... | collective-permute-start | bytes 1622024 | tf_op jit(solution)/shard_map/ppermute | solution.py:52
  78.0 4.7 %collective-permute-start.26 = (bf16[2112,128]{1,0:T(8,128)(2,1)S(1)}, bf16[2112,128]{1,0:T(8,128)(2,1)S(1)}, u32[]{:S(2)}, u32[]{:S(2)}) collective-permute-start(bf16[2112,128]{1,0:T(8,128)(2,1)S(1)} %collective-permute-done.3.refs_8_), channel_id=1, source_target_pairs={{0,16},{1,17},{2,18},{3,19},{4,20},{5,21},{6,22},{7,23},{8,24},{9,... | collective-permute-start | bytes 1622024 | tf_op jit(solution)/shard_map/ppermute | solution.py:52
  82.7 3.5 %collective-permute-start.11 = (bf16[2112,128]{1,0:T(8,128)(2,1)S(1)}, bf16[2112,128]{1,0:T(8,128)(2,1)S(1)}, u32[]{:S(2)}, u32[]{:S(2)}) collective-permute-start(bf16[2112,128]{1,0:T(8,128)(2,1)S(1)} %collective-permute-done.10.refs_7_), channel_id=1, source_target_pairs={{0,12},{1,13},{2,14},{3,15},{4,0},{5,1},{6,2},{7,3},{8,4},{9,5},{1... | collective-permute-start | bytes 1622024 | tf_op jit(solution)/shard_map/ppermute | solution.py:52
  86.3 1.4 collective-permute-start.16
  88.2 4.3 %collective-permute-done.11.refs_6_ = bf16[2112,128]{1,0:T(8,128)(2,1)S(1)} collective-permute-done((bf16[2112,128]{1,0:T(8,128)(2,1)S(1)}, bf16[2112,128]{1,0:T(8,128)(2,1)S(1)}, u32[]{:S(2)}, u32[]{:S(2)}) %collective-permute-start.11) | collective-permute-done | bytes 540704 | tf_op jit(solution)/shard_map/ppermute | solution.py:52
  92.9 5.3 %collective-permute-done.14.refs_10_ = bf16[2112,128]{1,0:T(8,128)(2,1)S(1)} collective-permute-done((bf16[2112,128]{1,0:T(8,128)(2,1)S(1)}, bf16[2112,128]{1,0:T(8,128)(2,1)S(1)}, u32[]{:S(2)}, u32[]{:S(2)}) %collective-permute-start.14) | collective-permute-done | bytes 540704 | tf_op jit(solution)/shard_map/ppermute | solution.py:52
  107.0 7.0 %shard_map.105 = (bf16[2048,128]{1,0:T(8,128)(2,1)S(1)}, bf16[2048,128]{1,0:T(8,128)(2,1)S(1)}, bf16[2048,128]{1,0:T(8,128)(2,1)S(1)}, f32[2048,128]{1,0:T(8,128)S(1)}) custom-call(s32[64]{0:T(128)S(1)} %copy-done.12, s32[256]{0:T(256)S(1)} %copy-done.10, f32[256]{0:T(256)S(1)} %copy-done.11, bf16[128,128]{1,0:T(8,128)(2,1)S(1)} %copy-done.7, ...), custom_call_target="tpu_custom_call" | custom-call | flops 100000000 | bytes 1048576 | tf_op jit(solution)/shard_map/pallas_call | solution.py:324
  114.0 1.9 collective-permute-start.34
  115.9 2.7 %collective-permute-start.36 = (bf16[2048,128]{1,0:T(8,128)(2,1)S(1)}, bf16[2048,128]{1,0:T(8,128)(2,1)S(1)}, u32[]{:S(2)}, u32[]{:S(2)}) collective-permute-start(bf16[2048,128]{1,0:T(8,128)(2,1)S(1)} %get-tuple-element.49), channel_id=1, source_target_pairs={{0,96},{1,97},{2,98},{3,99},{4,100},{5,101},{6,102},{7,103},{8,104... | collective-permute-start | bytes 1572872 | tf_op jit(solution)/shard_map/ppermute | solution.py:52
  118.6 26.5 %shard_map.108 = (bf16[2048,128]{1,0:T(8,128)(2,1)S(1)}, bf16[2048,128]{1,0:T(8,128)(2,1)S(1)}, bf16[2048,128]{1,0:T(8,128)(2,1)S(1)}) custom-call(bf16[128,128]{1,0:T(8,128)(2,1)S(1)} %copy-done.7, bf16[256,256]{1,0:T(8,128)(2,1)S(1)} %get-tuple-element.53.right_ref, bf16[256,256]{1,0:T(8,128)(2,1)S(1)} %get-tuple-element.54.left_ref, ...), custom_call_target="tpu_custom_call" | custom-call | flops 100000000 | bytes 1048576 | tf_op jit(solution)/shard_map/pallas_call | solution.py:336
  146.4 2.0 collective-permute-start.39
  148.3 13.0 %shard_map.107.own_ref = f32[2048,128]{1,0:T(8,128)S(1)} custom-call(bf16[128,128]{1,0:T(8,128)(2,1)S(1)} %copy-done.7, bf16[256,256]{1,0:T(8,128)(2,1)S(1)} %get-tuple-element.53.right_ref, bf16[256,256]{1,0:T(8,128)(2,1)S(1)} %get-tuple-element.54.left_ref, s32[32,8]{1,0:T(8,128)S(1)} %get-tuple-element.55.row_ref, ...), custom_call_target="tpu_custom_call" | custom-call | flops 100000000 | bytes 1048576 | tf_op jit(solution)/shard_map/pallas_call | solution.py:336
  161.5 6.2 %shard_map.106 = (bf16[2048,128]{1,0:T(8,128)(2,1)S(1)}, f32[4,2,128,128]{3,2,1,0:T(8,128)S(1)}) custom-call(f32[8]{0:T(128)S(1)} %copy-done.9, bf16[2048,128]{1,0:T(8,128)(2,1)S(1)} %bitcast.47, f32[2048,128]{1,0:T(8,128)S(1)} %get-tuple-element.46.own_ref, bf16[2048,128]{1,0:T(8,128)(2,1)S(1)} %collective-permute-done.34.a_ref, ...), custom_call_target="tpu_custom_call" | custom-call | flops 100000000 | bytes 1048576 | tf_op jit(solution)/shard_map/pallas_call | solution.py:407
  167.7 3.8 %collective-permute-done.38.b_ref = bf16[2048,128]{1,0:T(8,128)(2,1)S(1)} collective-permute-done((bf16[2048,128]{1,0:T(8,128)(2,1)S(1)}, bf16[2048,128]{1,0:T(8,128)(2,1)S(1)}, u32[]{:S(2)}, u32[]{:S(2)}) %collective-permute-start.38) | collective-permute-done | bytes 524320 | tf_op jit(solution)/shard_map/ppermute | solution.py:52
  171.4 7.0 %shard_map.109 = (bf16[2048,128]{1,0:T(8,128)(2,1)}, f32[4,2,128,128]{3,2,1,0:T(8,128)S(1)}) custom-call(f32[8]{0:T(128)S(1)} %copy-done.9, bf16[2048,128]{1,0:T(8,128)(2,1)S(1)} %get-tuple-element.52.lam_ref, f32[2048,128]{1,0:T(8,128)S(1)} %shard_map.107.own_ref, bf16[2048,128]{1,0:T(8,128)(2,1)S(1)} %collective-permute-done.37.a_ref, ...), custom_call_target="tpu_custom_call" | custom-call | flops 100000000 | bytes 1048576 | tf_op jit(solution)/shard_map/pallas_call | solution.py:407
  179.1 22.0 %all_to_all.5 = bf16[128,8,2,128]{3,2,1,0:T(2,128)(2,1)S(1)} all-to-all(bf16[128,8,2,128]{3,2,1,0:T(2,128)(2,1)S(1)} %copy.125), channel_id=1, replica_groups=mesh['y'=4,'c'=2,'z'=4,'x'=4] {'y','c','z','x'}, dimensions={0} | all-to-all | bytes 1048576 | tf_op jit(solution)/shard_map/all_to_all | solution.py:483
  (153 shorter events, 37.5 us)
Async XLA Ops:
  2.5 4.6 %collective-permute-start.2 = (f32[8,16]{1,0:T(8,128)S(1)}, f32[8,16]{1,0:T(8,128)S(1)}, u32[]{:S(2)}, u32[]{:S(2)}) collective-permute-start(f32[8,16]{1,0:T(8,128)S(1)} %pad.8), channel_id=1, source_target_pairs={{0,96},{1,97},{2,98},{3,99},{4,100},{5,101},{6,102},{7,103},{8,104... | collective-permute-start | bytes 1544 | tf_op jit(solution)/shard_map/ppermute | solution.py:52
  6.1 4.0 %collective-permute-start.1 = (f32[8,16]{1,0:T(8,128)S(1)}, f32[8,16]{1,0:T(8,128)S(1)}, u32[]{:S(2)}, u32[]{:S(2)}) collective-permute-start(f32[8,16]{1,0:T(8,128)S(1)} %pad.8), channel_id=1, source_target_pairs={{0,64},{1,65},{2,66},{3,67},{4,68},{5,69},{6,70},{7,71},{8,72},{9,... | collective-permute-start | bytes 1544 | tf_op jit(solution)/shard_map/ppermute | solution.py:52
  11.2 17.9 %collective-permute-start.4 = (bf16[2112,128]{1,0:T(8,128)(2,1)S(1)}, bf16[2112,128]{1,0:T(8,128)(2,1)S(1)}, u32[]{:S(2)}, u32[]{:S(2)}) collective-permute-start(bf16[2112,128]{1,0:T(8,128)(2,1)S(1)} %pad_maximum_fusion.refs_0_), channel_id=1, source_target_pairs={{0,3},{1,0},{2,1},{3,2},{4,7},{5,4},{6,5},{7,6},{8,11},{9,8},{10,9... | collective-permute-start | bytes 1622024 | tf_op jit(solution)/shard_map/ppermute | solution.py:52
  15.8 33.9 %collective-permute-start.3 = (bf16[2112,128]{1,0:T(8,128)(2,1)S(1)}, bf16[2112,128]{1,0:T(8,128)(2,1)S(1)}, u32[]{:S(2)}, u32[]{:S(2)}) collective-permute-start(bf16[2112,128]{1,0:T(8,128)(2,1)S(1)} %pad_maximum_fusion.refs_0_), channel_id=1, source_target_pairs={{0,2},{1,3},{2,0},{3,1},{4,6},{5,7},{6,4},{7,5},{8,10},{9,11},{10,... | collective-permute-start | bytes 1622024 | tf_op jit(solution)/shard_map/ppermute | solution.py:52
  15.8 33.9 %collective-permute-start.5 = (bf16[2112,128]{1,0:T(8,128)(2,1)S(1)}, bf16[2112,128]{1,0:T(8,128)(2,1)S(1)}, u32[]{:S(2)}, u32[]{:S(2)}) collective-permute-start(bf16[2112,128]{1,0:T(8,128)(2,1)S(1)} %pad_maximum_fusion.refs_0_), channel_id=1, source_target_pairs={{0,4},{1,5},{2,6},{3,7},{4,8},{5,9},{6,10},{7,11},{8,12},{9,13},{1... | collective-permute-start | bytes 1622024 | tf_op jit(solution)/shard_map/ppermute | solution.py:52
  17.0 36.7 %collective-permute-start.7 = (bf16[2112,128]{1,0:T(8,128)(2,1)S(1)}, bf16[2112,128]{1,0:T(8,128)(2,1)S(1)}, u32[]{:S(2)}, u32[]{:S(2)}) collective-permute-start(bf16[2112,128]{1,0:T(8,128)(2,1)S(1)} %pad_maximum_fusion.refs_0_), channel_id=1, source_target_pairs={{0,12},{1,13},{2,14},{3,15},{4,0},{5,1},{6,2},{7,3},{8,4},{9,5},{1... | collective-permute-start | bytes 1622024 | tf_op jit(solution)/shard_map/ppermute | solution.py:52
  18.5 32.3 %collective-permute-start.8 = (bf16[2112,128]{1,0:T(8,128)(2,1)S(1)}, bf16[2112,128]{1,0:T(8,128)(2,1)S(1)}, u32[]{:S(2)}, u32[]{:S(2)}) collective-permute-start(bf16[2112,128]{1,0:T(8,128)(2,1)S(1)} %pad_maximum_fusion.refs_0_), channel_id=1, source_target_pairs={{0,1},{1,2},{2,3},{3,0},{4,5},{5,6},{6,7},{7,4},{8,9},{9,10},{10,1... | collective-permute-start | bytes 1622024 | tf_op jit(solution)/shard_map/ppermute | solution.py:52
  29.2 25.3 %collective-permute-start.18 = (bf16[2112,128]{1,0:T(8,128)(2,1)S(1)}, bf16[2112,128]{1,0:T(8,128)(2,1)}, u32[]{:S(2)}, u32[]{:S(2)}) collective-permute-start(bf16[2112,128]{1,0:T(8,128)(2,1)S(1)} %pad_maximum_fusion.refs_0_), channel_id=1, source_target_pairs={{0,16},{1,17},{2,18},{3,19},{4,20},{5,21},{6,22},{7,23},{8,24},{9,... | collective-permute-start | bytes 1622024 | tf_op jit(solution)/shard_map/ppermute | solution.py:52
  49.7 10.9 %collective-permute-start.6 = (bf16[2112,128]{1,0:T(8,128)(2,1)S(1)}, bf16[2112,128]{1,0:T(8,128)(2,1)S(1)}, u32[]{:S(2)}, u32[]{:S(2)}) collective-permute-start(bf16[2112,128]{1,0:T(8,128)(2,1)S(1)} %collective-permute-done.5.refs_1_), channel_id=1, source_target_pairs={{0,4},{1,5},{2,6},{3,7},{4,8},{5,9},{6,10},{7,11},{8,12},{9,13},{1... | collective-permute-start | bytes 1622024 | tf_op jit(solution)/shard_map/ppermute | solution.py:52
  50.9 15.5 %collective-permute-start.9 = (bf16[2112,128]{1,0:T(8,128)(2,1)S(1)}, bf16[2112,128]{1,0:T(8,128)(2,1)S(1)}, u32[]{:S(2)}, u32[]{:S(2)}) collective-permute-start(bf16[2112,128]{1,0:T(8,128)(2,1)S(1)} %collective-permute-done.8.refs_4_), channel_id=1, source_target_pairs={{0,4},{1,5},{2,6},{3,7},{4,8},{5,9},{6,10},{7,11},{8,12},{9,13},{1... | collective-permute-start | bytes 1622024 | tf_op jit(solution)/shard_map/ppermute | solution.py:52
  52.1 15.8 %collective-permute-start.10 = (bf16[2112,128]{1,0:T(8,128)(2,1)S(1)}, bf16[2112,128]{1,0:T(8,128)(2,1)S(1)}, u32[]{:S(2)}, u32[]{:S(2)}) collective-permute-start(bf16[2112,128]{1,0:T(8,128)(2,1)S(1)} %collective-permute-done.8.refs_4_), channel_id=1, source_target_pairs={{0,12},{1,13},{2,14},{3,15},{4,0},{5,1},{6,2},{7,3},{8,4},{9,5},{1... | collective-permute-start | bytes 1622024 | tf_op jit(solution)/shard_map/ppermute | solution.py:52
  53.7 19.4 %collective-permute-start.12 = (bf16[2112,128]{1,0:T(8,128)(2,1)S(1)}, bf16[2112,128]{1,0:T(8,128)(2,1)S(1)}, u32[]{:S(2)}, u32[]{:S(2)}) collective-permute-start(bf16[2112,128]{1,0:T(8,128)(2,1)S(1)} %collective-permute-done.3.refs_8_), channel_id=1, source_target_pairs={{0,4},{1,5},{2,6},{3,7},{4,8},{5,9},{6,10},{7,11},{8,12},{9,13},{1... | collective-permute-start | bytes 1622024 | tf_op jit(solution)/shard_map/ppermute | solution.py:52
  54.4 22.5 %collective-permute-start.13 = (bf16[2112,128]{1,0:T(8,128)(2,1)S(1)}, bf16[2112,128]{1,0:T(8,128)(2,1)S(1)}, u32[]{:S(2)}, u32[]{:S(2)}) collective-permute-start(bf16[2112,128]{1,0:T(8,128)(2,1)S(1)} %collective-permute-done.3.refs_8_), channel_id=1, source_target_pairs={{0,12},{1,13},{2,14},{3,15},{4,0},{5,1},{6,2},{7,3},{8,4},{9,5},{1... | collective-permute-start | bytes 1622024 | tf_op jit(solution)/shard_map/ppermute | solution.py:52
  60.6 17.4 %collective-permute-start.15 = (bf16[2112,128]{1,0:T(8,128)(2,1)S(1)}, bf16[2112,128]{1,0:T(8,128)(2,1)S(1)}, u32[]{:S(2)}, u32[]{:S(2)}) collective-permute-start(bf16[2112,128]{1,0:T(8,128)(2,1)S(1)} %collective-permute-done.4.refs_12_), channel_id=1, source_target_pairs={{0,4},{1,5},{2,6},{3,7},{4,8},{5,9},{6,10},{7,11},{8,12},{9,13},{1... | collective-permute-start | bytes 1622024 | tf_op jit(solution)/shard_map/ppermute | solution.py:52
  66.4 16.3 %collective-permute-start.17 = (bf16[2112,128]{1,0:T(8,128)(2,1)S(1)}, bf16[2112,128]{1,0:T(8,128)(2,1)S(1)}, u32[]{:S(2)}, u32[]{:S(2)}) collective-permute-start(bf16[2112,128]{1,0:T(8,128)(2,1)S(1)} %collective-permute-done.4.refs_12_), channel_id=1, source_target_pairs={{0,12},{1,13},{2,14},{3,15},{4,0},{5,1},{6,2},{7,3},{8,4},{9,5},{1... | collective-permute-start | bytes 1622024 | tf_op jit(solution)/shard_map/ppermute | solution.py:52
  67.8 14.9 %collective-permute-start.19 = (bf16[2112,128]{1,0:T(8,128)(2,1)S(1)}, bf16[2112,128]{1,0:T(8,128)(2,1)S(1)}, u32[]{:S(2)}, u32[]{:S(2)}) collective-permute-start(bf16[2112,128]{1,0:T(8,128)(2,1)S(1)} %collective-permute-done.5.refs_1_), channel_id=1, source_target_pairs={{0,16},{1,17},{2,18},{3,19},{4,20},{5,21},{6,22},{7,23},{8,24},{9,... | collective-permute-start | bytes 1622024 | tf_op jit(solution)/shard_map/ppermute | solution.py:52
  73.1 13.0 %collective-permute-start.21 = (bf16[2112,128]{1,0:T(8,128)(2,1)S(1)}, bf16[2112,128]{1,0:T(8,128)(2,1)S(1)}, u32[]{:S(2)}, u32[]{:S(2)}) collective-permute-start(bf16[2112,128]{1,0:T(8,128)(2,1)S(1)} %collective-permute-done.7.refs_3_), channel_id=1, source_target_pairs={{0,16},{1,17},{2,18},{3,19},{4,20},{5,21},{6,22},{7,23},{8,24},{9,... | collective-permute-start | bytes 1622024 | tf_op jit(solution)/shard_map/ppermute | solution.py:52
  76.9 9.4 %collective-permute-start.22 = (bf16[2112,128]{1,0:T(8,128)(2,1)S(1)}, bf16[2112,128]{1,0:T(8,128)(2,1)S(1)}, u32[]{:S(2)}, u32[]{:S(2)}) collective-permute-start(bf16[2112,128]{1,0:T(8,128)(2,1)S(1)} %collective-permute-done.8.refs_4_), channel_id=1, source_target_pairs={{0,16},{1,17},{2,18},{3,19},{4,20},{5,21},{6,22},{7,23},{8,24},{9,... | collective-permute-start | bytes 1622024 | tf_op jit(solution)/shard_map/ppermute | solution.py:52
  78.0 9.7 %collective-permute-start.26 = (bf16[2112,128]{1,0:T(8,128)(2,1)S(1)}, bf16[2112,128]{1,0:T(8,128)(2,1)S(1)}, u32[]{:S(2)}, u32[]{:S(2)}) collective-permute-start(bf16[2112,128]{1,0:T(8,128)(2,1)S(1)} %collective-permute-done.3.refs_8_), channel_id=1, source_target_pairs={{0,16},{1,17},{2,18},{3,19},{4,20},{5,21},{6,22},{7,23},{8,24},{9,... | collective-permute-start | bytes 1622024 | tf_op jit(solution)/shard_map/ppermute | solution.py:52
  82.7 5.4 %collective-permute-start.30 = (bf16[2112,128]{1,0:T(8,128)(2,1)S(1)}, bf16[2112,128]{1,0:T(8,128)(2,1)S(1)}, u32[]{:S(2)}, u32[]{:S(2)}) collective-permute-start(bf16[2112,128]{1,0:T(8,128)(2,1)S(1)} %collective-permute-done.4.refs_12_), channel_id=1, source_target_pairs={{0,16},{1,17},{2,18},{3,19},{4,20},{5,21},{6,22},{7,23},{8,24},{9,... | collective-permute-start | bytes 1622024 | tf_op jit(solution)/shard_map/ppermute | solution.py:52
  82.7 9.8 %collective-permute-start.11 = (bf16[2112,128]{1,0:T(8,128)(2,1)S(1)}, bf16[2112,128]{1,0:T(8,128)(2,1)S(1)}, u32[]{:S(2)}, u32[]{:S(2)}) collective-permute-start(bf16[2112,128]{1,0:T(8,128)(2,1)S(1)} %collective-permute-done.10.refs_7_), channel_id=1, source_target_pairs={{0,12},{1,13},{2,14},{3,15},{4,0},{5,1},{6,2},{7,3},{8,4},{9,5},{1... | collective-permute-start | bytes 1622024 | tf_op jit(solution)/shard_map/ppermute | solution.py:52
  86.2 12.1 %collective-permute-start.14 = (bf16[2112,128]{1,0:T(8,128)(2,1)S(1)}, bf16[2112,128]{1,0:T(8,128)(2,1)S(1)}, u32[]{:S(2)}, u32[]{:S(2)}) collective-permute-start(bf16[2112,128]{1,0:T(8,128)(2,1)S(1)} %collective-permute-done.13.refs_11_), channel_id=1, source_target_pairs={{0,12},{1,13},{2,14},{3,15},{4,0},{5,1},{6,2},{7,3},{8,4},{9,5},{1... | collective-permute-start | bytes 1622024 | tf_op jit(solution)/shard_map/ppermute | solution.py:52
  86.3 12.5 %collective-permute-start.16 = (bf16[2112,128]{1,0:T(8,128)(2,1)S(1)}, bf16[2112,128]{1,0:T(8,128)(2,1)S(1)}, u32[]{:S(2)}, u32[]{:S(2)}) collective-permute-start(bf16[2112,128]{1,0:T(8,128)(2,1)S(1)} %collective-permute-done.15.refs_13_), channel_id=1, source_target_pairs={{0,4},{1,5},{2,6},{3,7},{4,8},{5,9},{6,10},{7,11},{8,12},{9,13},{1... | collective-permute-start | bytes 1622024 | tf_op jit(solution)/shard_map/ppermute | solution.py:52
  87.6 11.1 %collective-permute-start.20 = (bf16[2112,128]{1,0:T(8,128)(2,1)S(1)}, bf16[2112,128]{1,0:T(8,128)(2,1)S(1)}, u32[]{:S(2)}, u32[]{:S(2)}) collective-permute-start(bf16[2112,128]{1,0:T(8,128)(2,1)S(1)} %collective-permute-done.6.refs_2_), channel_id=1, source_target_pairs={{0,16},{1,17},{2,18},{3,19},{4,20},{5,21},{6,22},{7,23},{8,24},{9,... | collective-permute-start | bytes 1622024 | tf_op jit(solution)/shard_map/ppermute | solution.py:52
  88.1 11.1 %collective-permute-start.23 = (bf16[2112,128]{1,0:T(8,128)(2,1)S(1)}, bf16[2112,128]{1,0:T(8,128)(2,1)S(1)}, u32[]{:S(2)}, u32[]{:S(2)}) collective-permute-start(bf16[2112,128]{1,0:T(8,128)(2,1)S(1)} %collective-permute-done.9.refs_5_), channel_id=1, source_target_pairs={{0,16},{1,17},{2,18},{3,19},{4,20},{5,21},{6,22},{7,23},{8,24},{9,... | collective-permute-start | bytes 1622024 | tf_op jit(solution)/shard_map/ppermute | solution.py:52
  92.5 7.1 %collective-permute-start.25 = (bf16[2112,128]{1,0:T(8,128)(2,1)S(1)}, bf16[2112,128]{1,0:T(8,128)(2,1)S(1)}, u32[]{:S(2)}, u32[]{:S(2)}) collective-permute-start(bf16[2112,128]{1,0:T(8,128)(2,1)S(1)} %collective-permute-done.10.refs_7_), channel_id=1, source_target_pairs={{0,16},{1,17},{2,18},{3,19},{4,20},{5,21},{6,22},{7,23},{8,24},{9,... | collective-permute-start | bytes 1622024 | tf_op jit(solution)/shard_map/ppermute | solution.py:52
  114.0 32.4 %collective-permute-start.34 = (bf16[2048,128]{1,0:T(8,128)(2,1)S(1)}, bf16[2048,128]{1,0:T(8,128)(2,1)S(1)}, u32[]{:S(2)}, u32[]{:S(2)}) collective-permute-start(bf16[2048,128]{1,0:T(8,128)(2,1)S(1)} %get-tuple-element.47), channel_id=1, source_target_pairs={{0,64},{1,65},{2,66},{3,67},{4,68},{5,69},{6,70},{7,71},{8,72},{9,... | collective-permute-start | bytes 1572872 | tf_op jit(solution)/shard_map/ppermute | solution.py:52
  115.9 45.5 %collective-permute-start.35 = (bf16[2048,128]{1,0:T(8,128)(2,1)S(1)}, bf16[2048,128]{1,0:T(8,128)(2,1)S(1)}, u32[]{:S(2)}, u32[]{:S(2)}) collective-permute-start(bf16[2048,128]{1,0:T(8,128)(2,1)S(1)} %get-tuple-element.48), channel_id=1, source_target_pairs={{0,32},{1,33},{2,34},{3,35},{4,36},{5,37},{6,38},{7,39},{8,40},{9,... | collective-permute-start | bytes 1572872 | tf_op jit(solution)/shard_map/ppermute | solution.py:52
  115.9 45.5 %collective-permute-start.36 = (bf16[2048,128]{1,0:T(8,128)(2,1)S(1)}, bf16[2048,128]{1,0:T(8,128)(2,1)S(1)}, u32[]{:S(2)}, u32[]{:S(2)}) collective-permute-start(bf16[2048,128]{1,0:T(8,128)(2,1)S(1)} %get-tuple-element.49), channel_id=1, source_target_pairs={{0,96},{1,97},{2,98},{3,99},{4,100},{5,101},{6,102},{7,103},{8,104... | collective-permute-start | bytes 1572872 | tf_op jit(solution)/shard_map/ppermute | solution.py:52
  145.1 22.6 %collective-permute-start.37 = (bf16[2048,128]{1,0:T(8,128)(2,1)S(1)}, bf16[2048,128]{1,0:T(8,128)(2,1)S(1)}, u32[]{:S(2)}, u32[]{:S(2)}) collective-permute-start(bf16[2048,128]{1,0:T(8,128)(2,1)S(1)} %get-tuple-element.58), channel_id=1, source_target_pairs={{0,64},{1,65},{2,66},{3,67},{4,68},{5,69},{6,70},{7,71},{8,72},{9,... | collective-permute-start | bytes 1572872 | tf_op jit(solution)/shard_map/ppermute | solution.py:52
  145.3 26.1 %collective-permute-start.38 = (bf16[2048,128]{1,0:T(8,128)(2,1)S(1)}, bf16[2048,128]{1,0:T(8,128)(2,1)S(1)}, u32[]{:S(2)}, u32[]{:S(2)}) collective-permute-start(bf16[2048,128]{1,0:T(8,128)(2,1)S(1)} %get-tuple-element.59), channel_id=1, source_target_pairs={{0,32},{1,33},{2,34},{3,35},{4,36},{5,37},{6,38},{7,39},{8,40},{9,... | collective-permute-start | bytes 1572872 | tf_op jit(solution)/shard_map/ppermute | solution.py:52
  146.4 25.1 %collective-permute-start.39 = (bf16[2048,128]{1,0:T(8,128)(2,1)S(1)}, bf16[2048,128]{1,0:T(8,128)(2,1)S(1)}, u32[]{:S(2)}, u32[]{:S(2)}) collective-permute-start(bf16[2048,128]{1,0:T(8,128)(2,1)S(1)} %get-tuple-element.60), channel_id=1, source_target_pairs={{0,96},{1,97},{2,98},{3,99},{4,100},{5,101},{6,102},{7,103},{8,104... | collective-permute-start | bytes 1572872 | tf_op jit(solution)/shard_map/ppermute | solution.py:52
  (27 other events, 343.5 us)

commit v3 on v2

--- a/solution.py
+++ b/solution.py
@@ -2,6 +2,7 @@
 
 import jax
 import jax.numpy as jnp
+import numpy as np
 from jax import lax
 from jax.experimental import pallas as pl
 from jax.experimental.pallas import tpu as pltpu
@@ -56,19 +57,22 @@
     near = {0: block}
     for s in (1, 3, 2):
         near[s] = send(block, first(s))
-    made = prepare(near[3])
-    near[2], made = lax.optimization_barrier((near[2], made))
-    held = {}
-    for s in (0, 1, 3, 2):
+    held = {(0, 0): block}
+    twins = {(0, 0): send(block, SIBLING)}
+    held[0, 1], held[0, 3] = send(block, second(1)), send(block, second(3))
+    made = prepare(twins[0, 0])
+    near[1], made = lax.optimization_barrier((near[1], made))
+    for s in (1, 3, 2):
         held[s, 0] = near[s]
         held[s, 1] = send(near[s], second(1))
         held[s, 3] = send(near[s], second(3))
-        if s in (0, 3):
-            held[s, 2] = send(held[s, 1], second(1))
-        else:
-            held[s, 2] = send(held[s, 3], second(3))
-    mine = [held[s, t] for s in range(4) for t in range(4)]
-    return made, mine + [send(b, SIBLING) for b in mine]
+    for s, t in ((0, 1), (1, 3), (3, 1), (2, 3)):
+        held[s, 2] = send(held[s, t], second(t))
+    for key, value in held.items():
+        if key not in twins:
+            twins[key] = send(value, SIBLING)
+    spots = [(s, t) for s in range(4) for t in range(4)]
+    return made, [held[k] for k in spots] + [twins[k] for k in spots]
 
 
 def own_meta(ladder, decay):
@@ -94,21 +98,6 @@
     return jnp.where(dy == 0, slot, -1)
 
 
-def compact(slot, values):
-    count = slot.shape[-1]
-    keep = (slot >= 0) & (values[0] != 0)
-    before = jnp.arange(count)[:, None] < jnp.arange(count)[None, :]
-    at = jnp.sum((keep[..., :, None] & before).astype(jnp.int32), axis=-2)
-    moved = keep[..., :, None] & (at[..., :, None] == jnp.arange(count))
-    lists = [jnp.sum(jnp.where(moved, v[..., :, None], 0), axis=-2).reshape(-1) for v in [slot, *values]]
-    return [jnp.sum(keep.astype(jnp.int32), axis=-1).reshape(-1), *lists]
-
-
-def pick(rows, table):
-    hot = (rows.reshape(-1)[:, None] == jnp.arange(table.shape[0])[None, :]).astype(BF)
-    return jnp.dot(hot, table.astype(BF), preferred_element_type=F32)
-
-
 def own_links(higher, lower, at):
     y, c, z, x = at
     rows = []
@@ -119,24 +108,22 @@
     return jnp.concatenate(rows)
 
 
-def near_lists(partner, weights, at):
-    return compact(slot_of(partner, at).reshape(32, 2, 4), [weights.reshape(32, 2, 4)])
-
-
-def spread(v):
-    return v.reshape(32, 2, 4, 2, 4).transpose(0, 1, 3, 2, 4).reshape(32, 64)
-
-
-def far_tables(partner, higher, lower, strengths, at):
+def tables_of(higher, lower, at):
+    partner = own_links(higher, lower, at)
     dy, slot = place(partner, at)
-    near = jnp.where(dy == 0, slot, -1).astype(F32)
-    table = jnp.concatenate([slot_of(higher, at), slot_of(lower, at)], axis=1).astype(F32)
-    far = spread(pick(partner, table))
-    slots = jnp.concatenate([far, near, jnp.full((32, 56), -1, F32)], axis=1)
-    up, down = strengths[0, :4], strengths[0, 4:]
-    products = [(a[:, None] * b[None, :]).reshape(16) for a in (up, down) for b in (up, down)]
-    scale = jnp.concatenate([*products, up, down, jnp.zeros((56,), F32)]).reshape(1, DIM)
-    return (slot >> 3) * EXTRA + dy * 16 + (slot & 7), slots, scale
+    table = jnp.concatenate([slot_of(higher, at), slot_of(lower, at)], axis=1).astype(BF)
+    rows = (slot >> 3) * EXTRA + dy * 16 + (slot & 7)
+    return partner, rows, jnp.where(dy == 0, slot, -1), table
+
+
+def link_scale(rates):
+    lane = np.arange(DIM)
+    kind, near, far = lane >> 4, lane - 64, lane < 64
+    outer = np.where(far, (kind >> 1) * 4 + ((lane >> 2) & 3), near)
+    inner = np.where(far, (kind & 1) * 4 + (lane & 3), -1)
+    eight = rates.reshape(1, 8)
+    take = lambda n: jnp.sum(jnp.where(n[:, None] == np.arange(8)[None, :], eight, 0.0), axis=1)
+    return (take(outer) * jnp.where(far, take(inner), 1.0)).reshape(1, DIM)
 
 
 def copies_of(blocks, held, sems, start, rows):
@@ -146,16 +133,6 @@
     ]
 
 
-def link_sum(held, slots, weights, base, count):
-    def add(k, total):
-        for n in (base + 2 * k, base + 2 * k + 1):
-            start = pl.multiple_of(slots[n] * ROWS, ROWS)
-            total = total + weights[n] * held[pl.ds(start, ROWS), :].astype(F32)
-        return total
-
-    return lax.fori_loop(0, (count + 1) >> 1, add, jnp.zeros((ROWS, DIM), F32))
-
-
 def mm(a, b):
     return jnp.dot(a, b, preferred_element_type=F32)
 
@@ -164,15 +141,22 @@
     return jnp.concatenate([plus[DIM:], -plus[:DIM]], axis=1)
 
 
-def near_sums(order, held, count, slots, weights, c_ref, outs, lefts, rights):
+def near_sums(order, held, slots, weights, c_ref, outs, acc, lefts, rights):
     for dy, out in zip(order, outs):
 
         def links(i, _):
-            d = (dy * OWN + i) * 2
-            up = link_sum(held, slots, weights, d * 4, count[d])
-            down = link_sum(held, slots, weights, d * 4 + 4, count[d + 1])
-            lefts[i] = crossed((up + down).astype(BF))
-            rights[i] = (up - down).astype(BF)
+            d = dy * OWN + i
+            acc[...] = jnp.zeros((2, ROWS, DIM), F32)
+            for k in range(2 * MODES):
+                slot = slots[d, k]
+
+                @pl.when(slot >= 0)
+                def _():
+                    start = pl.multiple_of(slot * ROWS, ROWS)
+                    acc[k // 4] = acc[k // 4] + weights[d, k] * held[pl.ds(start, ROWS), :].astype(F32)
+
+            lefts[i] = crossed((acc[0] + acc[1]).astype(BF))
+            rights[i] = (acc[0] - acc[1]).astype(BF)
             return 0
 
         lax.fori_loop(0, OWN, links, 0)
@@ -183,23 +167,25 @@
             out[pl.ds(i * ROWS + DIM, DIM), :] = (left[:, DIM:] + right[:DIM]).astype(out.dtype)
 
 
-def near_kernel(order, count, slots, weights, c_ref, *refs):
+def near_kernel(order, slots, weights, c_ref, *refs):
     blocks, outs = refs[:32], refs[32 : 32 + len(order)]
-    held, sems, lefts, rights = refs[32 + len(order) :]
+    held, sems, acc, lefts, rights = refs[32 + len(order) :]
     copies = copies_of(blocks, held, sems, 0, BLOCK)
     for copy in copies:
         copy.start()
     for copy in copies:
         copy.wait()
-    near_sums(order, held, count, slots, weights, c_ref, outs, lefts, rights)
-
-
-def make_lists(row_ref, ladder_ref, scale_ref, slot_ref, table, code_v, weight_v):
+    near_sums(order, held, slots, weights, c_ref, outs, acc, lefts, rights)
+
+
+def make_lists(partner_ref, row_ref, ladder_ref, scale_ref, slot_ref, links, table, code_v, weight_v):
     lane = lax.broadcasted_iota(jnp.int32, (32, DIM), 1)
     row = lax.broadcasted_iota(jnp.int32, (DIM, DIM), 0)
     col = lax.broadcasted_iota(jnp.int32, (DIM, DIM), 1)
     wide = lax.broadcasted_iota(jnp.int32, (32, 32 * EXTRA), 1)
+    index = lax.broadcasted_iota(jnp.int32, (32, links.shape[0]), 1)
     total = jnp.zeros((32, DIM), F32)
+    slot = jnp.zeros((32, DIM), F32)
     for k in range(2 * MODES):
         hot = jnp.where(row_ref[:, k : k + 1] == wide, 1.0, 0.0).astype(BF)
         wanted = mm(hot, table[...])
@@ -207,10 +193,12 @@
         target = ((k // 4) * 2 + (row >> 2)) * 16 + (k % 4) * 4 + (row & 3)
         shift = jnp.where((row < 2 * MODES) & (col == target), 1.0, 0.0).astype(BF)
         total = total + mm((wanted * mine).astype(BF), shift)
+        found = jnp.where(partner_ref[:, k : k + 1] == index, 1.0, 0.0).astype(BF)
+        slot = slot + mm(mm(found, links[...]).astype(BF), shift[: 2 * MODES])
+        slot = jnp.where(lane == 64 + k, slot_ref[:, k : k + 1].astype(F32), slot)
         decay = wanted[:, 8:9] + wanted[:, 9:10] + wanted[:, 10:11]
         total = jnp.where(lane == 64 + k, decay * mine, total)
-    slot = slot_ref[...]
-    keep = (slot >= 0) & (total != 0)
+    keep = (lane < 72) & (slot >= 0) & (total != 0)
     kept = jnp.where(keep, 1.0, 0.0)
     spot = mm(kept.astype(BF), jnp.where(row < col, 1.0, 0.0).astype(BF)).astype(jnp.int32)
     spot = jnp.where(keep, spot, -1)
@@ -226,7 +214,7 @@
     weight_v[...] = weights
 
 
-def far_kernel(order, c_ref, right_ref, left_ref, row_ref, ladder_ref, scale_ref, slot_ref, *refs):
+def far_kernel(order, c_ref, right_ref, left_ref, partner_ref, row_ref, ladder_ref, scale_ref, slot_ref, links, *refs):
     blocks, outs = refs[:32], refs[32 : 32 + len(order)]
     held, extra, main_sems, extra_sems, *rest = refs[32 + len(order) :]
     acc, lefts, rights, kept, double, code_v, weight_v, code_s, weight_s, sems = rest
@@ -236,7 +224,7 @@
         copy.start()
     for copy in tails:
         copy.wait()
-    make_lists(row_ref, ladder_ref, scale_ref, slot_ref, extra, code_v, weight_v)
+    make_lists(partner_ref, row_ref, ladder_ref, scale_ref, slot_ref, links, extra, code_v, weight_v)
     codes = pltpu.make_async_copy(code_v, code_s, sems.at[0])
     weights = pltpu.make_async_copy(weight_v, weight_s, sems.at[1])
     codes.start()
@@ -317,14 +305,14 @@
 
 
 def near_scratch():
-    return [pltpu.VMEM((OWN, DIM, ROWS), BF), pltpu.VMEM((OWN, ROWS, DIM), BF)]
+    return [pltpu.VMEM((2, ROWS, DIM), F32), pltpu.VMEM((OWN, DIM, ROWS), BF), pltpu.VMEM((OWN, ROWS, DIM), BF)]
 
 
 def near_parts(order, lists, coupling, blocks):
     return pl.pallas_call(
         functools.partial(near_kernel, order),
         out_shape=part_shapes(order),
-        in_specs=[SM] * 3 + [VM] + [FAR] * 32,
+        in_specs=[SM] * 2 + [VM] + [FAR] * 32,
         out_specs=[VM] * len(order),
         scratch_shapes=[pltpu.VMEM((32 * BLOCK, DIM), BF), pltpu.SemaphoreType.DMA((32,))] + near_scratch(),
         compiler_params=pltpu.CompilerParams(vmem_limit_bytes=26 << 20),
@@ -425,7 +413,11 @@
     out[DIM:ROWS, DIM:ROWS] = re
 
 
-def sides_kernel(prop_ref, whole_right, whole_left, right_ref, left_ref):
+def sides_kernel(prop_ref, *refs):
+    small = (len(refs) - 4) // 2
+    for given, out in zip(refs[:small], refs[small + 4 :]):
+        out[...] = given[...]
+    whole_right, whole_left, right_ref, left_ref = refs[small : small + 4]
     for n in range(8):
         re, im = prop_ref[n, 0], prop_ref[n, 1]
         fill_right(right_ref.at[n], re, im)
@@ -440,14 +432,15 @@
     fill_right(whole_left, hi(re.T), hi(im.T))
 
 
-def sides(props):
+def sides(props, small):
     return pl.pallas_call(
         sides_kernel,
-        out_shape=[jax.ShapeDtypeStruct((ROWS, ROWS), BF)] * 2 + [jax.ShapeDtypeStruct((8, ROWS, ROWS), BF)] * 2,
-        in_specs=[VM],
-        out_specs=[VM] * 4,
+        out_shape=[jax.ShapeDtypeStruct((ROWS, ROWS), BF)] * 2 + [jax.ShapeDtypeStruct((8, ROWS, ROWS), BF)] * 2
+        + [jax.ShapeDtypeStruct(v.shape, v.dtype) for v in small],
+        in_specs=[VM] * (1 + len(small)),
+        out_specs=[VM] * (4 + len(small)),
         compiler_params=pltpu.CompilerParams(vmem_limit_bytes=8 << 20),
-    )(props)
+    )(props, *small)
 
 
 def body(adjoint, saved, propagators, coupling, higher, lower, ladder, rates, decay):
@@ -457,20 +450,19 @@
     by_y = [meta] + [send(meta, along_y(s)) for s in (1, 2, 3)]
     ladders = jnp.concatenate([by_y[(4 - dy) % 4][:, :8] for dy in range(4)])
     tail = jnp.pad(jnp.stack(by_y).astype(BF), ((0, 0), (0, 16 - OWN), (0, DIM - 16))).reshape(EXTRA, DIM)
-    strengths = rates.reshape(1, 8)
+    weights = ladders * rates.reshape(1, 8)
+    scale = link_scale(rates)
 
     def prepare(arrived):
-        tied = (propagators, higher, lower, ladders, strengths, arrived)
-        props, up, down, wanted, factors, _ = lax.optimization_barrier(tied)
-        partner = own_links(up, down, at)
-        near = near_lists(partner, wanted * factors, at)
-        return near, far_tables(partner, up, down, factors, at), sides(props.reshape(8, 2, DIM, DIM))
+        tied = (propagators, higher, lower, weights, ladders, scale, arrived)
+        props, up, down, *rest, _ = lax.optimization_barrier(tied)
+        return sides(props.reshape(8, 2, DIM, DIM), [*rest, *tables_of(up, down, at)])
 
     made, blocks = gather_layer(jnp.concatenate([lam, tail]), prepare)
-    one_list, (rows, slots, scale), (whole_right, whole_left, right, left) = made
-    one_2, one_1, one_3, one_0 = near_parts((2, 1, 3, 0), one_list, coupling, blocks)
+    whole_right, whole_left, right, left, weights, ladders, scale, partner, rows, slots, table = made
+    one_2, one_1, one_3, one_0 = near_parts((2, 1, 3, 0), [slots, weights], coupling, blocks)
     got_one = [one_0] + [send(p, along_y(s)) for p, s in ((one_2, 2), (one_1, 1), (one_3, 3))]
-    arrays = [coupling, whole_right, whole_left, rows, ladders, scale, slots]
+    arrays = [coupling, whole_right, whole_left, partner, rows, ladders, scale, slots, table]
     two_2, two_1, two_3 = far_parts((2, 1, 3), arrays, blocks)
     got_two = [send(p, along_y(s)) for p, s in ((two_2, 2), (two_1, 1), (two_3, 3))]
     [two_0] = far_parts((0,), arrays, blocks)

time: 203 us -> 182 us (0.90)
  local copies, waits for them, and re-layouts: 19.9 us -> 6.01 us
  waiting for transfers between devices: 41.8 us -> 37 us
  starting transfers between devices: 49.8 us -> 45.1 us
  Pallas kernels: 60.4 us -> 64.3 us
    ppermute x40, waiting for transfers between devices: 41.8 us -> 37 us  [send(): return lax.ppermute(a, AXES, route)]
    reshape x6 -> x0, local copies, waits for them, and re-layouts: 4.72 us -> none  [the longest x2 2.54 us: spread(): return v.reshape(32, 2, 4, 2, 4).transpose(0, 1, 3, 2, 4).reshape(32, 64)]
    ppermute x40, starting transfers between devices: 49.8 us -> 45.1 us  [send(): return lax.ppermute(a, AXES, route)]
    mul x6 -> x1, local copies, waits for them, and re-layouts: 5.3 us -> 0.76 us  [body(): weights = ladders * rates.reshape(1, 8)]
    pallas_call x2, Pallas kernels: 39.5 us -> 41.7 us  [far_parts(): pl.pallas_call(functools.partial(far_kernel, order), out_shape=part_shape...]
    unnamed x38 -> x26, local copies, waits for them, and re-layouts: 5.1 us -> 3.17 us
  transfers between devices with their start and end apart: 40 -> 40, of which waited for: 16 -> 18; matrix products, arithmetic and copies ran while one was open for 9% -> 2% of each run, Pallas kernels for 23% -> 27%
where the time goes in v3:
time: 182 us; the launch traced here: 181 us
  Pallas kernels  64.3 us (35%)
  starting transfers between devices  45.1 us (25%)
  waiting for transfers between devices  37 us (20%)
  blocking collectives  22.4 us (12%)
  local copies, waits for them, and re-layouts  6.01 us (3%)
  other arithmetic  5.76 us (3%)
    ppermute x40, starting transfers between devices, send(): return lax.ppermute(a, AXES, route)  45.1 us
    pallas_call x2, Pallas kernels, far_parts(): pl.pallas_call(functools.partial(far_kernel, order), out_shape=part_shape...  41.7 us
    ppermute x40, waiting for transfers between devices, send(): return lax.ppermute(a, AXES, route)  37 us
    all_to_all x1, blocking collectives, body(): grad = lax.all_to_all(grad, AXES, 0, 0, tiled=True)  22.4 us
    pallas_call x2, Pallas kernels, chain(): pl.pallas_call(functools.partial(chain_kernel, step), out_shape=[jax.Shap...  13.2 us
    pallas_call x1, Pallas kernels, near_parts(): pl.pallas_call(functools.partial(near_kernel, order), out_shape=part_shap...  8.57 us
  transfers between devices with their start and end apart: 40, of which 18 were waited for; matrix products, arithmetic and copies ran while one was open for 2% of the time, Pallas kernels for 27%

profile of v3, /device:TPU:1, one launch (start us, length us, event | category | flops | bytes accessed | tf_op | source)
XLA Modules:
  0.0 181.4 jit_solution(227000763421923123)
XLA Ops:
  2.6 3.6 %collective-permute-start.2 = (f32[8,16]{1,0:T(8,128)S(1)}, f32[8,16]{1,0:T(8,128)S(1)}, u32[]{:S(2)}, u32[]{:S(2)}) collective-permute-start(f32[8,16]{1,0:T(8,128)S(1)} %pad.8), channel_id=1, source_target_pairs={{0,96},{1,97},{2,98},{3,99},{4,100},{5,101},{6,102},{7,103},{8,104... | collective-permute-start | bytes 1544 | tf_op jit(solution)/shard_map/ppermute | solution.py:53
  8.0 2.1 %collective-permute-done.1 = f32[8,16]{1,0:T(8,128)S(1)} collective-permute-done((f32[8,16]{1,0:T(8,128)S(1)}, f32[8,16]{1,0:T(8,128)S(1)}, u32[]{:S(2)}, u32[]{:S(2)}) %collective-permute-start.1) | collective-permute-done | bytes 544 | tf_op jit(solution)/shard_map/ppermute | solution.py:53
  11.3 2.5 %collective-permute-start.4 = (bf16[2112,128]{1,0:T(8,128)(2,1)S(1)}, bf16[2112,128]{1,0:T(8,128)(2,1)S(1)}, u32[]{:S(2)}, u32[]{:S(2)}) collective-permute-start(bf16[2112,128]{1,0:T(8,128)(2,1)S(1)} %pad_maximum_fusion.refs_0_), channel_id=1, source_target_pairs={{0,16},{1,17},{2,18},{3,19},{4,20},{5,21},{6,22},{7,23},{8,24},{9,... | collective-permute-start | bytes 1622024 | tf_op jit(solution)/shard_map/ppermute | solution.py:53
  14.4 1.6 collective-permute-start.3
  16.0 1.2 collective-permute-start.5
  17.2 1.5 collective-permute-start.7
  18.7 3.3 %collective-permute-start.11 = (bf16[2112,128]{1,0:T(8,128)(2,1)S(1)}, bf16[2112,128]{1,0:T(8,128)(2,1)S(1)}, u32[]{:S(2)}, u32[]{:S(2)}) collective-permute-start(bf16[2112,128]{1,0:T(8,128)(2,1)S(1)} %pad_maximum_fusion.refs_0_), channel_id=1, source_target_pairs={{0,2},{1,3},{2,0},{3,1},{4,6},{5,7},{6,4},{7,5},{8,10},{9,11},{10,... | collective-permute-start | bytes 1622024 | tf_op jit(solution)/shard_map/ppermute | solution.py:53
  29.2 1.3 collective-permute-done.5.refs_1_
  31.6 1.1 collective-permute-start.8
  32.8 2.4 %collective-permute-start.9 = (bf16[2112,128]{1,0:T(8,128)(2,1)S(1)}, bf16[2112,128]{1,0:T(8,128)(2,1)S(1)}, u32[]{:S(2)}, u32[]{:S(2)}) collective-permute-start(bf16[2112,128]{1,0:T(8,128)(2,1)S(1)} %collective-permute-done.3.refs_4_), channel_id=1, source_target_pairs={{0,12},{1,13},{2,14},{3,15},{4,0},{5,1},{6,2},{7,3},{8,4},{9,5},{1... | collective-permute-start | bytes 1622024 | tf_op jit(solution)/shard_map/ppermute | solution.py:53
  35.1 2.8 %collective-permute-done.11.refs_8_ = bf16[2112,128]{1,0:T(8,128)(2,1)S(1)} collective-permute-done((bf16[2112,128]{1,0:T(8,128)(2,1)S(1)}, bf16[2112,128]{1,0:T(8,128)(2,1)S(1)}, u32[]{:S(2)}, u32[]{:S(2)}) %collective-permute-start.11) | collective-permute-done | bytes 540704 | tf_op jit(solution)/shard_map/ppermute | solution.py:53
  39.0 1.7 collective-permute-start.13
  40.6 2.3 %collective-permute-done.6.refs_2_ = bf16[2112,128]{1,0:T(8,128)(2,1)S(1)} collective-permute-done((bf16[2112,128]{1,0:T(8,128)(2,1)S(1)}, bf16[2112,128]{1,0:T(8,128)(2,1)S(1)}, u32[]{:S(2)}, u32[]{:S(2)}) %collective-permute-start.6) | collective-permute-done | bytes 540704 | tf_op jit(solution)/shard_map/ppermute | solution.py:53
  42.9 5.8 %collective-permute-done.8.refs_5_ = bf16[2112,128]{1,0:T(8,128)(2,1)S(1)} collective-permute-done((bf16[2112,128]{1,0:T(8,128)(2,1)S(1)}, bf16[2112,128]{1,0:T(8,128)(2,1)S(1)}, u32[]{:S(2)}, u32[]{:S(2)}) %collective-permute-start.8) | collective-permute-done | bytes 540704 | tf_op jit(solution)/shard_map/ppermute | solution.py:53
  49.0 3.4 %collective-permute-start.19 = (bf16[2112,128]{1,0:T(8,128)(2,1)S(1)}, bf16[2112,128]{1,0:T(8,128)(2,1)S(1)}, u32[]{:S(2)}, u32[]{:S(2)}) collective-permute-start(bf16[2112,128]{1,0:T(8,128)(2,1)S(1)} %collective-permute-done.5.refs_1_), channel_id=1, source_target_pairs={{0,16},{1,17},{2,18},{3,19},{4,20},{5,21},{6,22},{7,23},{8,24},{9,... | collective-permute-start | bytes 1622024 | tf_op jit(solution)/shard_map/ppermute | solution.py:53
  52.4 2.1 %collective-permute-done.12.refs_9_ = bf16[2112,128]{1,0:T(8,128)(2,1)S(1)} collective-permute-done((bf16[2112,128]{1,0:T(8,128)(2,1)S(1)}, bf16[2112,128]{1,0:T(8,128)(2,1)S(1)}, u32[]{:S(2)}, u32[]{:S(2)}) %collective-permute-start.12) | collective-permute-done | bytes 540704 | tf_op jit(solution)/shard_map/ppermute | solution.py:53
  54.5 1.2 collective-permute-start.21
  55.7 4.6 %collective-permute-done.16.refs_13_ = bf16[2112,128]{1,0:T(8,128)(2,1)S(1)} collective-permute-done((bf16[2112,128]{1,0:T(8,128)(2,1)}, bf16[2112,128]{1,0:T(8,128)(2,1)S(1)}, u32[]{:S(2)}, u32[]{:S(2)}) %collective-permute-start.16) | collective-permute-done | bytes 540704 | tf_op jit(solution)/shard_map/ppermute | solution.py:53
  60.3 1.2 collective-permute-start.26
  61.5 2.5 %collective-permute-start.10 = (bf16[2112,128]{1,0:T(8,128)(2,1)S(1)}, bf16[2112,128]{1,0:T(8,128)(2,1)S(1)}, u32[]{:S(2)}, u32[]{:S(2)}) collective-permute-start(bf16[2112,128]{1,0:T(8,128)(2,1)S(1)} %collective-permute-done.9.refs_7_), channel_id=1, source_target_pairs={{0,12},{1,13},{2,14},{3,15},{4,0},{5,1},{6,2},{7,3},{8,4},{9,5},{1... | collective-permute-start | bytes 1622024 | tf_op jit(solution)/shard_map/ppermute | solution.py:53
  66.7 3.6 %collective-permute-done.10.refs_6_ = bf16[2112,128]{1,0:T(8,128)(2,1)S(1)} collective-permute-done((bf16[2112,128]{1,0:T(8,128)(2,1)S(1)}, bf16[2112,128]{1,0:T(8,128)(2,1)S(1)}, u32[]{:S(2)}, u32[]{:S(2)}) %collective-permute-start.10) | collective-permute-done | bytes 540704 | tf_op jit(solution)/shard_map/ppermute | solution.py:53
  71.4 4.8 %collective-permute-done.14.refs_10_ = bf16[2112,128]{1,0:T(8,128)(2,1)S(1)} collective-permute-done((bf16[2112,128]{1,0:T(8,128)(2,1)S(1)}, bf16[2112,128]{1,0:T(8,128)(2,1)S(1)}, u32[]{:S(2)}, u32[]{:S(2)}) %collective-permute-start.14) | collective-permute-done | bytes 540704 | tf_op jit(solution)/shard_map/ppermute | solution.py:53
  83.4 8.6 %shard_map.132 = (bf16[2048,128]{1,0:T(8,128)(2,1)S(1)}, bf16[2048,128]{1,0:T(8,128)(2,1)S(1)}, bf16[2048,128]{1,0:T(8,128)(2,1)S(1)}, f32[2048,128]{1,0:T(8,128)S(1)}) custom-call(s32[32,8]{1,0:T(8,128)S(1)} %get-tuple-element.59.slots.slot_ref, f32[32,8]{1,0:T(8,128)S(1)} %get-tuple-element.60.weights, bf16[128,128]{1,0:T(8,128)(2,1)S(1)} %copy-done.3, ...), custom_call_target="tpu_custom_call" | custom-call | flops 100000000 | bytes 1048576 | tf_op jit(solution)/shard_map/pallas_call | solution.py:312
  92.0 1.6 collective-permute-start.34
  93.5 2.7 %collective-permute-start.36 = (bf16[2048,128]{1,0:T(8,128)(2,1)S(1)}, bf16[2048,128]{1,0:T(8,128)(2,1)S(1)}, u32[]{:S(2)}, u32[]{:S(2)}) collective-permute-start(bf16[2048,128]{1,0:T(8,128)(2,1)S(1)} %get-tuple-element.65), channel_id=1, source_target_pairs={{0,96},{1,97},{2,98},{3,99},{4,100},{5,101},{6,102},{7,103},{8,104... | collective-permute-start | bytes 1572872 | tf_op jit(solution)/shard_map/ppermute | solution.py:53
  96.2 27.4 %shard_map.135 = (bf16[2048,128]{1,0:T(8,128)(2,1)S(1)}, bf16[2048,128]{1,0:T(8,128)(2,1)S(1)}, bf16[2048,128]{1,0:T(8,128)(2,1)S(1)}) custom-call(bf16[128,128]{1,0:T(8,128)(2,1)S(1)} %copy-done.3, bf16[256,256]{1,0:T(8,128)(2,1)S(1)} %get-tuple-element.69.right_ref, bf16[256,256]{1,0:T(8,128)(2,1)S(1)} %get-tuple-element.70.left_ref, ...), custom_call_target="tpu_custom_call" | custom-call | flops 100000000 | bytes 1048576 | tf_op jit(solution)/shard_map/pallas_call | solution.py:324
  124.4 2.3 %collective-permute-start.39 = (bf16[2048,128]{1,0:T(8,128)(2,1)S(1)}, bf16[2048,128]{1,0:T(8,128)(2,1)S(1)}, u32[]{:S(2)}, u32[]{:S(2)}) collective-permute-start(bf16[2048,128]{1,0:T(8,128)(2,1)S(1)} %get-tuple-element.78), channel_id=1, source_target_pairs={{0,96},{1,97},{2,98},{3,99},{4,100},{5,101},{6,102},{7,103},{8,104... | collective-permute-start | bytes 1572872 | tf_op jit(solution)/shard_map/ppermute | solution.py:53
  126.7 14.3 %shard_map.134.own_ref = f32[2048,128]{1,0:T(8,128)S(1)} custom-call(bf16[128,128]{1,0:T(8,128)(2,1)S(1)} %copy-done.3, bf16[256,256]{1,0:T(8,128)(2,1)S(1)} %get-tuple-element.69.right_ref, bf16[256,256]{1,0:T(8,128)(2,1)S(1)} %get-tuple-element.70.left_ref, s32[32,8]{1,0:T(8,128)S(1)} %get-tuple-element.71.partner_ref, ...), custom_call_target="tpu_custom_call" | custom-call | flops 100000000 | bytes 1048576 | tf_op jit(solution)/shard_map/pallas_call | solution.py:324
  141.0 6.2 %shard_map.133 = (bf16[2048,128]{1,0:T(8,128)(2,1)S(1)}, f32[4,2,128,128]{3,2,1,0:T(8,128)S(1)}) custom-call(f32[8]{0:T(128)S(1)} %copy-done.6, bf16[2048,128]{1,0:T(8,128)(2,1)S(1)} %bitcast.34, f32[2048,128]{1,0:T(8,128)S(1)} %get-tuple-element.62.own_ref, bf16[2048,128]{1,0:T(8,128)(2,1)S(1)} %collective-permute-done.34.a_ref, ...), custom_call_target="tpu_custom_call" | custom-call | flops 100000000 | bytes 1048576 | tf_op jit(solution)/shard_map/pallas_call | solution.py:395
  147.3 3.0 %collective-permute-done.38.b_ref = bf16[2048,128]{1,0:T(8,128)(2,1)S(1)} collective-permute-done((bf16[2048,128]{1,0:T(8,128)(2,1)S(1)}, bf16[2048,128]{1,0:T(8,128)(2,1)S(1)}, u32[]{:S(2)}, u32[]{:S(2)}) %collective-permute-start.38) | collective-permute-done | bytes 524320 | tf_op jit(solution)/shard_map/ppermute | solution.py:53
  150.3 7.0 %shard_map.136 = (bf16[2048,128]{1,0:T(8,128)(2,1)}, f32[4,2,128,128]{3,2,1,0:T(8,128)S(1)}) custom-call(f32[8]{0:T(128)S(1)} %copy-done.6, bf16[2048,128]{1,0:T(8,128)(2,1)S(1)} %get-tuple-element.68.lam_ref, f32[2048,128]{1,0:T(8,128)S(1)} %shard_map.134.own_ref, bf16[2048,128]{1,0:T(8,128)(2,1)S(1)} %collective-permute-done.37.a_ref, ...), custom_call_target="tpu_custom_call" | custom-call | flops 100000000 | bytes 1048576 | tf_op jit(solution)/shard_map/pallas_call | solution.py:395
  158.0 22.4 %all_to_all.5 = bf16[128,8,2,128]{3,2,1,0:T(2,128)(2,1)S(1)} all-to-all(bf16[128,8,2,128]{3,2,1,0:T(2,128)(2,1)S(1)} %copy.97), channel_id=1, replica_groups=mesh['y'=4,'c'=2,'z'=4,'x'=4] {'y','c','z','x'}, dimensions={0} | all-to-all | bytes 1048576 | tf_op jit(solution)/shard_map/all_to_all | solution.py:475
  (112 shorter events, 28.6 us)
Async XLA Ops:
  2.6 5.4 %collective-permute-start.2 = (f32[8,16]{1,0:T(8,128)S(1)}, f32[8,16]{1,0:T(8,128)S(1)}, u32[]{:S(2)}, u32[]{:S(2)}) collective-permute-start(f32[8,16]{1,0:T(8,128)S(1)} %pad.8), channel_id=1, source_target_pairs={{0,96},{1,97},{2,98},{3,99},{4,100},{5,101},{6,102},{7,103},{8,104... | collective-permute-start | bytes 1544 | tf_op jit(solution)/shard_map/ppermute | solution.py:53
  11.3 11.4 %collective-permute-start.4 = (bf16[2112,128]{1,0:T(8,128)(2,1)S(1)}, bf16[2112,128]{1,0:T(8,128)(2,1)S(1)}, u32[]{:S(2)}, u32[]{:S(2)}) collective-permute-start(bf16[2112,128]{1,0:T(8,128)(2,1)S(1)} %pad_maximum_fusion.refs_0_), channel_id=1, source_target_pairs={{0,16},{1,17},{2,18},{3,19},{4,20},{5,21},{6,22},{7,23},{8,24},{9,... | collective-permute-start | bytes 1622024 | tf_op jit(solution)/shard_map/ppermute | solution.py:53
  14.4 14.9 %collective-permute-start.3 = (bf16[2112,128]{1,0:T(8,128)(2,1)S(1)}, bf16[2112,128]{1,0:T(8,128)(2,1)S(1)}, u32[]{:S(2)}, u32[]{:S(2)}) collective-permute-start(bf16[2112,128]{1,0:T(8,128)(2,1)S(1)} %pad_maximum_fusion.refs_0_), channel_id=1, source_target_pairs={{0,1},{1,2},{2,3},{3,0},{4,5},{5,6},{6,7},{7,4},{8,9},{9,10},{10,1... | collective-permute-start | bytes 1622024 | tf_op jit(solution)/shard_map/ppermute | solution.py:53
  16.0 14.5 %collective-permute-start.5 = (bf16[2112,128]{1,0:T(8,128)(2,1)S(1)}, bf16[2112,128]{1,0:T(8,128)(2,1)S(1)}, u32[]{:S(2)}, u32[]{:S(2)}) collective-permute-start(bf16[2112,128]{1,0:T(8,128)(2,1)S(1)} %pad_maximum_fusion.refs_0_), channel_id=1, source_target_pairs={{0,4},{1,5},{2,6},{3,7},{4,8},{5,9},{6,10},{7,11},{8,12},{9,13},{1... | collective-permute-start | bytes 1622024 | tf_op jit(solution)/shard_map/ppermute | solution.py:53
  17.2 15.5 %collective-permute-start.7 = (bf16[2112,128]{1,0:T(8,128)(2,1)S(1)}, bf16[2112,128]{1,0:T(8,128)(2,1)S(1)}, u32[]{:S(2)}, u32[]{:S(2)}) collective-permute-start(bf16[2112,128]{1,0:T(8,128)(2,1)S(1)} %pad_maximum_fusion.refs_0_), channel_id=1, source_target_pairs={{0,12},{1,13},{2,14},{3,15},{4,0},{5,1},{6,2},{7,3},{8,4},{9,5},{1... | collective-permute-start | bytes 1622024 | tf_op jit(solution)/shard_map/ppermute | solution.py:53
  18.7 19.2 %collective-permute-start.11 = (bf16[2112,128]{1,0:T(8,128)(2,1)S(1)}, bf16[2112,128]{1,0:T(8,128)(2,1)S(1)}, u32[]{:S(2)}, u32[]{:S(2)}) collective-permute-start(bf16[2112,128]{1,0:T(8,128)(2,1)S(1)} %pad_maximum_fusion.refs_0_), channel_id=1, source_target_pairs={{0,2},{1,3},{2,0},{3,1},{4,6},{5,7},{6,4},{7,5},{8,10},{9,11},{10,... | collective-permute-start | bytes 1622024 | tf_op jit(solution)/shard_map/ppermute | solution.py:53
  22.7 16.3 %collective-permute-start.15 = (bf16[2112,128]{1,0:T(8,128)(2,1)S(1)}, bf16[2112,128]{1,0:T(8,128)(2,1)}, u32[]{:S(2)}, u32[]{:S(2)}) collective-permute-start(bf16[2112,128]{1,0:T(8,128)(2,1)S(1)} %pad_maximum_fusion.refs_0_), channel_id=1, source_target_pairs={{0,3},{1,0},{2,1},{3,2},{4,7},{5,4},{6,5},{7,6},{8,11},{9,8},{10,9... | collective-permute-start | bytes 1622024 | tf_op jit(solution)/shard_map/ppermute | solution.py:53
  30.5 12.4 %collective-permute-start.6 = (bf16[2112,128]{1,0:T(8,128)(2,1)S(1)}, bf16[2112,128]{1,0:T(8,128)(2,1)S(1)}, u32[]{:S(2)}, u32[]{:S(2)}) collective-permute-start(bf16[2112,128]{1,0:T(8,128)(2,1)S(1)} %collective-permute-done.5.refs_1_), channel_id=1, source_target_pairs={{0,4},{1,5},{2,6},{3,7},{4,8},{5,9},{6,10},{7,11},{8,12},{9,13},{1... | collective-permute-start | bytes 1622024 | tf_op jit(solution)/shard_map/ppermute | solution.py:53
  31.6 17.1 %collective-permute-start.8 = (bf16[2112,128]{1,0:T(8,128)(2,1)S(1)}, bf16[2112,128]{1,0:T(8,128)(2,1)S(1)}, u32[]{:S(2)}, u32[]{:S(2)}) collective-permute-start(bf16[2112,128]{1,0:T(8,128)(2,1)S(1)} %collective-permute-done.3.refs_4_), channel_id=1, source_target_pairs={{0,4},{1,5},{2,6},{3,7},{4,8},{5,9},{6,10},{7,11},{8,12},{9,13},{1... | collective-permute-start | bytes 1622024 | tf_op jit(solution)/shard_map/ppermute | solution.py:53
  32.8 16.3 %collective-permute-start.9 = (bf16[2112,128]{1,0:T(8,128)(2,1)S(1)}, bf16[2112,128]{1,0:T(8,128)(2,1)S(1)}, u32[]{:S(2)}, u32[]{:S(2)}) collective-permute-start(bf16[2112,128]{1,0:T(8,128)(2,1)S(1)} %collective-permute-done.3.refs_4_), channel_id=1, source_target_pairs={{0,12},{1,13},{2,14},{3,15},{4,0},{5,1},{6,2},{7,3},{8,4},{9,5},{1... | collective-permute-start | bytes 1622024 | tf_op jit(solution)/shard_map/ppermute | solution.py:53
  37.9 16.6 %collective-permute-start.12 = (bf16[2112,128]{1,0:T(8,128)(2,1)S(1)}, bf16[2112,128]{1,0:T(8,128)(2,1)S(1)}, u32[]{:S(2)}, u32[]{:S(2)}) collective-permute-start(bf16[2112,128]{1,0:T(8,128)(2,1)S(1)} %collective-permute-done.11.refs_8_), channel_id=1, source_target_pairs={{0,4},{1,5},{2,6},{3,7},{4,8},{5,9},{6,10},{7,11},{8,12},{9,13},{1... | collective-permute-start | bytes 1622024 | tf_op jit(solution)/shard_map/ppermute | solution.py:53
  39.0 16.8 %collective-permute-start.13 = (bf16[2112,128]{1,0:T(8,128)(2,1)S(1)}, bf16[2112,128]{1,0:T(8,128)(2,1)S(1)}, u32[]{:S(2)}, u32[]{:S(2)}) collective-permute-start(bf16[2112,128]{1,0:T(8,128)(2,1)S(1)} %collective-permute-done.11.refs_8_), channel_id=1, source_target_pairs={{0,12},{1,13},{2,14},{3,15},{4,0},{5,1},{6,2},{7,3},{8,4},{9,5},{1... | collective-permute-start | bytes 1622024 | tf_op jit(solution)/shard_map/ppermute | solution.py:53
  42.9 17.4 %collective-permute-start.16 = (bf16[2112,128]{1,0:T(8,128)(2,1)}, bf16[2112,128]{1,0:T(8,128)(2,1)S(1)}, u32[]{:S(2)}, u32[]{:S(2)}) collective-permute-start(bf16[2112,128]{1,0:T(8,128)(2,1)} %collective-permute-done.15.refs_12_), channel_id=1, source_target_pairs={{0,4},{1,5},{2,6},{3,7},{4,8},{5,9},{6,10},{7,11},{8,12},{9,13},{1... | collective-permute-start | bytes 1622024 | tf_op jit(solution)/shard_map/ppermute | solution.py:53
  48.7 12.8 %collective-permute-start.18 = (bf16[2112,128]{1,0:T(8,128)(2,1)}, bf16[2112,128]{1,0:T(8,128)(2,1)S(1)}, u32[]{:S(2)}, u32[]{:S(2)}) collective-permute-start(bf16[2112,128]{1,0:T(8,128)(2,1)} %collective-permute-done.15.refs_12_), channel_id=1, source_target_pairs={{0,12},{1,13},{2,14},{3,15},{4,0},{5,1},{6,2},{7,3},{8,4},{9,5},{1... | collective-permute-start | bytes 1622024 | tf_op jit(solution)/shard_map/ppermute | solution.py:53
  49.0 12.5 %collective-permute-start.19 = (bf16[2112,128]{1,0:T(8,128)(2,1)S(1)}, bf16[2112,128]{1,0:T(8,128)(2,1)S(1)}, u32[]{:S(2)}, u32[]{:S(2)}) collective-permute-start(bf16[2112,128]{1,0:T(8,128)(2,1)S(1)} %collective-permute-done.5.refs_1_), channel_id=1, source_target_pairs={{0,16},{1,17},{2,18},{3,19},{4,20},{5,21},{6,22},{7,23},{8,24},{9,... | collective-permute-start | bytes 1622024 | tf_op jit(solution)/shard_map/ppermute | solution.py:53
  54.5 9.5 %collective-permute-start.21 = (bf16[2112,128]{1,0:T(8,128)(2,1)S(1)}, bf16[2112,128]{1,0:T(8,128)(2,1)S(1)}, u32[]{:S(2)}, u32[]{:S(2)}) collective-permute-start(bf16[2112,128]{1,0:T(8,128)(2,1)S(1)} %collective-permute-done.7.refs_3_), channel_id=1, source_target_pairs={{0,16},{1,17},{2,18},{3,19},{4,20},{5,21},{6,22},{7,23},{8,24},{9,... | collective-permute-start | bytes 1622024 | tf_op jit(solution)/shard_map/ppermute | solution.py:53
  55.7 8.9 %collective-permute-start.22 = (bf16[2112,128]{1,0:T(8,128)(2,1)S(1)}, bf16[2112,128]{1,0:T(8,128)(2,1)S(1)}, u32[]{:S(2)}, u32[]{:S(2)}) collective-permute-start(bf16[2112,128]{1,0:T(8,128)(2,1)S(1)} %collective-permute-done.3.refs_4_), channel_id=1, source_target_pairs={{0,16},{1,17},{2,18},{3,19},{4,20},{5,21},{6,22},{7,23},{8,24},{9,... | collective-permute-start | bytes 1622024 | tf_op jit(solution)/shard_map/ppermute | solution.py:53
  60.3 5.2 %collective-permute-start.26 = (bf16[2112,128]{1,0:T(8,128)(2,1)S(1)}, bf16[2112,128]{1,0:T(8,128)(2,1)S(1)}, u32[]{:S(2)}, u32[]{:S(2)}) collective-permute-start(bf16[2112,128]{1,0:T(8,128)(2,1)S(1)} %collective-permute-done.11.refs_8_), channel_id=1, source_target_pairs={{0,16},{1,17},{2,18},{3,19},{4,20},{5,21},{6,22},{7,23},{8,24},{9,... | collective-permute-start | bytes 1622024 | tf_op jit(solution)/shard_map/ppermute | solution.py:53
  61.5 5.1 %collective-permute-start.30 = (bf16[2112,128]{1,0:T(8,128)(2,1)}, bf16[2112,128]{1,0:T(8,128)(2,1)S(1)}, u32[]{:S(2)}, u32[]{:S(2)}) collective-permute-start(bf16[2112,128]{1,0:T(8,128)(2,1)} %collective-permute-done.15.refs_12_), channel_id=1, source_target_pairs={{0,16},{1,17},{2,18},{3,19},{4,20},{5,21},{6,22},{7,23},{8,24},{9,... | collective-permute-start | bytes 1622024 | tf_op jit(solution)/shard_map/ppermute | solution.py:53
  61.5 8.8 %collective-permute-start.10 = (bf16[2112,128]{1,0:T(8,128)(2,1)S(1)}, bf16[2112,128]{1,0:T(8,128)(2,1)S(1)}, u32[]{:S(2)}, u32[]{:S(2)}) collective-permute-start(bf16[2112,128]{1,0:T(8,128)(2,1)S(1)} %collective-permute-done.9.refs_7_), channel_id=1, source_target_pairs={{0,12},{1,13},{2,14},{3,15},{4,0},{5,1},{6,2},{7,3},{8,4},{9,5},{1... | collective-permute-start | bytes 1622024 | tf_op jit(solution)/shard_map/ppermute | solution.py:53
  64.1 12.1 %collective-permute-start.14 = (bf16[2112,128]{1,0:T(8,128)(2,1)S(1)}, bf16[2112,128]{1,0:T(8,128)(2,1)S(1)}, u32[]{:S(2)}, u32[]{:S(2)}) collective-permute-start(bf16[2112,128]{1,0:T(8,128)(2,1)S(1)} %collective-permute-done.13.refs_11_), channel_id=1, source_target_pairs={{0,12},{1,13},{2,14},{3,15},{4,0},{5,1},{6,2},{7,3},{8,4},{9,5},{1... | collective-permute-start | bytes 1622024 | tf_op jit(solution)/shard_map/ppermute | solution.py:53
  64.6 12.6 %collective-permute-start.17 = (bf16[2112,128]{1,0:T(8,128)(2,1)S(1)}, bf16[2112,128]{1,0:T(8,128)(2,1)S(1)}, u32[]{:S(2)}, u32[]{:S(2)}) collective-permute-start(bf16[2112,128]{1,0:T(8,128)(2,1)S(1)} %collective-permute-done.16.refs_13_), channel_id=1, source_target_pairs={{0,4},{1,5},{2,6},{3,7},{4,8},{5,9},{6,10},{7,11},{8,12},{9,13},{1... | collective-permute-start | bytes 1622024 | tf_op jit(solution)/shard_map/ppermute | solution.py:53
  65.5 11.7 %collective-permute-start.20 = (bf16[2112,128]{1,0:T(8,128)(2,1)S(1)}, bf16[2112,128]{1,0:T(8,128)(2,1)S(1)}, u32[]{:S(2)}, u32[]{:S(2)}) collective-permute-start(bf16[2112,128]{1,0:T(8,128)(2,1)S(1)} %collective-permute-done.6.refs_2_), channel_id=1, source_target_pairs={{0,16},{1,17},{2,18},{3,19},{4,20},{5,21},{6,22},{7,23},{8,24},{9,... | collective-permute-start | bytes 1622024 | tf_op jit(solution)/shard_map/ppermute | solution.py:53
  66.6 11.1 %collective-permute-start.23 = (bf16[2112,128]{1,0:T(8,128)(2,1)S(1)}, bf16[2112,128]{1,0:T(8,128)(2,1)S(1)}, u32[]{:S(2)}, u32[]{:S(2)}) collective-permute-start(bf16[2112,128]{1,0:T(8,128)(2,1)S(1)} %collective-permute-done.8.refs_5_), channel_id=1, source_target_pairs={{0,16},{1,17},{2,18},{3,19},{4,20},{5,21},{6,22},{7,23},{8,24},{9,... | collective-permute-start | bytes 1622024 | tf_op jit(solution)/shard_map/ppermute | solution.py:53
  70.4 7.4 %collective-permute-start.25 = (bf16[2112,128]{1,0:T(8,128)(2,1)S(1)}, bf16[2112,128]{1,0:T(8,128)(2,1)S(1)}, u32[]{:S(2)}, u32[]{:S(2)}) collective-permute-start(bf16[2112,128]{1,0:T(8,128)(2,1)S(1)} %collective-permute-done.9.refs_7_), channel_id=1, source_target_pairs={{0,16},{1,17},{2,18},{3,19},{4,20},{5,21},{6,22},{7,23},{8,24},{9,... | collective-permute-start | bytes 1622024 | tf_op jit(solution)/shard_map/ppermute | solution.py:53
  77.8 4.0 %collective-permute-start.24 = (bf16[2112,128]{1,0:T(8,128)(2,1)S(1)}, bf16[2112,128]{1,0:T(8,128)(2,1)S(1)}, u32[]{:S(2)}, u32[]{:S(2)}) collective-permute-start(bf16[2112,128]{1,0:T(8,128)(2,1)S(1)} %collective-permute-done.10.refs_6_), channel_id=1, source_target_pairs={{0,16},{1,17},{2,18},{3,19},{4,20},{5,21},{6,22},{7,23},{8,24},{9,... | collective-permute-start | bytes 1622024 | tf_op jit(solution)/shard_map/ppermute | solution.py:53
  92.0 32.4 %collective-permute-start.34 = (bf16[2048,128]{1,0:T(8,128)(2,1)S(1)}, bf16[2048,128]{1,0:T(8,128)(2,1)S(1)}, u32[]{:S(2)}, u32[]{:S(2)}) collective-permute-start(bf16[2048,128]{1,0:T(8,128)(2,1)S(1)} %get-tuple-element.63), channel_id=1, source_target_pairs={{0,64},{1,65},{2,66},{3,67},{4,68},{5,69},{6,70},{7,71},{8,72},{9,... | collective-permute-start | bytes 1572872 | tf_op jit(solution)/shard_map/ppermute | solution.py:53
  93.5 47.5 %collective-permute-start.35 = (bf16[2048,128]{1,0:T(8,128)(2,1)S(1)}, bf16[2048,128]{1,0:T(8,128)(2,1)S(1)}, u32[]{:S(2)}, u32[]{:S(2)}) collective-permute-start(bf16[2048,128]{1,0:T(8,128)(2,1)S(1)} %get-tuple-element.64), channel_id=1, source_target_pairs={{0,32},{1,33},{2,34},{3,35},{4,36},{5,37},{6,38},{7,39},{8,40},{9,... | collective-permute-start | bytes 1572872 | tf_op jit(solution)/shard_map/ppermute | solution.py:53
  93.5 47.5 %collective-permute-start.36 = (bf16[2048,128]{1,0:T(8,128)(2,1)S(1)}, bf16[2048,128]{1,0:T(8,128)(2,1)S(1)}, u32[]{:S(2)}, u32[]{:S(2)}) collective-permute-start(bf16[2048,128]{1,0:T(8,128)(2,1)S(1)} %get-tuple-element.65), channel_id=1, source_target_pairs={{0,96},{1,97},{2,98},{3,99},{4,100},{5,101},{6,102},{7,103},{8,104... | collective-permute-start | bytes 1572872 | tf_op jit(solution)/shard_map/ppermute | solution.py:53
  123.6 23.6 %collective-permute-start.37 = (bf16[2048,128]{1,0:T(8,128)(2,1)S(1)}, bf16[2048,128]{1,0:T(8,128)(2,1)S(1)}, u32[]{:S(2)}, u32[]{:S(2)}) collective-permute-start(bf16[2048,128]{1,0:T(8,128)(2,1)S(1)} %get-tuple-element.76), channel_id=1, source_target_pairs={{0,64},{1,65},{2,66},{3,67},{4,68},{5,69},{6,70},{7,71},{8,72},{9,... | collective-permute-start | bytes 1572872 | tf_op jit(solution)/shard_map/ppermute | solution.py:53
  124.0 26.3 %collective-permute-start.38 = (bf16[2048,128]{1,0:T(8,128)(2,1)S(1)}, bf16[2048,128]{1,0:T(8,128)(2,1)S(1)}, u32[]{:S(2)}, u32[]{:S(2)}) collective-permute-start(bf16[2048,128]{1,0:T(8,128)(2,1)S(1)} %get-tuple-element.77), channel_id=1, source_target_pairs={{0,32},{1,33},{2,34},{3,35},{4,36},{5,37},{6,38},{7,39},{8,40},{9,... | collective-permute-start | bytes 1572872 | tf_op jit(solution)/shard_map/ppermute | solution.py:53
  124.4 25.9 %collective-permute-start.39 = (bf16[2048,128]{1,0:T(8,128)(2,1)S(1)}, bf16[2048,128]{1,0:T(8,128)(2,1)S(1)}, u32[]{:S(2)}, u32[]{:S(2)}) collective-permute-start(bf16[2048,128]{1,0:T(8,128)(2,1)S(1)} %get-tuple-element.78), channel_id=1, source_target_pairs={{0,96},{1,97},{2,98},{3,99},{4,100},{5,101},{6,102},{7,103},{8,104... | collective-permute-start | bytes 1572872 | tf_op jit(solution)/shard_map/ppermute | solution.py:53
  (21 other events, 235.6 us)

commit v4 on v3

--- a/solution.py
+++ b/solution.py
@@ -17,7 +17,7 @@
 DIM = 128
 ROWS = 2 * DIM
 BLOCK = OWN * ROWS
-GROUP = 4
+GROUP = 8
 EXTRA = 64
 
 
@@ -204,27 +204,51 @@
     spot = jnp.where(keep, spot, -1)
     kind = jnp.where(lane < 64, lane >> 4, 4 + ((lane - 64) >> 2)).astype(F32)
     code, weight = slot + 256.0 * kind, total * scale_ref[...]
-    codes = jnp.where(lane == DIM - 1, jnp.sum(kept, axis=1, keepdims=True), 0.0)
-    weights = jnp.zeros((32, DIM), F32)
-    for n in range(72):
-        here = spot == n
-        codes = jnp.where(lane == n, jnp.sum(jnp.where(here, code, 0.0), axis=1, keepdims=True), codes)
-        weights = jnp.where(lane == n, jnp.sum(jnp.where(here, weight, 0.0), axis=1, keepdims=True), weights)
+    counts = jnp.sum(kept, axis=1, keepdims=True)
+
+    def place_some(step, lists):
+        codes, weights = lists
+        for e in range(8):
+            n = step * 8 + e
+            here = spot == n
+            one = jnp.sum(jnp.where(here, code, 0.0), axis=1, keepdims=True)
+            two = jnp.sum(jnp.where(here, weight, 0.0), axis=1, keepdims=True)
+            codes, weights = jnp.where(lane == n, one, codes), jnp.where(lane == n, two, weights)
+        return codes, weights
+
+    empty = (jnp.zeros((32, DIM), F32), jnp.zeros((32, DIM), F32))
+    codes, weights = lax.fori_loop(0, (jnp.max(counts).astype(jnp.int32) + 7) >> 3, place_some, empty)
+    codes = jnp.where(lane == DIM - 1, counts, codes)
     code_v[...] = codes.astype(jnp.int32)
     weight_v[...] = weights
 
 
-def far_kernel(order, c_ref, right_ref, left_ref, partner_ref, row_ref, ladder_ref, scale_ref, slot_ref, links, *refs):
-    blocks, outs = refs[:32], refs[32 : 32 + len(order)]
-    held, extra, main_sems, extra_sems, *rest = refs[32 + len(order) :]
-    acc, lefts, rights, kept, double, code_v, weight_v, code_s, weight_s, sems = rest
+def far_kernel(order, c_ref, right_ref, left_ref, *refs):
+    small, blocks, refs = refs[:6], refs[6:38], refs[38:]
+    outs, code_v, weight_v = refs[: len(order)], refs[len(order)], refs[len(order) + 1]
+    held, main_sems, extra, extra_sems, *rest = refs[len(order) + 2 :]
     tails = copies_of(blocks, extra, extra_sems, BLOCK, EXTRA)
     mains = copies_of(blocks, held, main_sems, 0, BLOCK)
     for copy in tails + mains:
         copy.start()
     for copy in tails:
         copy.wait()
-    make_lists(partner_ref, row_ref, ladder_ref, scale_ref, slot_ref, links, extra, code_v, weight_v)
+    make_lists(*small, extra, code_v, weight_v)
+    far_sums(order, c_ref, right_ref, left_ref, outs, held, mains, code_v, weight_v, *rest)
+
+
+def own_kernel(slots, weights, c_ref, right_ref, left_ref, code_v, weight_v, *refs):
+    blocks, (far_out, near_out) = refs[:32], refs[32:34]
+    held, main_sems, near_acc, near_lefts, near_rights, *rest = refs[34:]
+    mains = copies_of(blocks, held, main_sems, 0, BLOCK)
+    for copy in mains:
+        copy.start()
+    far_sums((0,), c_ref, right_ref, left_ref, (far_out,), held, mains, code_v, weight_v, *rest)
+    near_sums((0,), held, slots, weights, c_ref, (near_out,), near_acc, near_lefts, near_rights)
+
+
+def far_sums(order, c_ref, right_ref, left_ref, outs, held, mains, code_v, weight_v, *refs):
+    acc, lefts, rights, kept, double, code_s, weight_s, sems = refs
     codes = pltpu.make_async_copy(code_v, code_s, sems.at[0])
     weights = pltpu.make_async_copy(weight_v, weight_s, sems.at[1])
     codes.start()
@@ -257,30 +281,33 @@
                 lax.fori_loop(0, (code_s[d, DIM - 1] + 1) >> 1, add, 0)
                 kept[g, 0] = acc[4] + acc[5]
                 kept[g, 1] = acc[4] - acc[5]
-                lefts[g, 0:DIM] = crossed((acc[0] + acc[1]).astype(BF))
-                lefts[g, DIM:ROWS] = crossed((acc[2] + acc[3]).astype(BF))
-                rights[g, :, 0:DIM] = (acc[0] - acc[1]).astype(BF)
-                rights[g, :, DIM:ROWS] = (acc[2] - acc[3]).astype(BF)
+                at = pl.multiple_of(g * ROWS, ROWS)
+                lefts[0:DIM, pl.ds(at, ROWS)] = crossed((acc[0] + acc[1]).astype(BF))
+                lefts[DIM:ROWS, pl.ds(at, ROWS)] = crossed((acc[2] + acc[3]).astype(BF))
+                rights[pl.ds(at, ROWS), 0:DIM] = (acc[0] - acc[1]).astype(BF)
+                rights[pl.ds(at, ROWS), DIM:ROWS] = (acc[2] - acc[3]).astype(BF)
                 return 0
 
             lax.fori_loop(0, GROUP, links, 0)
             c, cc, w, wh = c_ref[...], double[...], right_ref[...], left_ref[...]
-            turned = []
-            for g in range(GROUP):
-                left, right = mm(cc, lefts[g]), mm(rights[g], cc)
-                halves = []
+            cuts = [slice(g * ROWS, (g + 1) * ROWS) for g in range(GROUP)]
+            left, right = mm(cc, lefts[...]), mm(rights[...], cc)
+            halves = []
+            for g, at in enumerate(cuts):
                 for k in range(2):
-                    side, cols = left[k * DIM : (k + 1) * DIM], right[:, k * DIM : (k + 1) * DIM]
+                    side, cols = left[k * DIM : (k + 1) * DIM, at], right[at, k * DIM : (k + 1) * DIM]
                     re = kept[g, k, 0:DIM] + side[:, :DIM] - cols[DIM:]
                     im = kept[g, k, DIM:ROWS] + side[:, DIM:] + cols[:DIM]
                     halves.append(jnp.concatenate([re, im], axis=1).astype(BF))
-                mid = mm(jnp.concatenate(halves), w).astype(BF)
-                turned.append(mm(wh, stack_parts(mid)).astype(BF))
-            for g in range(GROUP):
-                left, right = mm(c, crossed(turned[g][:, :DIM])), mm(turned[g][:, DIM:], c)
-                at = pl.multiple_of((h * GROUP + g) * ROWS, ROWS)
-                out[pl.ds(at, DIM), :] = (left[:, :DIM] - right[DIM:]).astype(out.dtype)
-                out[pl.ds(at + DIM, DIM), :] = (left[:, DIM:] + right[:DIM]).astype(out.dtype)
+            mid = mm(jnp.concatenate(halves), w).astype(BF)
+            turned = mm(wh, jnp.concatenate([stack_parts(mid[at]) for at in cuts], axis=1)).astype(BF)
+            parts = [turned[:, at] for at in cuts]
+            left = mm(c, jnp.concatenate([crossed(t[:, :DIM]) for t in parts], axis=1))
+            right = mm(jnp.concatenate([t[:, DIM:] for t in parts]), c)
+            for g, at in enumerate(cuts):
+                to = pl.multiple_of((h * GROUP + g) * ROWS, ROWS)
+                out[pl.ds(to, DIM), :] = (left[:, at][:, :DIM] - right[at][DIM:]).astype(out.dtype)
+                out[pl.ds(to + DIM, DIM), :] = (left[:, at][:, DIM:] + right[at][:DIM]).astype(out.dtype)
             return 0
 
         lax.fori_loop(0, OWN // GROUP, group, 0)
@@ -320,31 +347,48 @@
     )(*lists, coupling, *blocks)
 
 
+def far_scratch():
+    return [
+        pltpu.VMEM((6, ROWS, DIM), F32),
+        pltpu.VMEM((ROWS, GROUP * ROWS), BF),
+        pltpu.VMEM((GROUP * ROWS, ROWS), BF),
+        pltpu.VMEM((GROUP, 2, ROWS, DIM), F32),
+        pltpu.VMEM((ROWS, ROWS), BF),
+        pltpu.SMEM((32, DIM), jnp.int32),
+        pltpu.SMEM((32, DIM), F32),
+        pltpu.SemaphoreType.DMA((2,)),
+    ]
+
+
+def held_scratch(rows):
+    return [pltpu.VMEM((32 * rows, DIM), BF), pltpu.SemaphoreType.DMA((32,))]
+
+
+LISTS = [jax.ShapeDtypeStruct((32, DIM), jnp.int32), jax.ShapeDtypeStruct((32, DIM), F32)]
+
+
 def far_parts(order, arrays, blocks):
     return pl.pallas_call(
         functools.partial(far_kernel, order),
-        out_shape=part_shapes(order),
+        out_shape=part_shapes(order) + LISTS,
         in_specs=[VM] * len(arrays) + [FAR] * 32,
-        out_specs=[VM] * len(order),
-        scratch_shapes=[
-            pltpu.VMEM((32 * BLOCK, DIM), BF),
-            pltpu.VMEM((32 * EXTRA, DIM), BF),
-            pltpu.SemaphoreType.DMA((32,)),
-            pltpu.SemaphoreType.DMA((32,)),
-            pltpu.VMEM((6, ROWS, DIM), F32),
-            pltpu.VMEM((GROUP, ROWS, ROWS), BF),
-            pltpu.VMEM((GROUP, ROWS, ROWS), BF),
-            pltpu.VMEM((GROUP, 2, ROWS, DIM), F32),
-            pltpu.VMEM((ROWS, ROWS), BF),
-            pltpu.VMEM((32, DIM), jnp.int32),
-            pltpu.VMEM((32, DIM), F32),
-            pltpu.SMEM((32, DIM), jnp.int32),
-            pltpu.SMEM((32, DIM), F32),
-            pltpu.SemaphoreType.DMA((2,)),
-        ],
+        out_specs=[VM] * (len(order) + 2),
+        scratch_shapes=held_scratch(BLOCK) + held_scratch(EXTRA) + far_scratch(),
         compiler_params=pltpu.CompilerParams(vmem_limit_bytes=30 << 20),
         cost_estimate=pl.CostEstimate(flops=10**8, bytes_accessed=1 << 20, transcendentals=0),
     )(*arrays, *blocks)
+
+
+def own_parts(scalars, arrays, blocks):
+    return pl.pallas_call(
+        own_kernel,
+        out_shape=part_shapes((0, 0)),
+        in_specs=[SM] * 2 + [VM] * len(arrays) + [FAR] * 32,
+        out_specs=[VM] * 2,
+        scratch_shapes=held_scratch(BLOCK) + near_scratch() + far_scratch(),
+        compiler_params=pltpu.CompilerParams(vmem_limit_bytes=30 << 20),
+        cost_estimate=pl.CostEstimate(flops=10**8, bytes_accessed=1 << 20, transcendentals=0),
+    )(*scalars, *arrays, *blocks)
 
 
 def chain_kernel(step, decay, lam_ref, own_ref, a_ref, b_ref, d_ref, right_ref, left_ref, saved_hbm, *refs):
@@ -460,13 +504,14 @@
 
     made, blocks = gather_layer(jnp.concatenate([lam, tail]), prepare)
     whole_right, whole_left, right, left, weights, ladders, scale, partner, rows, slots, table = made
-    one_2, one_1, one_3, one_0 = near_parts((2, 1, 3, 0), [slots, weights], coupling, blocks)
-    got_one = [one_0] + [send(p, along_y(s)) for p, s in ((one_2, 2), (one_1, 1), (one_3, 3))]
-    arrays = [coupling, whole_right, whole_left, partner, rows, ladders, scale, slots, table]
-    two_2, two_1, two_3 = far_parts((2, 1, 3), arrays, blocks)
+    one_2, one_1, one_3 = near_parts((2, 1, 3), [slots, weights], coupling, blocks)
+    got_one = [send(p, along_y(s)) for p, s in ((one_2, 2), (one_1, 1), (one_3, 3))]
+    whole = [coupling, whole_right, whole_left]
+    small = [partner, rows, ladders, scale, slots, table]
+    two_2, two_1, two_3, *lists = far_parts((2, 1, 3), whole + small, blocks)
     got_two = [send(p, along_y(s)) for p, s in ((two_2, 2), (two_1, 1), (two_3, 3))]
-    [two_0] = far_parts((0,), arrays, blocks)
-    got_two = [two_0] + got_two
+    two_0, one_0 = own_parts([slots, weights], whole + lists, blocks)
+    got_one, got_two = [one_0] + got_one, [two_0] + got_two
     saved = saved.reshape(8, BLOCK, DIM)
     lam, grad_one = chain(0, decay, lam, got_one, right, left, saved)
     lam, grad_two = chain(1, decay, lam, got_two, right, left, saved)

time: 182 us -> 173 us (0.951)
  Pallas kernels: 64.3 us -> 52 us
  waiting for transfers between devices: 37 us -> 41.5 us
    pallas_call x2 -> x1, Pallas kernels: 41.7 us -> 21.1 us  [far_parts(): pl.pallas_call(functools.partial(far_kernel, order), out_shape=part_shape...]
    pallas_call x0 -> x1, Pallas kernels: none -> 9.71 us  [own_parts(): pl.pallas_call(own_kernel, out_shape=part_shapes((0, 0)), in_specs=[SM] *...]
    ppermute x40, waiting for transfers between devices: 37 us -> 41.5 us  [send(): return lax.ppermute(a, AXES, route)]
  transfers between devices with their start and end apart: 40 -> 40, of which waited for: 18 -> 18; matrix products, arithmetic and copies ran while one was open for 2% -> 2% of each run, Pallas kernels for 27% -> 22%
where the time goes in v4:
time: 173 us
  Pallas kernels  52 us (30%)
  starting transfers between devices  44.9 us (26%)
  waiting for transfers between devices  41.5 us (24%)
  blocking collectives  21.9 us (13%)
  local copies, waits for them, and re-layouts  6.01 us (3%)
  other arithmetic  5.76 us (3%)
    ppermute x40, starting transfers between devices, send(): return lax.ppermute(a, AXES, route)  44.9 us
    ppermute x40, waiting for transfers between devices, send(): return lax.ppermute(a, AXES, route)  41.5 us
    all_to_all x1, blocking collectives, body(): grad = lax.all_to_all(grad, AXES, 0, 0, tiled=True)  21.9 us
    pallas_call x1, Pallas kernels, far_parts(): pl.pallas_call(functools.partial(far_kernel, order), out_shape=part_shape...  21.1 us
    pallas_call x2, Pallas kernels, chain(): pl.pallas_call(functools.partial(chain_kernel, step), out_shape=[jax.Shap...  13.2 us
    pallas_call x1, Pallas kernels, own_parts(): pl.pallas_call(own_kernel, out_shape=part_shapes((0, 0)), in_specs=[SM] *...  9.71 us
    pallas_call x1, Pallas kernels, near_parts(): pl.pallas_call(functools.partial(near_kernel, order), out_shape=part_shap...  7.18 us
  transfers between devices with their start and end apart: 40, of which 18 were waited for; matrix products, arithmetic and copies ran while one was open for 2% of the time, Pallas kernels for 22%

profile of v4, /device:TPU:1, one launch (start us, length us, event | category | flops | bytes accessed | tf_op | source)
XLA Modules:
  0.0 173.0 jit_solution(5498554546432593326)
XLA Ops:
  2.6 3.6 %collective-permute-start.2 = (f32[8,16]{1,0:T(8,128)S(1)}, f32[8,16]{1,0:T(8,128)S(1)}, u32[]{:S(2)}, u32[]{:S(2)}) collective-permute-start(f32[8,16]{1,0:T(8,128)S(1)} %pad.8), channel_id=1, source_target_pairs={{0,96},{1,97},{2,98},{3,99},{4,100},{5,101},{6,102},{7,103},{8,104... | collective-permute-start | bytes 1544 | tf_op jit(solution)/shard_map/ppermute | solution.py:53
  8.0 2.1 %collective-permute-done.1 = f32[8,16]{1,0:T(8,128)S(1)} collective-permute-done((f32[8,16]{1,0:T(8,128)S(1)}, f32[8,16]{1,0:T(8,128)S(1)}, u32[]{:S(2)}, u32[]{:S(2)}) %collective-permute-start.1) | collective-permute-done | bytes 544 | tf_op jit(solution)/shard_map/ppermute | solution.py:53
  11.3 2.5 %collective-permute-start.4 = (bf16[2112,128]{1,0:T(8,128)(2,1)S(1)}, bf16[2112,128]{1,0:T(8,128)(2,1)S(1)}, u32[]{:S(2)}, u32[]{:S(2)}) collective-permute-start(bf16[2112,128]{1,0:T(8,128)(2,1)S(1)} %pad_maximum_fusion.refs_6_.refs_0_), channel_id=1, source_target_pairs={{0,16},{1,17},{2,18},{3,19},{4,20},{5,21},{6,22},{7,23},{8,24},{9,... | collective-permute-start | bytes 1622024 | tf_op jit(solution)/shard_map/ppermute | solution.py:53
  14.4 1.6 collective-permute-start.3
  16.0 1.2 collective-permute-start.5
  17.2 1.5 collective-permute-start.7
  18.7 3.3 %collective-permute-start.11 = (bf16[2112,128]{1,0:T(8,128)(2,1)S(1)}, bf16[2112,128]{1,0:T(8,128)(2,1)S(1)}, u32[]{:S(2)}, u32[]{:S(2)}) collective-permute-start(bf16[2112,128]{1,0:T(8,128)(2,1)S(1)} %pad_maximum_fusion.refs_6_.refs_0_), channel_id=1, source_target_pairs={{0,2},{1,3},{2,0},{3,1},{4,6},{5,7},{6,4},{7,5},{8,10},{9,11},{10,... | collective-permute-start | bytes 1622024 | tf_op jit(solution)/shard_map/ppermute | solution.py:53
  29.2 1.3 collective-permute-done.5.refs_7_.refs_1_
  31.6 1.1 collective-permute-start.8
  32.8 2.4 %collective-permute-start.9 = (bf16[2112,128]{1,0:T(8,128)(2,1)S(1)}, bf16[2112,128]{1,0:T(8,128)(2,1)S(1)}, u32[]{:S(2)}, u32[]{:S(2)}) collective-permute-start(bf16[2112,128]{1,0:T(8,128)(2,1)S(1)} %collective-permute-done.3.refs_10_.refs_4_), channel_id=1, source_target_pairs={{0,12},{1,13},{2,14},{3,15},{4,0},{5,1},{6,2},{7,3},{8,4},{9,5},{1... | collective-permute-start | bytes 1622024 | tf_op jit(solution)/shard_map/ppermute | solution.py:53
  35.1 2.8 %collective-permute-done.11.refs_14_.refs_8_ = bf16[2112,128]{1,0:T(8,128)(2,1)S(1)} collective-permute-done((bf16[2112,128]{1,0:T(8,128)(2,1)S(1)}, bf16[2112,128]{1,0:T(8,128)(2,1)S(1)}, u32[]{:S(2)}, u32[]{:S(2)}) %collective-permute-start.11) | collective-permute-done | bytes 540704 | tf_op jit(solution)/shard_map/ppermute | solution.py:53
  39.0 1.7 collective-permute-start.13
  40.6 2.3 %collective-permute-done.6.refs_8_.refs_2_ = bf16[2112,128]{1,0:T(8,128)(2,1)S(1)} collective-permute-done((bf16[2112,128]{1,0:T(8,128)(2,1)S(1)}, bf16[2112,128]{1,0:T(8,128)(2,1)S(1)}, u32[]{:S(2)}, u32[]{:S(2)}) %collective-permute-start.6) | collective-permute-done | bytes 540704 | tf_op jit(solution)/shard_map/ppermute | solution.py:53
  42.9 5.8 %collective-permute-done.8.refs_11_.refs_5_ = bf16[2112,128]{1,0:T(8,128)(2,1)S(1)} collective-permute-done((bf16[2112,128]{1,0:T(8,128)(2,1)S(1)}, bf16[2112,128]{1,0:T(8,128)(2,1)S(1)}, u32[]{:S(2)}, u32[]{:S(2)}) %collective-permute-start.8) | collective-permute-done | bytes 540704 | tf_op jit(solution)/shard_map/ppermute | solution.py:53
  49.0 3.4 %collective-permute-start.19 = (bf16[2112,128]{1,0:T(8,128)(2,1)S(1)}, bf16[2112,128]{1,0:T(8,128)(2,1)S(1)}, u32[]{:S(2)}, u32[]{:S(2)}) collective-permute-start(bf16[2112,128]{1,0:T(8,128)(2,1)S(1)} %collective-permute-done.5.refs_7_.refs_1_), channel_id=1, source_target_pairs={{0,16},{1,17},{2,18},{3,19},{4,20},{5,21},{6,22},{7,23},{8,24},{9,... | collective-permute-start | bytes 1622024 | tf_op jit(solution)/shard_map/ppermute | solution.py:53
  52.4 2.1 %collective-permute-done.12.refs_15_.refs_9_ = bf16[2112,128]{1,0:T(8,128)(2,1)S(1)} collective-permute-done((bf16[2112,128]{1,0:T(8,128)(2,1)S(1)}, bf16[2112,128]{1,0:T(8,128)(2,1)S(1)}, u32[]{:S(2)}, u32[]{:S(2)}) %collective-permute-start.12) | collective-permute-done | bytes 540704 | tf_op jit(solution)/shard_map/ppermute | solution.py:53
  54.5 1.2 collective-permute-start.21
  55.7 4.6 %collective-permute-done.16.refs_19_.refs_13_ = bf16[2112,128]{1,0:T(8,128)(2,1)S(1)} collective-permute-done((bf16[2112,128]{1,0:T(8,128)(2,1)}, bf16[2112,128]{1,0:T(8,128)(2,1)S(1)}, u32[]{:S(2)}, u32[]{:S(2)}) %collective-permute-start.16) | collective-permute-done | bytes 540704 | tf_op jit(solution)/shard_map/ppermute | solution.py:53
  60.3 1.2 collective-permute-start.26
  61.5 2.5 %collective-permute-start.10 = (bf16[2112,128]{1,0:T(8,128)(2,1)S(1)}, bf16[2112,128]{1,0:T(8,128)(2,1)S(1)}, u32[]{:S(2)}, u32[]{:S(2)}) collective-permute-start(bf16[2112,128]{1,0:T(8,128)(2,1)S(1)} %collective-permute-done.9.refs_13_.refs_7_), channel_id=1, source_target_pairs={{0,12},{1,13},{2,14},{3,15},{4,0},{5,1},{6,2},{7,3},{8,4},{9,5},{1... | collective-permute-start | bytes 1622024 | tf_op jit(solution)/shard_map/ppermute | solution.py:53
  66.7 3.6 %collective-permute-done.10.refs_12_.refs_6_ = bf16[2112,128]{1,0:T(8,128)(2,1)S(1)} collective-permute-done((bf16[2112,128]{1,0:T(8,128)(2,1)S(1)}, bf16[2112,128]{1,0:T(8,128)(2,1)S(1)}, u32[]{:S(2)}, u32[]{:S(2)}) %collective-permute-start.10) | collective-permute-done | bytes 540704 | tf_op jit(solution)/shard_map/ppermute | solution.py:53
  71.4 4.8 %collective-permute-done.14.refs_16_.refs_10_ = bf16[2112,128]{1,0:T(8,128)(2,1)S(1)} collective-permute-done((bf16[2112,128]{1,0:T(8,128)(2,1)S(1)}, bf16[2112,128]{1,0:T(8,128)(2,1)S(1)}, u32[]{:S(2)}, u32[]{:S(2)}) %collective-permute-start.14) | collective-permute-done | bytes 540704 | tf_op jit(solution)/shard_map/ppermute | solution.py:53
  83.4 7.2 %shard_map.134 = (bf16[2048,128]{1,0:T(8,128)(2,1)S(1)}, bf16[2048,128]{1,0:T(8,128)(2,1)S(1)}, bf16[2048,128]{1,0:T(8,128)(2,1)S(1)}) custom-call(s32[32,8]{1,0:T(8,128)S(1)} %get-tuple-element.62.refs_4_.slots, f32[32,8]{1,0:T(8,128)S(1)} %get-tuple-element.63.weights, bf16[128,128]{1,0:T(8,128)(2,1)S(1)} %copy-done.3, ...), custom_call_target="tpu_custom_call" | custom-call | flops 100000000 | bytes 1048576 | tf_op jit(solution)/shard_map/pallas_call | solution.py:339
  90.6 1.4 collective-permute-start.34
  92.0 2.7 %collective-permute-start.36 = (bf16[2048,128]{1,0:T(8,128)(2,1)S(1)}, bf16[2048,128]{1,0:T(8,128)(2,1)S(1)}, u32[]{:S(2)}, u32[]{:S(2)}) collective-permute-start(bf16[2048,128]{1,0:T(8,128)(2,1)S(1)} %get-tuple-element.77), channel_id=1, source_target_pairs={{0,96},{1,97},{2,98},{3,99},{4,100},{5,101},{6,102},{7,103},{8,104... | collective-permute-start | bytes 1572872 | tf_op jit(solution)/shard_map/ppermute | solution.py:53
  94.7 21.1 %shard_map.132 = (bf16[2048,128]{1,0:T(8,128)(2,1)S(1)}, bf16[2048,128]{1,0:T(8,128)(2,1)S(1)}, bf16[2048,128]{1,0:T(8,128)(2,1)S(1)}, s32[32,128]{1,0:T(8,128)S(1)}, f32[32,128]{1,0:T(8,128)S(1)}) custom-call(bf16[128,128]{1,0:T(8,128)(2,1)S(1)} %copy-done.3, bf16[256,256]{1,0:T(8,128)(2,1)S(1)} %get-tuple-element.64.right_ref, ...), custom_call_target="tpu_custom_call" | custom-call | flops 100000000 | bytes 1048576 | tf_op jit(solution)/shard_map/pallas_call | solution.py:371
  116.4 2.4 %collective-permute-start.39 = (bf16[2048,128]{1,0:T(8,128)(2,1)S(1)}, bf16[2048,128]{1,0:T(8,128)(2,1)S(1)}, u32[]{:S(2)}, u32[]{:S(2)}) collective-permute-start(bf16[2048,128]{1,0:T(8,128)(2,1)S(1)} %get-tuple-element.84), channel_id=1, source_target_pairs={{0,96},{1,97},{2,98},{3,99},{4,100},{5,101},{6,102},{7,103},{8,104... | collective-permute-start | bytes 1572872 | tf_op jit(solution)/shard_map/ppermute | solution.py:53
  118.8 9.7 %shard_map.133 = (f32[2048,128]{1,0:T(8,128)S(1)}, f32[2048,128]{1,0:T(8,128)S(1)}) custom-call(s32[32,8]{1,0:T(8,128)S(1)} %get-tuple-element.62.refs_4_.slots, f32[32,8]{1,0:T(8,128)S(1)} %get-tuple-element.63.weights, bf16[128,128]{1,0:T(8,128)(2,1)S(1)} %copy-done.3, bf16[256,256]{1,0:T(8,128)(2,1)S(1)} %get-tuple-element.64.right_ref, ...), custom_call_target="tpu_custom_call" | custom-call | flops 100000000 | bytes 1048576 | tf_op jit(solution)/shard_map/pallas_call | solution.py:383
  128.6 6.2 %shard_map.135 = (bf16[2048,128]{1,0:T(8,128)(2,1)S(1)}, f32[4,2,128,128]{3,2,1,0:T(8,128)S(1)}) custom-call(f32[8]{0:T(128)S(1)} %copy-done.6, bf16[2048,128]{1,0:T(8,128)(2,1)S(1)} %bitcast.34, f32[2048,128]{1,0:T(8,128)S(1)} %get-tuple-element.74.own_ref, bf16[2048,128]{1,0:T(8,128)(2,1)S(1)} %collective-permute-done.34.a_ref, ...), custom_call_target="tpu_custom_call" | custom-call | flops 100000000 | bytes 1048576 | tf_op jit(solution)/shard_map/pallas_call | solution.py:439
  134.8 7.5 %collective-permute-done.38.b_ref = bf16[2048,128]{1,0:T(8,128)(2,1)S(1)} collective-permute-done((bf16[2048,128]{1,0:T(8,128)(2,1)S(1)}, bf16[2048,128]{1,0:T(8,128)(2,1)S(1)}, u32[]{:S(2)}, u32[]{:S(2)}) %collective-permute-start.38) | collective-permute-done | bytes 524320 | tf_op jit(solution)/shard_map/ppermute | solution.py:53
  142.3 7.0 %shard_map.136 = (bf16[2048,128]{1,0:T(8,128)(2,1)}, f32[4,2,128,128]{3,2,1,0:T(8,128)S(1)}) custom-call(f32[8]{0:T(128)S(1)} %copy-done.6, bf16[2048,128]{1,0:T(8,128)(2,1)S(1)} %get-tuple-element.80.lam_ref, f32[2048,128]{1,0:T(8,128)S(1)} %get-tuple-element.81.own_ref, bf16[2048,128]{1,0:T(8,128)(2,1)S(1)} %collective-permute-done.37.a_ref, ...), custom_call_target="tpu_custom_call" | custom-call | flops 100000000 | bytes 1048576 | tf_op jit(solution)/shard_map/pallas_call | solution.py:439
  150.0 21.9 %all_to_all.5 = bf16[128,8,2,128]{3,2,1,0:T(2,128)(2,1)S(1)} all-to-all(bf16[128,8,2,128]{3,2,1,0:T(2,128)(2,1)S(1)} %copy.97), channel_id=1, replica_groups=mesh['y'=4,'c'=2,'z'=4,'x'=4] {'y','c','z','x'}, dimensions={0} | all-to-all | bytes 1048576 | tf_op jit(solution)/shard_map/all_to_all | solution.py:520
  (112 shorter events, 28.3 us)
Async XLA Ops:
  2.6 5.4 %collective-permute-start.2 = (f32[8,16]{1,0:T(8,128)S(1)}, f32[8,16]{1,0:T(8,128)S(1)}, u32[]{:S(2)}, u32[]{:S(2)}) collective-permute-start(f32[8,16]{1,0:T(8,128)S(1)} %pad.8), channel_id=1, source_target_pairs={{0,96},{1,97},{2,98},{3,99},{4,100},{5,101},{6,102},{7,103},{8,104... | collective-permute-start | bytes 1544 | tf_op jit(solution)/shard_map/ppermute | solution.py:53
  11.3 11.4 %collective-permute-start.4 = (bf16[2112,128]{1,0:T(8,128)(2,1)S(1)}, bf16[2112,128]{1,0:T(8,128)(2,1)S(1)}, u32[]{:S(2)}, u32[]{:S(2)}) collective-permute-start(bf16[2112,128]{1,0:T(8,128)(2,1)S(1)} %pad_maximum_fusion.refs_6_.refs_0_), channel_id=1, source_target_pairs={{0,16},{1,17},{2,18},{3,19},{4,20},{5,21},{6,22},{7,23},{8,24},{9,... | collective-permute-start | bytes 1622024 | tf_op jit(solution)/shard_map/ppermute | solution.py:53
  14.4 14.9 %collective-permute-start.3 = (bf16[2112,128]{1,0:T(8,128)(2,1)S(1)}, bf16[2112,128]{1,0:T(8,128)(2,1)S(1)}, u32[]{:S(2)}, u32[]{:S(2)}) collective-permute-start(bf16[2112,128]{1,0:T(8,128)(2,1)S(1)} %pad_maximum_fusion.refs_6_.refs_0_), channel_id=1, source_target_pairs={{0,1},{1,2},{2,3},{3,0},{4,5},{5,6},{6,7},{7,4},{8,9},{9,10},{10,1... | collective-permute-start | bytes 1622024 | tf_op jit(solution)/shard_map/ppermute | solution.py:53
  16.0 14.5 %collective-permute-start.5 = (bf16[2112,128]{1,0:T(8,128)(2,1)S(1)}, bf16[2112,128]{1,0:T(8,128)(2,1)S(1)}, u32[]{:S(2)}, u32[]{:S(2)}) collective-permute-start(bf16[2112,128]{1,0:T(8,128)(2,1)S(1)} %pad_maximum_fusion.refs_6_.refs_0_), channel_id=1, source_target_pairs={{0,4},{1,5},{2,6},{3,7},{4,8},{5,9},{6,10},{7,11},{8,12},{9,13},{1... | collective-permute-start | bytes 1622024 | tf_op jit(solution)/shard_map/ppermute | solution.py:53
  17.2 15.5 %collective-permute-start.7 = (bf16[2112,128]{1,0:T(8,128)(2,1)S(1)}, bf16[2112,128]{1,0:T(8,128)(2,1)S(1)}, u32[]{:S(2)}, u32[]{:S(2)}) collective-permute-start(bf16[2112,128]{1,0:T(8,128)(2,1)S(1)} %pad_maximum_fusion.refs_6_.refs_0_), channel_id=1, source_target_pairs={{0,12},{1,13},{2,14},{3,15},{4,0},{5,1},{6,2},{7,3},{8,4},{9,5},{1... | collective-permute-start | bytes 1622024 | tf_op jit(solution)/shard_map/ppermute | solution.py:53
  18.7 19.2 %collective-permute-start.11 = (bf16[2112,128]{1,0:T(8,128)(2,1)S(1)}, bf16[2112,128]{1,0:T(8,128)(2,1)S(1)}, u32[]{:S(2)}, u32[]{:S(2)}) collective-permute-start(bf16[2112,128]{1,0:T(8,128)(2,1)S(1)} %pad_maximum_fusion.refs_6_.refs_0_), channel_id=1, source_target_pairs={{0,2},{1,3},{2,0},{3,1},{4,6},{5,7},{6,4},{7,5},{8,10},{9,11},{10,... | collective-permute-start | bytes 1622024 | tf_op jit(solution)/shard_map/ppermute | solution.py:53
  22.7 16.3 %collective-permute-start.15 = (bf16[2112,128]{1,0:T(8,128)(2,1)S(1)}, bf16[2112,128]{1,0:T(8,128)(2,1)}, u32[]{:S(2)}, u32[]{:S(2)}) collective-permute-start(bf16[2112,128]{1,0:T(8,128)(2,1)S(1)} %pad_maximum_fusion.refs_6_.refs_0_), channel_id=1, source_target_pairs={{0,3},{1,0},{2,1},{3,2},{4,7},{5,4},{6,5},{7,6},{8,11},{9,8},{10,9... | collective-permute-start | bytes 1622024 | tf_op jit(solution)/shard_map/ppermute | solution.py:53
  30.5 12.4 %collective-permute-start.6 = (bf16[2112,128]{1,0:T(8,128)(2,1)S(1)}, bf16[2112,128]{1,0:T(8,128)(2,1)S(1)}, u32[]{:S(2)}, u32[]{:S(2)}) collective-permute-start(bf16[2112,128]{1,0:T(8,128)(2,1)S(1)} %collective-permute-done.5.refs_7_.refs_1_), channel_id=1, source_target_pairs={{0,4},{1,5},{2,6},{3,7},{4,8},{5,9},{6,10},{7,11},{8,12},{9,13},{1... | collective-permute-start | bytes 1622024 | tf_op jit(solution)/shard_map/ppermute | solution.py:53
  31.6 17.1 %collective-permute-start.8 = (bf16[2112,128]{1,0:T(8,128)(2,1)S(1)}, bf16[2112,128]{1,0:T(8,128)(2,1)S(1)}, u32[]{:S(2)}, u32[]{:S(2)}) collective-permute-start(bf16[2112,128]{1,0:T(8,128)(2,1)S(1)} %collective-permute-done.3.refs_10_.refs_4_), channel_id=1, source_target_pairs={{0,4},{1,5},{2,6},{3,7},{4,8},{5,9},{6,10},{7,11},{8,12},{9,13},{1... | collective-permute-start | bytes 1622024 | tf_op jit(solution)/shard_map/ppermute | solution.py:53
  32.8 16.3 %collective-permute-start.9 = (bf16[2112,128]{1,0:T(8,128)(2,1)S(1)}, bf16[2112,128]{1,0:T(8,128)(2,1)S(1)}, u32[]{:S(2)}, u32[]{:S(2)}) collective-permute-start(bf16[2112,128]{1,0:T(8,128)(2,1)S(1)} %collective-permute-done.3.refs_10_.refs_4_), channel_id=1, source_target_pairs={{0,12},{1,13},{2,14},{3,15},{4,0},{5,1},{6,2},{7,3},{8,4},{9,5},{1... | collective-permute-start | bytes 1622024 | tf_op jit(solution)/shard_map/ppermute | solution.py:53
  37.9 16.6 %collective-permute-start.12 = (bf16[2112,128]{1,0:T(8,128)(2,1)S(1)}, bf16[2112,128]{1,0:T(8,128)(2,1)S(1)}, u32[]{:S(2)}, u32[]{:S(2)}) collective-permute-start(bf16[2112,128]{1,0:T(8,128)(2,1)S(1)} %collective-permute-done.11.refs_14_.refs_8_), channel_id=1, source_target_pairs={{0,4},{1,5},{2,6},{3,7},{4,8},{5,9},{6,10},{7,11},{8,12},{9,13},{1... | collective-permute-start | bytes 1622024 | tf_op jit(solution)/shard_map/ppermute | solution.py:53
  39.0 16.8 %collective-permute-start.13 = (bf16[2112,128]{1,0:T(8,128)(2,1)S(1)}, bf16[2112,128]{1,0:T(8,128)(2,1)S(1)}, u32[]{:S(2)}, u32[]{:S(2)}) collective-permute-start(bf16[2112,128]{1,0:T(8,128)(2,1)S(1)} %collective-permute-done.11.refs_14_.refs_8_), channel_id=1, source_target_pairs={{0,12},{1,13},{2,14},{3,15},{4,0},{5,1},{6,2},{7,3},{8,4},{9,5},{1... | collective-permute-start | bytes 1622024 | tf_op jit(solution)/shard_map/ppermute | solution.py:53
  42.9 17.4 %collective-permute-start.16 = (bf16[2112,128]{1,0:T(8,128)(2,1)}, bf16[2112,128]{1,0:T(8,128)(2,1)S(1)}, u32[]{:S(2)}, u32[]{:S(2)}) collective-permute-start(bf16[2112,128]{1,0:T(8,128)(2,1)} %collective-permute-done.15.refs_18_.refs_12_), channel_id=1, source_target_pairs={{0,4},{1,5},{2,6},{3,7},{4,8},{5,9},{6,10},{7,11},{8,12},{9,13},{1... | collective-permute-start | bytes 1622024 | tf_op jit(solution)/shard_map/ppermute | solution.py:53
  48.7 12.8 %collective-permute-start.18 = (bf16[2112,128]{1,0:T(8,128)(2,1)}, bf16[2112,128]{1,0:T(8,128)(2,1)S(1)}, u32[]{:S(2)}, u32[]{:S(2)}) collective-permute-start(bf16[2112,128]{1,0:T(8,128)(2,1)} %collective-permute-done.15.refs_18_.refs_12_), channel_id=1, source_target_pairs={{0,12},{1,13},{2,14},{3,15},{4,0},{5,1},{6,2},{7,3},{8,4},{9,5},{1... | collective-permute-start | bytes 1622024 | tf_op jit(solution)/shard_map/ppermute | solution.py:53
  49.0 12.5 %collective-permute-start.19 = (bf16[2112,128]{1,0:T(8,128)(2,1)S(1)}, bf16[2112,128]{1,0:T(8,128)(2,1)S(1)}, u32[]{:S(2)}, u32[]{:S(2)}) collective-permute-start(bf16[2112,128]{1,0:T(8,128)(2,1)S(1)} %collective-permute-done.5.refs_7_.refs_1_), channel_id=1, source_target_pairs={{0,16},{1,17},{2,18},{3,19},{4,20},{5,21},{6,22},{7,23},{8,24},{9,... | collective-permute-start | bytes 1622024 | tf_op jit(solution)/shard_map/ppermute | solution.py:53
  54.5 9.5 %collective-permute-start.21 = (bf16[2112,128]{1,0:T(8,128)(2,1)S(1)}, bf16[2112,128]{1,0:T(8,128)(2,1)S(1)}, u32[]{:S(2)}, u32[]{:S(2)}) collective-permute-start(bf16[2112,128]{1,0:T(8,128)(2,1)S(1)} %collective-permute-done.7.refs_9_.refs_3_), channel_id=1, source_target_pairs={{0,16},{1,17},{2,18},{3,19},{4,20},{5,21},{6,22},{7,23},{8,24},{9,... | collective-permute-start | bytes 1622024 | tf_op jit(solution)/shard_map/ppermute | solution.py:53
  55.7 8.9 %collective-permute-start.22 = (bf16[2112,128]{1,0:T(8,128)(2,1)S(1)}, bf16[2112,128]{1,0:T(8,128)(2,1)S(1)}, u32[]{:S(2)}, u32[]{:S(2)}) collective-permute-start(bf16[2112,128]{1,0:T(8,128)(2,1)S(1)} %collective-permute-done.3.refs_10_.refs_4_), channel_id=1, source_target_pairs={{0,16},{1,17},{2,18},{3,19},{4,20},{5,21},{6,22},{7,23},{8,24},{9,... | collective-permute-start | bytes 1622024 | tf_op jit(solution)/shard_map/ppermute | solution.py:53
  60.3 5.2 %collective-permute-start.26 = (bf16[2112,128]{1,0:T(8,128)(2,1)S(1)}, bf16[2112,128]{1,0:T(8,128)(2,1)S(1)}, u32[]{:S(2)}, u32[]{:S(2)}) collective-permute-start(bf16[2112,128]{1,0:T(8,128)(2,1)S(1)} %collective-permute-done.11.refs_14_.refs_8_), channel_id=1, source_target_pairs={{0,16},{1,17},{2,18},{3,19},{4,20},{5,21},{6,22},{7,23},{8,24},{9,... | collective-permute-start | bytes 1622024 | tf_op jit(solution)/shard_map/ppermute | solution.py:53
  61.5 5.1 %collective-permute-start.30 = (bf16[2112,128]{1,0:T(8,128)(2,1)}, bf16[2112,128]{1,0:T(8,128)(2,1)S(1)}, u32[]{:S(2)}, u32[]{:S(2)}) collective-permute-start(bf16[2112,128]{1,0:T(8,128)(2,1)} %collective-permute-done.15.refs_18_.refs_12_), channel_id=1, source_target_pairs={{0,16},{1,17},{2,18},{3,19},{4,20},{5,21},{6,22},{7,23},{8,24},{9,... | collective-permute-start | bytes 1622024 | tf_op jit(solution)/shard_map/ppermute | solution.py:53
  61.5 8.8 %collective-permute-start.10 = (bf16[2112,128]{1,0:T(8,128)(2,1)S(1)}, bf16[2112,128]{1,0:T(8,128)(2,1)S(1)}, u32[]{:S(2)}, u32[]{:S(2)}) collective-permute-start(bf16[2112,128]{1,0:T(8,128)(2,1)S(1)} %collective-permute-done.9.refs_13_.refs_7_), channel_id=1, source_target_pairs={{0,12},{1,13},{2,14},{3,15},{4,0},{5,1},{6,2},{7,3},{8,4},{9,5},{1... | collective-permute-start | bytes 1622024 | tf_op jit(solution)/shard_map/ppermute | solution.py:53
  64.1 12.1 %collective-permute-start.14 = (bf16[2112,128]{1,0:T(8,128)(2,1)S(1)}, bf16[2112,128]{1,0:T(8,128)(2,1)S(1)}, u32[]{:S(2)}, u32[]{:S(2)}) collective-permute-start(bf16[2112,128]{1,0:T(8,128)(2,1)S(1)} %collective-permute-done.13.refs_17_.refs_11_), channel_id=1, source_target_pairs={{0,12},{1,13},{2,14},{3,15},{4,0},{5,1},{6,2},{7,3},{8,4},{9,5},{1... | collective-permute-start | bytes 1622024 | tf_op jit(solution)/shard_map/ppermute | solution.py:53
  64.6 12.6 %collective-permute-start.17 = (bf16[2112,128]{1,0:T(8,128)(2,1)S(1)}, bf16[2112,128]{1,0:T(8,128)(2,1)S(1)}, u32[]{:S(2)}, u32[]{:S(2)}) collective-permute-start(bf16[2112,128]{1,0:T(8,128)(2,1)S(1)} %collective-permute-done.16.refs_19_.refs_13_), channel_id=1, source_target_pairs={{0,4},{1,5},{2,6},{3,7},{4,8},{5,9},{6,10},{7,11},{8,12},{9,13},{1... | collective-permute-start | bytes 1622024 | tf_op jit(solution)/shard_map/ppermute | solution.py:53
  65.5 11.7 %collective-permute-start.20 = (bf16[2112,128]{1,0:T(8,128)(2,1)S(1)}, bf16[2112,128]{1,0:T(8,128)(2,1)S(1)}, u32[]{:S(2)}, u32[]{:S(2)}) collective-permute-start(bf16[2112,128]{1,0:T(8,128)(2,1)S(1)} %collective-permute-done.6.refs_8_.refs_2_), channel_id=1, source_target_pairs={{0,16},{1,17},{2,18},{3,19},{4,20},{5,21},{6,22},{7,23},{8,24},{9,... | collective-permute-start | bytes 1622024 | tf_op jit(solution)/shard_map/ppermute | solution.py:53
  66.6 11.1 %collective-permute-start.23 = (bf16[2112,128]{1,0:T(8,128)(2,1)S(1)}, bf16[2112,128]{1,0:T(8,128)(2,1)S(1)}, u32[]{:S(2)}, u32[]{:S(2)}) collective-permute-start(bf16[2112,128]{1,0:T(8,128)(2,1)S(1)} %collective-permute-done.8.refs_11_.refs_5_), channel_id=1, source_target_pairs={{0,16},{1,17},{2,18},{3,19},{4,20},{5,21},{6,22},{7,23},{8,24},{9,... | collective-permute-start | bytes 1622024 | tf_op jit(solution)/shard_map/ppermute | solution.py:53
  70.4 7.4 %collective-permute-start.25 = (bf16[2112,128]{1,0:T(8,128)(2,1)S(1)}, bf16[2112,128]{1,0:T(8,128)(2,1)S(1)}, u32[]{:S(2)}, u32[]{:S(2)}) collective-permute-start(bf16[2112,128]{1,0:T(8,128)(2,1)S(1)} %collective-permute-done.9.refs_13_.refs_7_), channel_id=1, source_target_pairs={{0,16},{1,17},{2,18},{3,19},{4,20},{5,21},{6,22},{7,23},{8,24},{9,... | collective-permute-start | bytes 1622024 | tf_op jit(solution)/shard_map/ppermute | solution.py:53
  77.8 4.0 %collective-permute-start.24 = (bf16[2112,128]{1,0:T(8,128)(2,1)S(1)}, bf16[2112,128]{1,0:T(8,128)(2,1)S(1)}, u32[]{:S(2)}, u32[]{:S(2)}) collective-permute-start(bf16[2112,128]{1,0:T(8,128)(2,1)S(1)} %collective-permute-done.10.refs_12_.refs_6_), channel_id=1, source_target_pairs={{0,16},{1,17},{2,18},{3,19},{4,20},{5,21},{6,22},{7,23},{8,24},{9,... | collective-permute-start | bytes 1622024 | tf_op jit(solution)/shard_map/ppermute | solution.py:53
  90.6 25.8 %collective-permute-start.34 = (bf16[2048,128]{1,0:T(8,128)(2,1)S(1)}, bf16[2048,128]{1,0:T(8,128)(2,1)S(1)}, u32[]{:S(2)}, u32[]{:S(2)}) collective-permute-start(bf16[2048,128]{1,0:T(8,128)(2,1)S(1)} %get-tuple-element.75), channel_id=1, source_target_pairs={{0,64},{1,65},{2,66},{3,67},{4,68},{5,69},{6,70},{7,71},{8,72},{9,... | collective-permute-start | bytes 1572872 | tf_op jit(solution)/shard_map/ppermute | solution.py:53
  92.0 36.5 %collective-permute-start.35 = (bf16[2048,128]{1,0:T(8,128)(2,1)S(1)}, bf16[2048,128]{1,0:T(8,128)(2,1)S(1)}, u32[]{:S(2)}, u32[]{:S(2)}) collective-permute-start(bf16[2048,128]{1,0:T(8,128)(2,1)S(1)} %get-tuple-element.76), channel_id=1, source_target_pairs={{0,32},{1,33},{2,34},{3,35},{4,36},{5,37},{6,38},{7,39},{8,40},{9,... | collective-permute-start | bytes 1572872 | tf_op jit(solution)/shard_map/ppermute | solution.py:53
  92.0 36.5 %collective-permute-start.36 = (bf16[2048,128]{1,0:T(8,128)(2,1)S(1)}, bf16[2048,128]{1,0:T(8,128)(2,1)S(1)}, u32[]{:S(2)}, u32[]{:S(2)}) collective-permute-start(bf16[2048,128]{1,0:T(8,128)(2,1)S(1)} %get-tuple-element.77), channel_id=1, source_target_pairs={{0,96},{1,97},{2,98},{3,99},{4,100},{5,101},{6,102},{7,103},{8,104... | collective-permute-start | bytes 1572872 | tf_op jit(solution)/shard_map/ppermute | solution.py:53
  115.8 19.0 %collective-permute-start.37 = (bf16[2048,128]{1,0:T(8,128)(2,1)S(1)}, bf16[2048,128]{1,0:T(8,128)(2,1)S(1)}, u32[]{:S(2)}, u32[]{:S(2)}) collective-permute-start(bf16[2048,128]{1,0:T(8,128)(2,1)S(1)} %get-tuple-element.82), channel_id=1, source_target_pairs={{0,64},{1,65},{2,66},{3,67},{4,68},{5,69},{6,70},{7,71},{8,72},{9,... | collective-permute-start | bytes 1572872 | tf_op jit(solution)/shard_map/ppermute | solution.py:53
  116.1 26.2 %collective-permute-start.38 = (bf16[2048,128]{1,0:T(8,128)(2,1)S(1)}, bf16[2048,128]{1,0:T(8,128)(2,1)S(1)}, u32[]{:S(2)}, u32[]{:S(2)}) collective-permute-start(bf16[2048,128]{1,0:T(8,128)(2,1)S(1)} %get-tuple-element.83), channel_id=1, source_target_pairs={{0,32},{1,33},{2,34},{3,35},{4,36},{5,37},{6,38},{7,39},{8,40},{9,... | collective-permute-start | bytes 1572872 | tf_op jit(solution)/shard_map/ppermute | solution.py:53
  116.4 26.0 %collective-permute-start.39 = (bf16[2048,128]{1,0:T(8,128)(2,1)S(1)}, bf16[2048,128]{1,0:T(8,128)(2,1)S(1)}, u32[]{:S(2)}, u32[]{:S(2)}) collective-permute-start(bf16[2048,128]{1,0:T(8,128)(2,1)S(1)} %get-tuple-element.84), channel_id=1, source_target_pairs={{0,96},{1,97},{2,98},{3,99},{4,100},{5,101},{6,102},{7,103},{8,104... | collective-permute-start | bytes 1572872 | tf_op jit(solution)/shard_map/ppermute | solution.py:53
  (21 other events, 217.3 us)

commit v5 on v4

--- a/solution.py
+++ b/solution.py
@@ -237,6 +237,15 @@
     far_sums(order, c_ref, right_ref, left_ref, outs, held, mains, code_v, weight_v, *rest)
 
 
+def more_kernel(order, c_ref, right_ref, left_ref, code_v, weight_v, *refs):
+    blocks, outs = refs[:32], refs[32 : 32 + len(order)]
+    held, main_sems, *rest = refs[32 + len(order) :]
+    mains = copies_of(blocks, held, main_sems, 0, BLOCK)
+    for copy in mains:
+        copy.start()
+    far_sums(order, c_ref, right_ref, left_ref, outs, held, mains, code_v, weight_v, *rest)
+
+
 def own_kernel(slots, weights, c_ref, right_ref, left_ref, code_v, weight_v, *refs):
     blocks, (far_out, near_out) = refs[:32], refs[32:34]
     held, main_sems, near_acc, near_lefts, near_rights, *rest = refs[34:]
@@ -379,6 +388,18 @@
     )(*arrays, *blocks)
 
 
+def more_parts(order, arrays, blocks):
+    return pl.pallas_call(
+        functools.partial(more_kernel, order),
+        out_shape=part_shapes(order),
+        in_specs=[VM] * len(arrays) + [FAR] * 32,
+        out_specs=[VM] * len(order),
+        scratch_shapes=held_scratch(BLOCK) + far_scratch(),
+        compiler_params=pltpu.CompilerParams(vmem_limit_bytes=30 << 20),
+        cost_estimate=pl.CostEstimate(flops=10**8, bytes_accessed=1 << 20, transcendentals=0),
+    )(*arrays, *blocks)
+
+
 def own_parts(scalars, arrays, blocks):
     return pl.pallas_call(
         own_kernel,
@@ -409,18 +430,17 @@
 
     def substep(u, _):
         right, left = right_ref[step * 4 + u], left_ref[step * 4 + u]
-        for h in range(OWN // 2):
-            mid = mm(wide[pl.ds(h * ROWS, ROWS), :], right).astype(BF)
-            turned = mm(left, stack_parts(mid)).astype(BF)
-            for k in range(2):
-                re, im = turned[:DIM, k * DIM : (k + 1) * DIM], turned[DIM:, k * DIM : (k + 1) * DIM]
-                j = 2 * h + k
-                wide[pl.ds(j * DIM, DIM), 0:DIM] = re
-                wide[pl.ds(j * DIM, DIM), DIM:ROWS] = im
-                tall[pl.ds(j * ROWS, DIM), 0:DIM] = re
-                tall[pl.ds(j * ROWS, DIM), DIM:ROWS] = im
-                tall[pl.ds(j * ROWS + DIM, DIM), 0:DIM] = im
-                tall[pl.ds(j * ROWS + DIM, DIM), DIM:ROWS] = -re
+        mid = mm(wide[...], right).astype(BF)
+        pairs_of = [stack_parts(mid[h * ROWS : (h + 1) * ROWS]) for h in range(OWN // 2)]
+        turned = mm(left, jnp.concatenate(pairs_of, axis=1)).astype(BF)
+        for j in range(OWN):
+            re, im = turned[:DIM, j * DIM : (j + 1) * DIM], turned[DIM:, j * DIM : (j + 1) * DIM]
+            wide[pl.ds(j * DIM, DIM), 0:DIM] = re
+            wide[pl.ds(j * DIM, DIM), DIM:ROWS] = im
+            tall[pl.ds(j * ROWS, DIM), 0:DIM] = re
+            tall[pl.ds(j * ROWS, DIM), DIM:ROWS] = im
+            tall[pl.ds(j * ROWS + DIM, DIM), 0:DIM] = im
+            tall[pl.ds(j * ROWS + DIM, DIM), DIM:ROWS] = -re
         saved_copy(u).wait()
         terms = lax.dot_general(
             saved_ref[u], tall[...], (((0,), (0,)), ((), ())), preferred_element_type=F32
@@ -508,7 +528,8 @@
     got_one = [send(p, along_y(s)) for p, s in ((one_2, 2), (one_1, 1), (one_3, 3))]
     whole = [coupling, whole_right, whole_left]
     small = [partner, rows, ladders, scale, slots, table]
-    two_2, two_1, two_3, *lists = far_parts((2, 1, 3), whole + small, blocks)
+    two_2, *lists = far_parts((2,), whole + small, blocks)
+    two_1, two_3 = more_parts((1, 3), whole + lists, blocks)
     got_two = [send(p, along_y(s)) for p, s in ((two_2, 2), (two_1, 1), (two_3, 3))]
     two_0, one_0 = own_parts([slots, weights], whole + lists, blocks)
     got_one, got_two = [one_0] + got_one, [two_0] + got_two

time: 173 us -> 171 us (0.988)
  waiting for transfers between devices: 41.5 us -> 37.4 us
    pallas_call x0 -> x1, Pallas kernels: none -> 11.4 us  [more_parts(): pl.pallas_call(functools.partial(more_kernel, order), out_shape=part_shap...]
    pallas_call x1, Pallas kernels: 21.1 us -> 11.3 us  [far_parts(): pl.pallas_call(functools.partial(far_kernel, order), out_shape=part_shape...]
    ppermute x40, waiting for transfers between devices: 41.5 us -> 37.4 us  [send(): return lax.ppermute(a, AXES, route)]
  transfers between devices with their start and end apart: 40 -> 40, of which waited for: 18 -> 18; matrix products, arithmetic and copies ran while one was open for 2% -> 2% of each run, Pallas kernels for 22% -> 23%
where the time goes in v5:
time: 171 us; the launch traced here: 170 us
  Pallas kernels  52.1 us (30%)
  starting transfers between devices  45.6 us (27%)
  waiting for transfers between devices  37.4 us (22%)
  blocking collectives  22.7 us (13%)
  local copies, waits for them, and re-layouts  6.01 us (4%)
  other arithmetic  5.75 us (3%)
    ppermute x40, starting transfers between devices, send(): return lax.ppermute(a, AXES, route)  45.6 us
    ppermute x40, waiting for transfers between devices, send(): return lax.ppermute(a, AXES, route)  37.4 us
    all_to_all x1, blocking collectives, body(): grad = lax.all_to_all(grad, AXES, 0, 0, tiled=True)  22.7 us
    pallas_call x2, Pallas kernels, chain(): pl.pallas_call(functools.partial(chain_kernel, step), out_shape=[jax.Shap...  11.6 us
    pallas_call x1, Pallas kernels, more_parts(): pl.pallas_call(functools.partial(more_kernel, order), out_shape=part_shap...  11.4 us
    pallas_call x1, Pallas kernels, far_parts(): pl.pallas_call(functools.partial(far_kernel, order), out_shape=part_shape...  11.3 us
    pallas_call x1, Pallas kernels, own_parts(): pl.pallas_call(own_kernel, out_shape=part_shapes((0, 0)), in_specs=[SM] *...  9.81 us
    pallas_call x1, Pallas kernels, near_parts(): pl.pallas_call(functools.partial(near_kernel, order), out_shape=part_shap...  7.15 us
  transfers between devices with their start and end apart: 40, of which 18 were waited for; matrix products, arithmetic and copies ran while one was open for 2% of the time, Pallas kernels for 23%

profile of v5, /device:TPU:1, one launch (start us, length us, event | category | flops | bytes accessed | tf_op | source)
XLA Modules:
  0.0 170.5 jit_solution(7175208554960471394)
XLA Ops:
  2.6 3.6 %collective-permute-start.2 = (f32[8,16]{1,0:T(8,128)S(1)}, f32[8,16]{1,0:T(8,128)S(1)}, u32[]{:S(2)}, u32[]{:S(2)}) collective-permute-start(f32[8,16]{1,0:T(8,128)S(1)} %pad.8), channel_id=1, source_target_pairs={{0,96},{1,97},{2,98},{3,99},{4,100},{5,101},{6,102},{7,103},{8,104... | collective-permute-start | bytes 1544 | tf_op jit(solution)/shard_map/ppermute | solution.py:53
  8.0 2.1 %collective-permute-done.1 = f32[8,16]{1,0:T(8,128)S(1)} collective-permute-done((f32[8,16]{1,0:T(8,128)S(1)}, f32[8,16]{1,0:T(8,128)S(1)}, u32[]{:S(2)}, u32[]{:S(2)}) %collective-permute-start.1) | collective-permute-done | bytes 544 | tf_op jit(solution)/shard_map/ppermute | solution.py:53
  11.3 2.5 %collective-permute-start.4 = (bf16[2112,128]{1,0:T(8,128)(2,1)S(1)}, bf16[2112,128]{1,0:T(8,128)(2,1)S(1)}, u32[]{:S(2)}, u32[]{:S(2)}) collective-permute-start(bf16[2112,128]{1,0:T(8,128)(2,1)S(1)} %pad_maximum_fusion.refs_6_.refs_0_), channel_id=1, source_target_pairs={{0,16},{1,17},{2,18},{3,19},{4,20},{5,21},{6,22},{7,23},{8,24},{9,... | collective-permute-start | bytes 1622024 | tf_op jit(solution)/shard_map/ppermute | solution.py:53
  14.4 1.6 collective-permute-start.3
  16.0 1.2 collective-permute-start.5
  17.2 1.5 collective-permute-start.7
  18.7 3.3 %collective-permute-start.11 = (bf16[2112,128]{1,0:T(8,128)(2,1)S(1)}, bf16[2112,128]{1,0:T(8,128)(2,1)S(1)}, u32[]{:S(2)}, u32[]{:S(2)}) collective-permute-start(bf16[2112,128]{1,0:T(8,128)(2,1)S(1)} %pad_maximum_fusion.refs_6_.refs_0_), channel_id=1, source_target_pairs={{0,2},{1,3},{2,0},{3,1},{4,6},{5,7},{6,4},{7,5},{8,10},{9,11},{10,... | collective-permute-start | bytes 1622024 | tf_op jit(solution)/shard_map/ppermute | solution.py:53
  29.2 1.3 collective-permute-done.5.refs_7_.refs_1_
  32.8 2.4 %collective-permute-start.9 = (bf16[2112,128]{1,0:T(8,128)(2,1)S(1)}, bf16[2112,128]{1,0:T(8,128)(2,1)S(1)}, u32[]{:S(2)}, u32[]{:S(2)}) collective-permute-start(bf16[2112,128]{1,0:T(8,128)(2,1)S(1)} %collective-permute-done.3.refs_10_.refs_4_), channel_id=1, source_target_pairs={{0,12},{1,13},{2,14},{3,15},{4,0},{5,1},{6,2},{7,3},{8,4},{9,5},{1... | collective-permute-start | bytes 1622024 | tf_op jit(solution)/shard_map/ppermute | solution.py:53
  35.1 2.8 %collective-permute-done.11.refs_14_.refs_8_ = bf16[2112,128]{1,0:T(8,128)(2,1)S(1)} collective-permute-done((bf16[2112,128]{1,0:T(8,128)(2,1)S(1)}, bf16[2112,128]{1,0:T(8,128)(2,1)S(1)}, u32[]{:S(2)}, u32[]{:S(2)}) %collective-permute-start.11) | collective-permute-done | bytes 540704 | tf_op jit(solution)/shard_map/ppermute | solution.py:53
  39.0 1.7 collective-permute-start.13
  40.6 2.3 %collective-permute-done.6.refs_8_.refs_2_ = bf16[2112,128]{1,0:T(8,128)(2,1)S(1)} collective-permute-done((bf16[2112,128]{1,0:T(8,128)(2,1)S(1)}, bf16[2112,128]{1,0:T(8,128)(2,1)S(1)}, u32[]{:S(2)}, u32[]{:S(2)}) %collective-permute-start.6) | collective-permute-done | bytes 540704 | tf_op jit(solution)/shard_map/ppermute | solution.py:53
  42.9 5.8 %collective-permute-done.8.refs_11_.refs_5_ = bf16[2112,128]{1,0:T(8,128)(2,1)S(1)} collective-permute-done((bf16[2112,128]{1,0:T(8,128)(2,1)S(1)}, bf16[2112,128]{1,0:T(8,128)(2,1)S(1)}, u32[]{:S(2)}, u32[]{:S(2)}) %collective-permute-start.8) | collective-permute-done | bytes 540704 | tf_op jit(solution)/shard_map/ppermute | solution.py:53
  49.0 3.4 %collective-permute-start.19 = (bf16[2112,128]{1,0:T(8,128)(2,1)S(1)}, bf16[2112,128]{1,0:T(8,128)(2,1)S(1)}, u32[]{:S(2)}, u32[]{:S(2)}) collective-permute-start(bf16[2112,128]{1,0:T(8,128)(2,1)S(1)} %collective-permute-done.5.refs_7_.refs_1_), channel_id=1, source_target_pairs={{0,16},{1,17},{2,18},{3,19},{4,20},{5,21},{6,22},{7,23},{8,24},{9,... | collective-permute-start | bytes 1622024 | tf_op jit(solution)/shard_map/ppermute | solution.py:53
  52.4 2.1 %collective-permute-done.12.refs_15_.refs_9_ = bf16[2112,128]{1,0:T(8,128)(2,1)S(1)} collective-permute-done((bf16[2112,128]{1,0:T(8,128)(2,1)S(1)}, bf16[2112,128]{1,0:T(8,128)(2,1)S(1)}, u32[]{:S(2)}, u32[]{:S(2)}) %collective-permute-start.12) | collective-permute-done | bytes 540704 | tf_op jit(solution)/shard_map/ppermute | solution.py:53
  54.5 1.2 collective-permute-start.21
  55.7 4.6 %collective-permute-done.16.refs_19_.refs_13_ = bf16[2112,128]{1,0:T(8,128)(2,1)S(1)} collective-permute-done((bf16[2112,128]{1,0:T(8,128)(2,1)}, bf16[2112,128]{1,0:T(8,128)(2,1)S(1)}, u32[]{:S(2)}, u32[]{:S(2)}) %collective-permute-start.16) | collective-permute-done | bytes 540704 | tf_op jit(solution)/shard_map/ppermute | solution.py:53
  60.3 1.2 collective-permute-start.26
  61.5 2.5 %collective-permute-start.10 = (bf16[2112,128]{1,0:T(8,128)(2,1)S(1)}, bf16[2112,128]{1,0:T(8,128)(2,1)S(1)}, u32[]{:S(2)}, u32[]{:S(2)}) collective-permute-start(bf16[2112,128]{1,0:T(8,128)(2,1)S(1)} %collective-permute-done.9.refs_13_.refs_7_), channel_id=1, source_target_pairs={{0,12},{1,13},{2,14},{3,15},{4,0},{5,1},{6,2},{7,3},{8,4},{9,5},{1... | collective-permute-start | bytes 1622024 | tf_op jit(solution)/shard_map/ppermute | solution.py:53
  66.7 3.6 %collective-permute-done.10.refs_12_.refs_6_ = bf16[2112,128]{1,0:T(8,128)(2,1)S(1)} collective-permute-done((bf16[2112,128]{1,0:T(8,128)(2,1)S(1)}, bf16[2112,128]{1,0:T(8,128)(2,1)S(1)}, u32[]{:S(2)}, u32[]{:S(2)}) %collective-permute-start.10) | collective-permute-done | bytes 540704 | tf_op jit(solution)/shard_map/ppermute | solution.py:53
  71.4 4.8 %collective-permute-done.14.refs_16_.refs_10_ = bf16[2112,128]{1,0:T(8,128)(2,1)S(1)} collective-permute-done((bf16[2112,128]{1,0:T(8,128)(2,1)S(1)}, bf16[2112,128]{1,0:T(8,128)(2,1)S(1)}, u32[]{:S(2)}, u32[]{:S(2)}) %collective-permute-start.14) | collective-permute-done | bytes 540704 | tf_op jit(solution)/shard_map/ppermute | solution.py:53
  83.4 7.2 %shard_map.134 = (bf16[2048,128]{1,0:T(8,128)(2,1)S(1)}, bf16[2048,128]{1,0:T(8,128)(2,1)S(1)}, bf16[2048,128]{1,0:T(8,128)(2,1)S(1)}) custom-call(s32[32,8]{1,0:T(8,128)S(1)} %get-tuple-element.62.refs_4_.slots, f32[32,8]{1,0:T(8,128)S(1)} %get-tuple-element.63.weights, bf16[128,128]{1,0:T(8,128)(2,1)S(1)} %copy-done.2, ...), custom_call_target="tpu_custom_call" | custom-call | flops 100000000 | bytes 1048576 | tf_op jit(solution)/shard_map/pallas_call | solution.py:348
  90.6 1.5 collective-permute-start.34
  92.0 2.7 %collective-permute-start.36 = (bf16[2048,128]{1,0:T(8,128)(2,1)S(1)}, bf16[2048,128]{1,0:T(8,128)(2,1)S(1)}, u32[]{:S(2)}, u32[]{:S(2)}) collective-permute-start(bf16[2048,128]{1,0:T(8,128)(2,1)S(1)} %get-tuple-element.77), channel_id=1, source_target_pairs={{0,96},{1,97},{2,98},{3,99},{4,100},{5,101},{6,102},{7,103},{8,104... | collective-permute-start | bytes 1572872 | tf_op jit(solution)/shard_map/ppermute | solution.py:53
  94.7 11.3 %shard_map.132 = (bf16[2048,128]{1,0:T(8,128)(2,1)S(1)}, s32[32,128]{1,0:T(8,128)S(1)}, f32[32,128]{1,0:T(8,128)S(1)}) custom-call(bf16[128,128]{1,0:T(8,128)(2,1)S(1)} %copy-done.2, bf16[256,256]{1,0:T(8,128)(2,1)S(1)} %get-tuple-element.64.right_ref, bf16[256,256]{1,0:T(8,128)(2,1)S(1)} %get-tuple-element.65.left_ref, ...), custom_call_target="tpu_custom_call" | custom-call | flops 100000000 | bytes 1048576 | tf_op jit(solution)/shard_map/pallas_call | solution.py:380
  106.9 11.4 %shard_map.136 = (bf16[2048,128]{1,0:T(8,128)(2,1)S(1)}, bf16[2048,128]{1,0:T(8,128)(2,1)S(1)}) custom-call(bf16[128,128]{1,0:T(8,128)(2,1)S(1)} %copy-done.2, bf16[256,256]{1,0:T(8,128)(2,1)S(1)} %get-tuple-element.64.right_ref, bf16[256,256]{1,0:T(8,128)(2,1)S(1)} %get-tuple-element.65.left_ref, s32[32,128]{1,0:T(8,128)S(1)} %get-tuple-element.72.code_v, ...), custom_call_target="tpu_custom_call" | custom-call | flops 100000000 | bytes 1048576 | tf_op jit(solution)/shard_map/pallas_call | solution.py:392
  118.6 2.4 %collective-permute-start.39 = (bf16[2048,128]{1,0:T(8,128)(2,1)S(1)}, bf16[2048,128]{1,0:T(8,128)(2,1)S(1)}, u32[]{:S(2)}, u32[]{:S(2)}) collective-permute-start(bf16[2048,128]{1,0:T(8,128)(2,1)S(1)} %get-tuple-element.84), channel_id=1, source_target_pairs={{0,96},{1,97},{2,98},{3,99},{4,100},{5,101},{6,102},{7,103},{8,104... | collective-permute-start | bytes 1572872 | tf_op jit(solution)/shard_map/ppermute | solution.py:53
  121.1 9.8 %shard_map.133 = (f32[2048,128]{1,0:T(8,128)S(1)}, f32[2048,128]{1,0:T(8,128)S(1)}) custom-call(s32[32,8]{1,0:T(8,128)S(1)} %get-tuple-element.62.refs_4_.slots, f32[32,8]{1,0:T(8,128)S(1)} %get-tuple-element.63.weights, bf16[128,128]{1,0:T(8,128)(2,1)S(1)} %copy-done.2, bf16[256,256]{1,0:T(8,128)(2,1)S(1)} %get-tuple-element.64.right_ref, ...), custom_call_target="tpu_custom_call" | custom-call | flops 100000000 | bytes 1048576 | tf_op jit(solution)/shard_map/pallas_call | solution.py:404
  130.9 5.4 %shard_map.135 = (bf16[2048,128]{1,0:T(8,128)(2,1)S(1)}, f32[4,2,128,128]{3,2,1,0:T(8,128)S(1)}) custom-call(f32[8]{0:T(128)S(1)} %copy-done.6, bf16[2048,128]{1,0:T(8,128)(2,1)S(1)} %bitcast.34, f32[2048,128]{1,0:T(8,128)S(1)} %get-tuple-element.74.own_ref, bf16[2048,128]{1,0:T(8,128)(2,1)S(1)} %collective-permute-done.34.a_ref, ...), custom_call_target="tpu_custom_call" | custom-call | flops 100000000 | bytes 1048576 | tf_op jit(solution)/shard_map/pallas_call | solution.py:459
  136.3 3.4 %collective-permute-done.38.b_ref = bf16[2048,128]{1,0:T(8,128)(2,1)S(1)} collective-permute-done((bf16[2048,128]{1,0:T(8,128)(2,1)S(1)}, bf16[2048,128]{1,0:T(8,128)(2,1)S(1)}, u32[]{:S(2)}, u32[]{:S(2)}) %collective-permute-start.38) | collective-permute-done | bytes 524320 | tf_op jit(solution)/shard_map/ppermute | solution.py:53
  139.7 6.2 %shard_map.137 = (bf16[2048,128]{1,0:T(8,128)(2,1)}, f32[4,2,128,128]{3,2,1,0:T(8,128)S(1)}) custom-call(f32[8]{0:T(128)S(1)} %copy-done.6, bf16[2048,128]{1,0:T(8,128)(2,1)S(1)} %get-tuple-element.80.lam_ref, f32[2048,128]{1,0:T(8,128)S(1)} %get-tuple-element.81.own_ref, bf16[2048,128]{1,0:T(8,128)(2,1)S(1)} %collective-permute-done.37.a_ref, ...), custom_call_target="tpu_custom_call" | custom-call | flops 100000000 | bytes 1048576 | tf_op jit(solution)/shard_map/pallas_call | solution.py:459
  146.6 22.7 %all_to_all.5 = bf16[128,8,2,128]{3,2,1,0:T(2,128)(2,1)S(1)} all-to-all(bf16[128,8,2,128]{3,2,1,0:T(2,128)(2,1)S(1)} %copy.97), channel_id=1, replica_groups=mesh['y'=4,'c'=2,'z'=4,'x'=4] {'y','c','z','x'}, dimensions={0} | all-to-all | bytes 1048576 | tf_op jit(solution)/shard_map/all_to_all | solution.py:541
  (113 shorter events, 30.1 us)
Async XLA Ops:
  2.6 5.4 %collective-permute-start.2 = (f32[8,16]{1,0:T(8,128)S(1)}, f32[8,16]{1,0:T(8,128)S(1)}, u32[]{:S(2)}, u32[]{:S(2)}) collective-permute-start(f32[8,16]{1,0:T(8,128)S(1)} %pad.8), channel_id=1, source_target_pairs={{0,96},{1,97},{2,98},{3,99},{4,100},{5,101},{6,102},{7,103},{8,104... | collective-permute-start | bytes 1544 | tf_op jit(solution)/shard_map/ppermute | solution.py:53
  11.3 11.4 %collective-permute-start.4 = (bf16[2112,128]{1,0:T(8,128)(2,1)S(1)}, bf16[2112,128]{1,0:T(8,128)(2,1)S(1)}, u32[]{:S(2)}, u32[]{:S(2)}) collective-permute-start(bf16[2112,128]{1,0:T(8,128)(2,1)S(1)} %pad_maximum_fusion.refs_6_.refs_0_), channel_id=1, source_target_pairs={{0,16},{1,17},{2,18},{3,19},{4,20},{5,21},{6,22},{7,23},{8,24},{9,... | collective-permute-start | bytes 1622024 | tf_op jit(solution)/shard_map/ppermute | solution.py:53
  14.4 14.9 %collective-permute-start.3 = (bf16[2112,128]{1,0:T(8,128)(2,1)S(1)}, bf16[2112,128]{1,0:T(8,128)(2,1)S(1)}, u32[]{:S(2)}, u32[]{:S(2)}) collective-permute-start(bf16[2112,128]{1,0:T(8,128)(2,1)S(1)} %pad_maximum_fusion.refs_6_.refs_0_), channel_id=1, source_target_pairs={{0,1},{1,2},{2,3},{3,0},{4,5},{5,6},{6,7},{7,4},{8,9},{9,10},{10,1... | collective-permute-start | bytes 1622024 | tf_op jit(solution)/shard_map/ppermute | solution.py:53
  16.0 14.5 %collective-permute-start.5 = (bf16[2112,128]{1,0:T(8,128)(2,1)S(1)}, bf16[2112,128]{1,0:T(8,128)(2,1)S(1)}, u32[]{:S(2)}, u32[]{:S(2)}) collective-permute-start(bf16[2112,128]{1,0:T(8,128)(2,1)S(1)} %pad_maximum_fusion.refs_6_.refs_0_), channel_id=1, source_target_pairs={{0,4},{1,5},{2,6},{3,7},{4,8},{5,9},{6,10},{7,11},{8,12},{9,13},{1... | collective-permute-start | bytes 1622024 | tf_op jit(solution)/shard_map/ppermute | solution.py:53
  17.2 15.5 %collective-permute-start.7 = (bf16[2112,128]{1,0:T(8,128)(2,1)S(1)}, bf16[2112,128]{1,0:T(8,128)(2,1)S(1)}, u32[]{:S(2)}, u32[]{:S(2)}) collective-permute-start(bf16[2112,128]{1,0:T(8,128)(2,1)S(1)} %pad_maximum_fusion.refs_6_.refs_0_), channel_id=1, source_target_pairs={{0,12},{1,13},{2,14},{3,15},{4,0},{5,1},{6,2},{7,3},{8,4},{9,5},{1... | collective-permute-start | bytes 1622024 | tf_op jit(solution)/shard_map/ppermute | solution.py:53
  18.7 19.2 %collective-permute-start.11 = (bf16[2112,128]{1,0:T(8,128)(2,1)S(1)}, bf16[2112,128]{1,0:T(8,128)(2,1)S(1)}, u32[]{:S(2)}, u32[]{:S(2)}) collective-permute-start(bf16[2112,128]{1,0:T(8,128)(2,1)S(1)} %pad_maximum_fusion.refs_6_.refs_0_), channel_id=1, source_target_pairs={{0,2},{1,3},{2,0},{3,1},{4,6},{5,7},{6,4},{7,5},{8,10},{9,11},{10,... | collective-permute-start | bytes 1622024 | tf_op jit(solution)/shard_map/ppermute | solution.py:53
  22.7 16.3 %collective-permute-start.15 = (bf16[2112,128]{1,0:T(8,128)(2,1)S(1)}, bf16[2112,128]{1,0:T(8,128)(2,1)}, u32[]{:S(2)}, u32[]{:S(2)}) collective-permute-start(bf16[2112,128]{1,0:T(8,128)(2,1)S(1)} %pad_maximum_fusion.refs_6_.refs_0_), channel_id=1, source_target_pairs={{0,3},{1,0},{2,1},{3,2},{4,7},{5,4},{6,5},{7,6},{8,11},{9,8},{10,9... | collective-permute-start | bytes 1622024 | tf_op jit(solution)/shard_map/ppermute | solution.py:53
  30.5 12.4 %collective-permute-start.6 = (bf16[2112,128]{1,0:T(8,128)(2,1)S(1)}, bf16[2112,128]{1,0:T(8,128)(2,1)S(1)}, u32[]{:S(2)}, u32[]{:S(2)}) collective-permute-start(bf16[2112,128]{1,0:T(8,128)(2,1)S(1)} %collective-permute-done.5.refs_7_.refs_1_), channel_id=1, source_target_pairs={{0,4},{1,5},{2,6},{3,7},{4,8},{5,9},{6,10},{7,11},{8,12},{9,13},{1... | collective-permute-start | bytes 1622024 | tf_op jit(solution)/shard_map/ppermute | solution.py:53
  31.6 17.1 %collective-permute-start.8 = (bf16[2112,128]{1,0:T(8,128)(2,1)S(1)}, bf16[2112,128]{1,0:T(8,128)(2,1)S(1)}, u32[]{:S(2)}, u32[]{:S(2)}) collective-permute-start(bf16[2112,128]{1,0:T(8,128)(2,1)S(1)} %collective-permute-done.3.refs_10_.refs_4_), channel_id=1, source_target_pairs={{0,4},{1,5},{2,6},{3,7},{4,8},{5,9},{6,10},{7,11},{8,12},{9,13},{1... | collective-permute-start | bytes 1622024 | tf_op jit(solution)/shard_map/ppermute | solution.py:53
  32.8 16.3 %collective-permute-start.9 = (bf16[2112,128]{1,0:T(8,128)(2,1)S(1)}, bf16[2112,128]{1,0:T(8,128)(2,1)S(1)}, u32[]{:S(2)}, u32[]{:S(2)}) collective-permute-start(bf16[2112,128]{1,0:T(8,128)(2,1)S(1)} %collective-permute-done.3.refs_10_.refs_4_), channel_id=1, source_target_pairs={{0,12},{1,13},{2,14},{3,15},{4,0},{5,1},{6,2},{7,3},{8,4},{9,5},{1... | collective-permute-start | bytes 1622024 | tf_op jit(solution)/shard_map/ppermute | solution.py:53
  37.9 16.6 %collective-permute-start.12 = (bf16[2112,128]{1,0:T(8,128)(2,1)S(1)}, bf16[2112,128]{1,0:T(8,128)(2,1)S(1)}, u32[]{:S(2)}, u32[]{:S(2)}) collective-permute-start(bf16[2112,128]{1,0:T(8,128)(2,1)S(1)} %collective-permute-done.11.refs_14_.refs_8_), channel_id=1, source_target_pairs={{0,4},{1,5},{2,6},{3,7},{4,8},{5,9},{6,10},{7,11},{8,12},{9,13},{1... | collective-permute-start | bytes 1622024 | tf_op jit(solution)/shard_map/ppermute | solution.py:53
  39.0 16.8 %collective-permute-start.13 = (bf16[2112,128]{1,0:T(8,128)(2,1)S(1)}, bf16[2112,128]{1,0:T(8,128)(2,1)S(1)}, u32[]{:S(2)}, u32[]{:S(2)}) collective-permute-start(bf16[2112,128]{1,0:T(8,128)(2,1)S(1)} %collective-permute-done.11.refs_14_.refs_8_), channel_id=1, source_target_pairs={{0,12},{1,13},{2,14},{3,15},{4,0},{5,1},{6,2},{7,3},{8,4},{9,5},{1... | collective-permute-start | bytes 1622024 | tf_op jit(solution)/shard_map/ppermute | solution.py:53
  42.9 17.4 %collective-permute-start.16 = (bf16[2112,128]{1,0:T(8,128)(2,1)}, bf16[2112,128]{1,0:T(8,128)(2,1)S(1)}, u32[]{:S(2)}, u32[]{:S(2)}) collective-permute-start(bf16[2112,128]{1,0:T(8,128)(2,1)} %collective-permute-done.15.refs_18_.refs_12_), channel_id=1, source_target_pairs={{0,4},{1,5},{2,6},{3,7},{4,8},{5,9},{6,10},{7,11},{8,12},{9,13},{1... | collective-permute-start | bytes 1622024 | tf_op jit(solution)/shard_map/ppermute | solution.py:53
  48.7 12.8 %collective-permute-start.18 = (bf16[2112,128]{1,0:T(8,128)(2,1)}, bf16[2112,128]{1,0:T(8,128)(2,1)S(1)}, u32[]{:S(2)}, u32[]{:S(2)}) collective-permute-start(bf16[2112,128]{1,0:T(8,128)(2,1)} %collective-permute-done.15.refs_18_.refs_12_), channel_id=1, source_target_pairs={{0,12},{1,13},{2,14},{3,15},{4,0},{5,1},{6,2},{7,3},{8,4},{9,5},{1... | collective-permute-start | bytes 1622024 | tf_op jit(solution)/shard_map/ppermute | solution.py:53
  49.0 12.5 %collective-permute-start.19 = (bf16[2112,128]{1,0:T(8,128)(2,1)S(1)}, bf16[2112,128]{1,0:T(8,128)(2,1)S(1)}, u32[]{:S(2)}, u32[]{:S(2)}) collective-permute-start(bf16[2112,128]{1,0:T(8,128)(2,1)S(1)} %collective-permute-done.5.refs_7_.refs_1_), channel_id=1, source_target_pairs={{0,16},{1,17},{2,18},{3,19},{4,20},{5,21},{6,22},{7,23},{8,24},{9,... | collective-permute-start | bytes 1622024 | tf_op jit(solution)/shard_map/ppermute | solution.py:53
  54.5 9.5 %collective-permute-start.21 = (bf16[2112,128]{1,0:T(8,128)(2,1)S(1)}, bf16[2112,128]{1,0:T(8,128)(2,1)S(1)}, u32[]{:S(2)}, u32[]{:S(2)}) collective-permute-start(bf16[2112,128]{1,0:T(8,128)(2,1)S(1)} %collective-permute-done.7.refs_9_.refs_3_), channel_id=1, source_target_pairs={{0,16},{1,17},{2,18},{3,19},{4,20},{5,21},{6,22},{7,23},{8,24},{9,... | collective-permute-start | bytes 1622024 | tf_op jit(solution)/shard_map/ppermute | solution.py:53
  55.7 8.9 %collective-permute-start.22 = (bf16[2112,128]{1,0:T(8,128)(2,1)S(1)}, bf16[2112,128]{1,0:T(8,128)(2,1)S(1)}, u32[]{:S(2)}, u32[]{:S(2)}) collective-permute-start(bf16[2112,128]{1,0:T(8,128)(2,1)S(1)} %collective-permute-done.3.refs_10_.refs_4_), channel_id=1, source_target_pairs={{0,16},{1,17},{2,18},{3,19},{4,20},{5,21},{6,22},{7,23},{8,24},{9,... | collective-permute-start | bytes 1622024 | tf_op jit(solution)/shard_map/ppermute | solution.py:53
  60.3 5.2 %collective-permute-start.26 = (bf16[2112,128]{1,0:T(8,128)(2,1)S(1)}, bf16[2112,128]{1,0:T(8,128)(2,1)S(1)}, u32[]{:S(2)}, u32[]{:S(2)}) collective-permute-start(bf16[2112,128]{1,0:T(8,128)(2,1)S(1)} %collective-permute-done.11.refs_14_.refs_8_), channel_id=1, source_target_pairs={{0,16},{1,17},{2,18},{3,19},{4,20},{5,21},{6,22},{7,23},{8,24},{9,... | collective-permute-start | bytes 1622024 | tf_op jit(solution)/shard_map/ppermute | solution.py:53
  61.5 5.1 %collective-permute-start.30 = (bf16[2112,128]{1,0:T(8,128)(2,1)}, bf16[2112,128]{1,0:T(8,128)(2,1)S(1)}, u32[]{:S(2)}, u32[]{:S(2)}) collective-permute-start(bf16[2112,128]{1,0:T(8,128)(2,1)} %collective-permute-done.15.refs_18_.refs_12_), channel_id=1, source_target_pairs={{0,16},{1,17},{2,18},{3,19},{4,20},{5,21},{6,22},{7,23},{8,24},{9,... | collective-permute-start | bytes 1622024 | tf_op jit(solution)/shard_map/ppermute | solution.py:53
  61.5 8.8 %collective-permute-start.10 = (bf16[2112,128]{1,0:T(8,128)(2,1)S(1)}, bf16[2112,128]{1,0:T(8,128)(2,1)S(1)}, u32[]{:S(2)}, u32[]{:S(2)}) collective-permute-start(bf16[2112,128]{1,0:T(8,128)(2,1)S(1)} %collective-permute-done.9.refs_13_.refs_7_), channel_id=1, source_target_pairs={{0,12},{1,13},{2,14},{3,15},{4,0},{5,1},{6,2},{7,3},{8,4},{9,5},{1... | collective-permute-start | bytes 1622024 | tf_op jit(solution)/shard_map/ppermute | solution.py:53
  64.1 12.1 %collective-permute-start.14 = (bf16[2112,128]{1,0:T(8,128)(2,1)S(1)}, bf16[2112,128]{1,0:T(8,128)(2,1)S(1)}, u32[]{:S(2)}, u32[]{:S(2)}) collective-permute-start(bf16[2112,128]{1,0:T(8,128)(2,1)S(1)} %collective-permute-done.13.refs_17_.refs_11_), channel_id=1, source_target_pairs={{0,12},{1,13},{2,14},{3,15},{4,0},{5,1},{6,2},{7,3},{8,4},{9,5},{1... | collective-permute-start | bytes 1622024 | tf_op jit(solution)/shard_map/ppermute | solution.py:53
  64.6 12.6 %collective-permute-start.17 = (bf16[2112,128]{1,0:T(8,128)(2,1)S(1)}, bf16[2112,128]{1,0:T(8,128)(2,1)S(1)}, u32[]{:S(2)}, u32[]{:S(2)}) collective-permute-start(bf16[2112,128]{1,0:T(8,128)(2,1)S(1)} %collective-permute-done.16.refs_19_.refs_13_), channel_id=1, source_target_pairs={{0,4},{1,5},{2,6},{3,7},{4,8},{5,9},{6,10},{7,11},{8,12},{9,13},{1... | collective-permute-start | bytes 1622024 | tf_op jit(solution)/shard_map/ppermute | solution.py:53
  65.5 11.7 %collective-permute-start.20 = (bf16[2112,128]{1,0:T(8,128)(2,1)S(1)}, bf16[2112,128]{1,0:T(8,128)(2,1)S(1)}, u32[]{:S(2)}, u32[]{:S(2)}) collective-permute-start(bf16[2112,128]{1,0:T(8,128)(2,1)S(1)} %collective-permute-done.6.refs_8_.refs_2_), channel_id=1, source_target_pairs={{0,16},{1,17},{2,18},{3,19},{4,20},{5,21},{6,22},{7,23},{8,24},{9,... | collective-permute-start | bytes 1622024 | tf_op jit(solution)/shard_map/ppermute | solution.py:53
  66.6 11.1 %collective-permute-start.23 = (bf16[2112,128]{1,0:T(8,128)(2,1)S(1)}, bf16[2112,128]{1,0:T(8,128)(2,1)S(1)}, u32[]{:S(2)}, u32[]{:S(2)}) collective-permute-start(bf16[2112,128]{1,0:T(8,128)(2,1)S(1)} %collective-permute-done.8.refs_11_.refs_5_), channel_id=1, source_target_pairs={{0,16},{1,17},{2,18},{3,19},{4,20},{5,21},{6,22},{7,23},{8,24},{9,... | collective-permute-start | bytes 1622024 | tf_op jit(solution)/shard_map/ppermute | solution.py:53
  70.4 7.4 %collective-permute-start.25 = (bf16[2112,128]{1,0:T(8,128)(2,1)S(1)}, bf16[2112,128]{1,0:T(8,128)(2,1)S(1)}, u32[]{:S(2)}, u32[]{:S(2)}) collective-permute-start(bf16[2112,128]{1,0:T(8,128)(2,1)S(1)} %collective-permute-done.9.refs_13_.refs_7_), channel_id=1, source_target_pairs={{0,16},{1,17},{2,18},{3,19},{4,20},{5,21},{6,22},{7,23},{8,24},{9,... | collective-permute-start | bytes 1622024 | tf_op jit(solution)/shard_map/ppermute | solution.py:53
  77.8 4.0 %collective-permute-start.24 = (bf16[2112,128]{1,0:T(8,128)(2,1)S(1)}, bf16[2112,128]{1,0:T(8,128)(2,1)S(1)}, u32[]{:S(2)}, u32[]{:S(2)}) collective-permute-start(bf16[2112,128]{1,0:T(8,128)(2,1)S(1)} %collective-permute-done.10.refs_12_.refs_6_), channel_id=1, source_target_pairs={{0,16},{1,17},{2,18},{3,19},{4,20},{5,21},{6,22},{7,23},{8,24},{9,... | collective-permute-start | bytes 1622024 | tf_op jit(solution)/shard_map/ppermute | solution.py:53
  90.6 28.1 %collective-permute-start.34 = (bf16[2048,128]{1,0:T(8,128)(2,1)S(1)}, bf16[2048,128]{1,0:T(8,128)(2,1)S(1)}, u32[]{:S(2)}, u32[]{:S(2)}) collective-permute-start(bf16[2048,128]{1,0:T(8,128)(2,1)S(1)} %get-tuple-element.75), channel_id=1, source_target_pairs={{0,64},{1,65},{2,66},{3,67},{4,68},{5,69},{6,70},{7,71},{8,72},{9,... | collective-permute-start | bytes 1572872 | tf_op jit(solution)/shard_map/ppermute | solution.py:53
  92.0 38.8 %collective-permute-start.35 = (bf16[2048,128]{1,0:T(8,128)(2,1)S(1)}, bf16[2048,128]{1,0:T(8,128)(2,1)S(1)}, u32[]{:S(2)}, u32[]{:S(2)}) collective-permute-start(bf16[2048,128]{1,0:T(8,128)(2,1)S(1)} %get-tuple-element.76), channel_id=1, source_target_pairs={{0,32},{1,33},{2,34},{3,35},{4,36},{5,37},{6,38},{7,39},{8,40},{9,... | collective-permute-start | bytes 1572872 | tf_op jit(solution)/shard_map/ppermute | solution.py:53
  92.0 38.8 %collective-permute-start.36 = (bf16[2048,128]{1,0:T(8,128)(2,1)S(1)}, bf16[2048,128]{1,0:T(8,128)(2,1)S(1)}, u32[]{:S(2)}, u32[]{:S(2)}) collective-permute-start(bf16[2048,128]{1,0:T(8,128)(2,1)S(1)} %get-tuple-element.77), channel_id=1, source_target_pairs={{0,96},{1,97},{2,98},{3,99},{4,100},{5,101},{6,102},{7,103},{8,104... | collective-permute-start | bytes 1572872 | tf_op jit(solution)/shard_map/ppermute | solution.py:53
  106.0 30.3 %collective-permute-start.37 = (bf16[2048,128]{1,0:T(8,128)(2,1)S(1)}, bf16[2048,128]{1,0:T(8,128)(2,1)S(1)}, u32[]{:S(2)}, u32[]{:S(2)}) collective-permute-start(bf16[2048,128]{1,0:T(8,128)(2,1)S(1)} %get-tuple-element.82), channel_id=1, source_target_pairs={{0,64},{1,65},{2,66},{3,67},{4,68},{5,69},{6,70},{7,71},{8,72},{9,... | collective-permute-start | bytes 1572872 | tf_op jit(solution)/shard_map/ppermute | solution.py:53
  118.3 21.4 %collective-permute-start.38 = (bf16[2048,128]{1,0:T(8,128)(2,1)S(1)}, bf16[2048,128]{1,0:T(8,128)(2,1)S(1)}, u32[]{:S(2)}, u32[]{:S(2)}) collective-permute-start(bf16[2048,128]{1,0:T(8,128)(2,1)S(1)} %get-tuple-element.83), channel_id=1, source_target_pairs={{0,32},{1,33},{2,34},{3,35},{4,36},{5,37},{6,38},{7,39},{8,40},{9,... | collective-permute-start | bytes 1572872 | tf_op jit(solution)/shard_map/ppermute | solution.py:53
  118.6 21.1 %collective-permute-start.39 = (bf16[2048,128]{1,0:T(8,128)(2,1)S(1)}, bf16[2048,128]{1,0:T(8,128)(2,1)S(1)}, u32[]{:S(2)}, u32[]{:S(2)}) collective-permute-start(bf16[2048,128]{1,0:T(8,128)(2,1)S(1)} %get-tuple-element.84), channel_id=1, source_target_pairs={{0,96},{1,97},{2,98},{3,99},{4,100},{5,101},{6,102},{7,103},{8,104... | collective-permute-start | bytes 1572872 | tf_op jit(solution)/shard_map/ppermute | solution.py:53
  (21 other events, 222.4 us)

commit v6 on v5

--- a/solution.py
+++ b/solution.py
@@ -280,14 +280,14 @@
                     acc[k] = jnp.zeros((ROWS, DIM), F32)
 
                 def add(e, _):
-                    for n in (2 * e, 2 * e + 1):
+                    for n in (4 * e, 4 * e + 1, 4 * e + 2, 4 * e + 3):
                         code, weight = code_s[d, n], weight_s[d, n]
                         start = pl.multiple_of((code & 255) * ROWS, ROWS)
                         kind = code >> 8
                         acc[kind] = acc[kind] + weight * held[pl.ds(start, ROWS), :].astype(F32)
                     return 0
 
-                lax.fori_loop(0, (code_s[d, DIM - 1] + 1) >> 1, add, 0)
+                lax.fori_loop(0, (code_s[d, DIM - 1] + 3) >> 2, add, 0)
                 kept[g, 0] = acc[4] + acc[5]
                 kept[g, 1] = acc[4] - acc[5]
                 at = pl.multiple_of(g * ROWS, ROWS)

time: 171 us -> 171 us (level)
  transfers between devices with their start and end apart: 40 -> 40, of which waited for: 18 -> 18; matrix products, arithmetic and copies ran while one was open for 2% -> 2% of each run, Pallas kernels for 23% -> 22%
where the time goes in v6:
time: 171 us
  Pallas kernels  51.3 us (30%)
  starting transfers between devices  45.1 us (26%)
  waiting for transfers between devices  38.6 us (23%)
  blocking collectives  22.9 us (13%)
  local copies, waits for them, and re-layouts  6.01 us (4%)
  other arithmetic  5.75 us (3%)
    ppermute x40, starting transfers between devices, send(): return lax.ppermute(a, AXES, route)  45.1 us
    ppermute x40, waiting for transfers between devices, send(): return lax.ppermute(a, AXES, route)  38.6 us
    all_to_all x1, blocking collectives, body(): grad = lax.all_to_all(grad, AXES, 0, 0, tiled=True)  22.9 us
    pallas_call x1, Pallas kernels, far_parts(): pl.pallas_call(functools.partial(far_kernel, order), out_shape=part_shape...  11.6 us
    pallas_call x2, Pallas kernels, chain(): pl.pallas_call(functools.partial(chain_kernel, step), out_shape=[jax.Shap...  11.6 us
    pallas_call x1, Pallas kernels, more_parts(): pl.pallas_call(functools.partial(more_kernel, order), out_shape=part_shap...  11 us
    pallas_call x1, Pallas kernels, own_parts(): pl.pallas_call(own_kernel, out_shape=part_shapes((0, 0)), in_specs=[SM] *...  9.06 us
    pallas_call x1, Pallas kernels, near_parts(): pl.pallas_call(functools.partial(near_kernel, order), out_shape=part_shap...  7.15 us
  transfers between devices with their start and end apart: 40, of which 18 were waited for; matrix products, arithmetic and copies ran while one was open for 2% of the time, Pallas kernels for 22%

profile of v6, /device:TPU:1, one launch (start us, length us, event | category | flops | bytes accessed | tf_op | source)
XLA Modules:
  0.0 170.6 jit_solution(12571761437027677206)
XLA Ops:
  2.6 3.6 %collective-permute-start.2 = (f32[8,16]{1,0:T(8,128)S(1)}, f32[8,16]{1,0:T(8,128)S(1)}, u32[]{:S(2)}, u32[]{:S(2)}) collective-permute-start(f32[8,16]{1,0:T(8,128)S(1)} %pad.8), channel_id=1, source_target_pairs={{0,96},{1,97},{2,98},{3,99},{4,100},{5,101},{6,102},{7,103},{8,104... | collective-permute-start | bytes 1544 | tf_op jit(solution)/shard_map/ppermute | solution.py:53
  8.0 2.1 %collective-permute-done.1 = f32[8,16]{1,0:T(8,128)S(1)} collective-permute-done((f32[8,16]{1,0:T(8,128)S(1)}, f32[8,16]{1,0:T(8,128)S(1)}, u32[]{:S(2)}, u32[]{:S(2)}) %collective-permute-start.1) | collective-permute-done | bytes 544 | tf_op jit(solution)/shard_map/ppermute | solution.py:53
  11.3 2.5 %collective-permute-start.4 = (bf16[2112,128]{1,0:T(8,128)(2,1)S(1)}, bf16[2112,128]{1,0:T(8,128)(2,1)S(1)}, u32[]{:S(2)}, u32[]{:S(2)}) collective-permute-start(bf16[2112,128]{1,0:T(8,128)(2,1)S(1)} %pad_maximum_fusion.refs_6_.refs_0_), channel_id=1, source_target_pairs={{0,16},{1,17},{2,18},{3,19},{4,20},{5,21},{6,22},{7,23},{8,24},{9,... | collective-permute-start | bytes 1622024 | tf_op jit(solution)/shard_map/ppermute | solution.py:53
  14.4 1.6 collective-permute-start.3
  16.0 1.2 collective-permute-start.5
  17.2 1.5 collective-permute-start.7
  18.7 3.3 %collective-permute-start.11 = (bf16[2112,128]{1,0:T(8,128)(2,1)S(1)}, bf16[2112,128]{1,0:T(8,128)(2,1)S(1)}, u32[]{:S(2)}, u32[]{:S(2)}) collective-permute-start(bf16[2112,128]{1,0:T(8,128)(2,1)S(1)} %pad_maximum_fusion.refs_6_.refs_0_), channel_id=1, source_target_pairs={{0,2},{1,3},{2,0},{3,1},{4,6},{5,7},{6,4},{7,5},{8,10},{9,11},{10,... | collective-permute-start | bytes 1622024 | tf_op jit(solution)/shard_map/ppermute | solution.py:53
  29.2 1.3 collective-permute-done.5.refs_7_.refs_1_
  32.8 2.4 %collective-permute-start.9 = (bf16[2112,128]{1,0:T(8,128)(2,1)S(1)}, bf16[2112,128]{1,0:T(8,128)(2,1)S(1)}, u32[]{:S(2)}, u32[]{:S(2)}) collective-permute-start(bf16[2112,128]{1,0:T(8,128)(2,1)S(1)} %collective-permute-done.3.refs_10_.refs_4_), channel_id=1, source_target_pairs={{0,12},{1,13},{2,14},{3,15},{4,0},{5,1},{6,2},{7,3},{8,4},{9,5},{1... | collective-permute-start | bytes 1622024 | tf_op jit(solution)/shard_map/ppermute | solution.py:53
  35.1 2.8 %collective-permute-done.11.refs_14_.refs_8_ = bf16[2112,128]{1,0:T(8,128)(2,1)S(1)} collective-permute-done((bf16[2112,128]{1,0:T(8,128)(2,1)S(1)}, bf16[2112,128]{1,0:T(8,128)(2,1)S(1)}, u32[]{:S(2)}, u32[]{:S(2)}) %collective-permute-start.11) | collective-permute-done | bytes 540704 | tf_op jit(solution)/shard_map/ppermute | solution.py:53
  39.0 1.7 collective-permute-start.13
  40.6 2.3 %collective-permute-done.6.refs_8_.refs_2_ = bf16[2112,128]{1,0:T(8,128)(2,1)S(1)} collective-permute-done((bf16[2112,128]{1,0:T(8,128)(2,1)S(1)}, bf16[2112,128]{1,0:T(8,128)(2,1)S(1)}, u32[]{:S(2)}, u32[]{:S(2)}) %collective-permute-start.6) | collective-permute-done | bytes 540704 | tf_op jit(solution)/shard_map/ppermute | solution.py:53
  42.9 5.8 %collective-permute-done.8.refs_11_.refs_5_ = bf16[2112,128]{1,0:T(8,128)(2,1)S(1)} collective-permute-done((bf16[2112,128]{1,0:T(8,128)(2,1)S(1)}, bf16[2112,128]{1,0:T(8,128)(2,1)S(1)}, u32[]{:S(2)}, u32[]{:S(2)}) %collective-permute-start.8) | collective-permute-done | bytes 540704 | tf_op jit(solution)/shard_map/ppermute | solution.py:53
  49.0 3.4 %collective-permute-start.19 = (bf16[2112,128]{1,0:T(8,128)(2,1)S(1)}, bf16[2112,128]{1,0:T(8,128)(2,1)S(1)}, u32[]{:S(2)}, u32[]{:S(2)}) collective-permute-start(bf16[2112,128]{1,0:T(8,128)(2,1)S(1)} %collective-permute-done.5.refs_7_.refs_1_), channel_id=1, source_target_pairs={{0,16},{1,17},{2,18},{3,19},{4,20},{5,21},{6,22},{7,23},{8,24},{9,... | collective-permute-start | bytes 1622024 | tf_op jit(solution)/shard_map/ppermute | solution.py:53
  52.4 2.1 %collective-permute-done.12.refs_15_.refs_9_ = bf16[2112,128]{1,0:T(8,128)(2,1)S(1)} collective-permute-done((bf16[2112,128]{1,0:T(8,128)(2,1)S(1)}, bf16[2112,128]{1,0:T(8,128)(2,1)S(1)}, u32[]{:S(2)}, u32[]{:S(2)}) %collective-permute-start.12) | collective-permute-done | bytes 540704 | tf_op jit(solution)/shard_map/ppermute | solution.py:53
  54.5 1.2 collective-permute-start.21
  55.7 4.6 %collective-permute-done.16.refs_19_.refs_13_ = bf16[2112,128]{1,0:T(8,128)(2,1)S(1)} collective-permute-done((bf16[2112,128]{1,0:T(8,128)(2,1)}, bf16[2112,128]{1,0:T(8,128)(2,1)S(1)}, u32[]{:S(2)}, u32[]{:S(2)}) %collective-permute-start.16) | collective-permute-done | bytes 540704 | tf_op jit(solution)/shard_map/ppermute | solution.py:53
  60.3 1.2 collective-permute-start.26
  61.5 2.5 %collective-permute-start.10 = (bf16[2112,128]{1,0:T(8,128)(2,1)S(1)}, bf16[2112,128]{1,0:T(8,128)(2,1)S(1)}, u32[]{:S(2)}, u32[]{:S(2)}) collective-permute-start(bf16[2112,128]{1,0:T(8,128)(2,1)S(1)} %collective-permute-done.9.refs_13_.refs_7_), channel_id=1, source_target_pairs={{0,12},{1,13},{2,14},{3,15},{4,0},{5,1},{6,2},{7,3},{8,4},{9,5},{1... | collective-permute-start | bytes 1622024 | tf_op jit(solution)/shard_map/ppermute | solution.py:53
  66.7 3.6 %collective-permute-done.10.refs_12_.refs_6_ = bf16[2112,128]{1,0:T(8,128)(2,1)S(1)} collective-permute-done((bf16[2112,128]{1,0:T(8,128)(2,1)S(1)}, bf16[2112,128]{1,0:T(8,128)(2,1)S(1)}, u32[]{:S(2)}, u32[]{:S(2)}) %collective-permute-start.10) | collective-permute-done | bytes 540704 | tf_op jit(solution)/shard_map/ppermute | solution.py:53
  71.4 4.8 %collective-permute-done.14.refs_16_.refs_10_ = bf16[2112,128]{1,0:T(8,128)(2,1)S(1)} collective-permute-done((bf16[2112,128]{1,0:T(8,128)(2,1)S(1)}, bf16[2112,128]{1,0:T(8,128)(2,1)S(1)}, u32[]{:S(2)}, u32[]{:S(2)}) %collective-permute-start.14) | collective-permute-done | bytes 540704 | tf_op jit(solution)/shard_map/ppermute | solution.py:53
  83.4 7.2 %shard_map.134 = (bf16[2048,128]{1,0:T(8,128)(2,1)S(1)}, bf16[2048,128]{1,0:T(8,128)(2,1)S(1)}, bf16[2048,128]{1,0:T(8,128)(2,1)S(1)}) custom-call(s32[32,8]{1,0:T(8,128)S(1)} %get-tuple-element.62.refs_4_.slots, f32[32,8]{1,0:T(8,128)S(1)} %get-tuple-element.63.weights, bf16[128,128]{1,0:T(8,128)(2,1)S(1)} %copy-done.2, ...), custom_call_target="tpu_custom_call" | custom-call | flops 100000000 | bytes 1048576 | tf_op jit(solution)/shard_map/pallas_call | solution.py:348
  90.6 1.6 collective-permute-start.34
  92.1 2.7 %collective-permute-start.36 = (bf16[2048,128]{1,0:T(8,128)(2,1)S(1)}, bf16[2048,128]{1,0:T(8,128)(2,1)S(1)}, u32[]{:S(2)}, u32[]{:S(2)}) collective-permute-start(bf16[2048,128]{1,0:T(8,128)(2,1)S(1)} %get-tuple-element.77), channel_id=1, source_target_pairs={{0,96},{1,97},{2,98},{3,99},{4,100},{5,101},{6,102},{7,103},{8,104... | collective-permute-start | bytes 1572872 | tf_op jit(solution)/shard_map/ppermute | solution.py:53
  94.8 11.6 %shard_map.132 = (bf16[2048,128]{1,0:T(8,128)(2,1)S(1)}, s32[32,128]{1,0:T(8,128)S(1)}, f32[32,128]{1,0:T(8,128)S(1)}) custom-call(bf16[128,128]{1,0:T(8,128)(2,1)S(1)} %copy-done.2, bf16[256,256]{1,0:T(8,128)(2,1)S(1)} %get-tuple-element.64.right_ref, bf16[256,256]{1,0:T(8,128)(2,1)S(1)} %get-tuple-element.65.left_ref, ...), custom_call_target="tpu_custom_call" | custom-call | flops 100000000 | bytes 1048576 | tf_op jit(solution)/shard_map/pallas_call | solution.py:380
  106.7 11.0 %shard_map.136 = (bf16[2048,128]{1,0:T(8,128)(2,1)S(1)}, bf16[2048,128]{1,0:T(8,128)(2,1)S(1)}) custom-call(bf16[128,128]{1,0:T(8,128)(2,1)S(1)} %copy-done.2, bf16[256,256]{1,0:T(8,128)(2,1)S(1)} %get-tuple-element.64.right_ref, bf16[256,256]{1,0:T(8,128)(2,1)S(1)} %get-tuple-element.65.left_ref, s32[32,128]{1,0:T(8,128)S(1)} %get-tuple-element.72.code_v, ...), custom_call_target="tpu_custom_call" | custom-call | flops 100000000 | bytes 1048576 | tf_op jit(solution)/shard_map/pallas_call | solution.py:392
  118.5 2.0 %collective-permute-start.39 = (bf16[2048,128]{1,0:T(8,128)(2,1)S(1)}, bf16[2048,128]{1,0:T(8,128)(2,1)S(1)}, u32[]{:S(2)}, u32[]{:S(2)}) collective-permute-start(bf16[2048,128]{1,0:T(8,128)(2,1)S(1)} %get-tuple-element.84), channel_id=1, source_target_pairs={{0,96},{1,97},{2,98},{3,99},{4,100},{5,101},{6,102},{7,103},{8,104... | collective-permute-start | bytes 1572872 | tf_op jit(solution)/shard_map/ppermute | solution.py:53
  120.5 9.1 %shard_map.133 = (f32[2048,128]{1,0:T(8,128)S(1)}, f32[2048,128]{1,0:T(8,128)S(1)}) custom-call(s32[32,8]{1,0:T(8,128)S(1)} %get-tuple-element.62.refs_4_.slots, f32[32,8]{1,0:T(8,128)S(1)} %get-tuple-element.63.weights, bf16[128,128]{1,0:T(8,128)(2,1)S(1)} %copy-done.2, bf16[256,256]{1,0:T(8,128)(2,1)S(1)} %get-tuple-element.64.right_ref, ...), custom_call_target="tpu_custom_call" | custom-call | flops 100000000 | bytes 1048576 | tf_op jit(solution)/shard_map/pallas_call | solution.py:404
  129.6 5.4 %shard_map.135 = (bf16[2048,128]{1,0:T(8,128)(2,1)S(1)}, f32[4,2,128,128]{3,2,1,0:T(8,128)S(1)}) custom-call(f32[8]{0:T(128)S(1)} %copy-done.6, bf16[2048,128]{1,0:T(8,128)(2,1)S(1)} %bitcast.34, f32[2048,128]{1,0:T(8,128)S(1)} %get-tuple-element.74.own_ref, bf16[2048,128]{1,0:T(8,128)(2,1)S(1)} %collective-permute-done.34.a_ref, ...), custom_call_target="tpu_custom_call" | custom-call | flops 100000000 | bytes 1048576 | tf_op jit(solution)/shard_map/pallas_call | solution.py:459
  135.1 4.7 %collective-permute-done.38.b_ref = bf16[2048,128]{1,0:T(8,128)(2,1)S(1)} collective-permute-done((bf16[2048,128]{1,0:T(8,128)(2,1)S(1)}, bf16[2048,128]{1,0:T(8,128)(2,1)S(1)}, u32[]{:S(2)}, u32[]{:S(2)}) %collective-permute-start.38) | collective-permute-done | bytes 524320 | tf_op jit(solution)/shard_map/ppermute | solution.py:53
  139.7 6.2 %shard_map.137 = (bf16[2048,128]{1,0:T(8,128)(2,1)}, f32[4,2,128,128]{3,2,1,0:T(8,128)S(1)}) custom-call(f32[8]{0:T(128)S(1)} %copy-done.6, bf16[2048,128]{1,0:T(8,128)(2,1)S(1)} %get-tuple-element.80.lam_ref, f32[2048,128]{1,0:T(8,128)S(1)} %get-tuple-element.81.own_ref, bf16[2048,128]{1,0:T(8,128)(2,1)S(1)} %collective-permute-done.37.a_ref, ...), custom_call_target="tpu_custom_call" | custom-call | flops 100000000 | bytes 1048576 | tf_op jit(solution)/shard_map/pallas_call | solution.py:459
  146.6 22.9 %all_to_all.5 = bf16[128,8,2,128]{3,2,1,0:T(2,128)(2,1)S(1)} all-to-all(bf16[128,8,2,128]{3,2,1,0:T(2,128)(2,1)S(1)} %copy.97), channel_id=1, replica_groups=mesh['y'=4,'c'=2,'z'=4,'x'=4] {'y','c','z','x'}, dimensions={0} | all-to-all | bytes 1048576 | tf_op jit(solution)/shard_map/all_to_all | solution.py:541
  (113 shorter events, 30.0 us)
Async XLA Ops:
  2.6 5.4 %collective-permute-start.2 = (f32[8,16]{1,0:T(8,128)S(1)}, f32[8,16]{1,0:T(8,128)S(1)}, u32[]{:S(2)}, u32[]{:S(2)}) collective-permute-start(f32[8,16]{1,0:T(8,128)S(1)} %pad.8), channel_id=1, source_target_pairs={{0,96},{1,97},{2,98},{3,99},{4,100},{5,101},{6,102},{7,103},{8,104... | collective-permute-start | bytes 1544 | tf_op jit(solution)/shard_map/ppermute | solution.py:53
  11.3 11.4 %collective-permute-start.4 = (bf16[2112,128]{1,0:T(8,128)(2,1)S(1)}, bf16[2112,128]{1,0:T(8,128)(2,1)S(1)}, u32[]{:S(2)}, u32[]{:S(2)}) collective-permute-start(bf16[2112,128]{1,0:T(8,128)(2,1)S(1)} %pad_maximum_fusion.refs_6_.refs_0_), channel_id=1, source_target_pairs={{0,16},{1,17},{2,18},{3,19},{4,20},{5,21},{6,22},{7,23},{8,24},{9,... | collective-permute-start | bytes 1622024 | tf_op jit(solution)/shard_map/ppermute | solution.py:53
  14.4 14.9 %collective-permute-start.3 = (bf16[2112,128]{1,0:T(8,128)(2,1)S(1)}, bf16[2112,128]{1,0:T(8,128)(2,1)S(1)}, u32[]{:S(2)}, u32[]{:S(2)}) collective-permute-start(bf16[2112,128]{1,0:T(8,128)(2,1)S(1)} %pad_maximum_fusion.refs_6_.refs_0_), channel_id=1, source_target_pairs={{0,1},{1,2},{2,3},{3,0},{4,5},{5,6},{6,7},{7,4},{8,9},{9,10},{10,1... | collective-permute-start | bytes 1622024 | tf_op jit(solution)/shard_map/ppermute | solution.py:53
  16.0 14.5 %collective-permute-start.5 = (bf16[2112,128]{1,0:T(8,128)(2,1)S(1)}, bf16[2112,128]{1,0:T(8,128)(2,1)S(1)}, u32[]{:S(2)}, u32[]{:S(2)}) collective-permute-start(bf16[2112,128]{1,0:T(8,128)(2,1)S(1)} %pad_maximum_fusion.refs_6_.refs_0_), channel_id=1, source_target_pairs={{0,4},{1,5},{2,6},{3,7},{4,8},{5,9},{6,10},{7,11},{8,12},{9,13},{1... | collective-permute-start | bytes 1622024 | tf_op jit(solution)/shard_map/ppermute | solution.py:53
  17.2 15.5 %collective-permute-start.7 = (bf16[2112,128]{1,0:T(8,128)(2,1)S(1)}, bf16[2112,128]{1,0:T(8,128)(2,1)S(1)}, u32[]{:S(2)}, u32[]{:S(2)}) collective-permute-start(bf16[2112,128]{1,0:T(8,128)(2,1)S(1)} %pad_maximum_fusion.refs_6_.refs_0_), channel_id=1, source_target_pairs={{0,12},{1,13},{2,14},{3,15},{4,0},{5,1},{6,2},{7,3},{8,4},{9,5},{1... | collective-permute-start | bytes 1622024 | tf_op jit(solution)/shard_map/ppermute | solution.py:53
  18.7 19.2 %collective-permute-start.11 = (bf16[2112,128]{1,0:T(8,128)(2,1)S(1)}, bf16[2112,128]{1,0:T(8,128)(2,1)S(1)}, u32[]{:S(2)}, u32[]{:S(2)}) collective-permute-start(bf16[2112,128]{1,0:T(8,128)(2,1)S(1)} %pad_maximum_fusion.refs_6_.refs_0_), channel_id=1, source_target_pairs={{0,2},{1,3},{2,0},{3,1},{4,6},{5,7},{6,4},{7,5},{8,10},{9,11},{10,... | collective-permute-start | bytes 1622024 | tf_op jit(solution)/shard_map/ppermute | solution.py:53
  22.7 16.3 %collective-permute-start.15 = (bf16[2112,128]{1,0:T(8,128)(2,1)S(1)}, bf16[2112,128]{1,0:T(8,128)(2,1)}, u32[]{:S(2)}, u32[]{:S(2)}) collective-permute-start(bf16[2112,128]{1,0:T(8,128)(2,1)S(1)} %pad_maximum_fusion.refs_6_.refs_0_), channel_id=1, source_target_pairs={{0,3},{1,0},{2,1},{3,2},{4,7},{5,4},{6,5},{7,6},{8,11},{9,8},{10,9... | collective-permute-start | bytes 1622024 | tf_op jit(solution)/shard_map/ppermute | solution.py:53
  30.5 12.4 %collective-permute-start.6 = (bf16[2112,128]{1,0:T(8,128)(2,1)S(1)}, bf16[2112,128]{1,0:T(8,128)(2,1)S(1)}, u32[]{:S(2)}, u32[]{:S(2)}) collective-permute-start(bf16[2112,128]{1,0:T(8,128)(2,1)S(1)} %collective-permute-done.5.refs_7_.refs_1_), channel_id=1, source_target_pairs={{0,4},{1,5},{2,6},{3,7},{4,8},{5,9},{6,10},{7,11},{8,12},{9,13},{1... | collective-permute-start | bytes 1622024 | tf_op jit(solution)/shard_map/ppermute | solution.py:53
  31.6 17.1 %collective-permute-start.8 = (bf16[2112,128]{1,0:T(8,128)(2,1)S(1)}, bf16[2112,128]{1,0:T(8,128)(2,1)S(1)}, u32[]{:S(2)}, u32[]{:S(2)}) collective-permute-start(bf16[2112,128]{1,0:T(8,128)(2,1)S(1)} %collective-permute-done.3.refs_10_.refs_4_), channel_id=1, source_target_pairs={{0,4},{1,5},{2,6},{3,7},{4,8},{5,9},{6,10},{7,11},{8,12},{9,13},{1... | collective-permute-start | bytes 1622024 | tf_op jit(solution)/shard_map/ppermute | solution.py:53
  32.8 16.3 %collective-permute-start.9 = (bf16[2112,128]{1,0:T(8,128)(2,1)S(1)}, bf16[2112,128]{1,0:T(8,128)(2,1)S(1)}, u32[]{:S(2)}, u32[]{:S(2)}) collective-permute-start(bf16[2112,128]{1,0:T(8,128)(2,1)S(1)} %collective-permute-done.3.refs_10_.refs_4_), channel_id=1, source_target_pairs={{0,12},{1,13},{2,14},{3,15},{4,0},{5,1},{6,2},{7,3},{8,4},{9,5},{1... | collective-permute-start | bytes 1622024 | tf_op jit(solution)/shard_map/ppermute | solution.py:53
  37.9 16.6 %collective-permute-start.12 = (bf16[2112,128]{1,0:T(8,128)(2,1)S(1)}, bf16[2112,128]{1,0:T(8,128)(2,1)S(1)}, u32[]{:S(2)}, u32[]{:S(2)}) collective-permute-start(bf16[2112,128]{1,0:T(8,128)(2,1)S(1)} %collective-permute-done.11.refs_14_.refs_8_), channel_id=1, source_target_pairs={{0,4},{1,5},{2,6},{3,7},{4,8},{5,9},{6,10},{7,11},{8,12},{9,13},{1... | collective-permute-start | bytes 1622024 | tf_op jit(solution)/shard_map/ppermute | solution.py:53
  39.0 16.8 %collective-permute-start.13 = (bf16[2112,128]{1,0:T(8,128)(2,1)S(1)}, bf16[2112,128]{1,0:T(8,128)(2,1)S(1)}, u32[]{:S(2)}, u32[]{:S(2)}) collective-permute-start(bf16[2112,128]{1,0:T(8,128)(2,1)S(1)} %collective-permute-done.11.refs_14_.refs_8_), channel_id=1, source_target_pairs={{0,12},{1,13},{2,14},{3,15},{4,0},{5,1},{6,2},{7,3},{8,4},{9,5},{1... | collective-permute-start | bytes 1622024 | tf_op jit(solution)/shard_map/ppermute | solution.py:53
  42.9 17.4 %collective-permute-start.16 = (bf16[2112,128]{1,0:T(8,128)(2,1)}, bf16[2112,128]{1,0:T(8,128)(2,1)S(1)}, u32[]{:S(2)}, u32[]{:S(2)}) collective-permute-start(bf16[2112,128]{1,0:T(8,128)(2,1)} %collective-permute-done.15.refs_18_.refs_12_), channel_id=1, source_target_pairs={{0,4},{1,5},{2,6},{3,7},{4,8},{5,9},{6,10},{7,11},{8,12},{9,13},{1... | collective-permute-start | bytes 1622024 | tf_op jit(solution)/shard_map/ppermute | solution.py:53
  48.7 12.8 %collective-permute-start.18 = (bf16[2112,128]{1,0:T(8,128)(2,1)}, bf16[2112,128]{1,0:T(8,128)(2,1)S(1)}, u32[]{:S(2)}, u32[]{:S(2)}) collective-permute-start(bf16[2112,128]{1,0:T(8,128)(2,1)} %collective-permute-done.15.refs_18_.refs_12_), channel_id=1, source_target_pairs={{0,12},{1,13},{2,14},{3,15},{4,0},{5,1},{6,2},{7,3},{8,4},{9,5},{1... | collective-permute-start | bytes 1622024 | tf_op jit(solution)/shard_map/ppermute | solution.py:53
  49.0 12.5 %collective-permute-start.19 = (bf16[2112,128]{1,0:T(8,128)(2,1)S(1)}, bf16[2112,128]{1,0:T(8,128)(2,1)S(1)}, u32[]{:S(2)}, u32[]{:S(2)}) collective-permute-start(bf16[2112,128]{1,0:T(8,128)(2,1)S(1)} %collective-permute-done.5.refs_7_.refs_1_), channel_id=1, source_target_pairs={{0,16},{1,17},{2,18},{3,19},{4,20},{5,21},{6,22},{7,23},{8,24},{9,... | collective-permute-start | bytes 1622024 | tf_op jit(solution)/shard_map/ppermute | solution.py:53
  54.5 9.5 %collective-permute-start.21 = (bf16[2112,128]{1,0:T(8,128)(2,1)S(1)}, bf16[2112,128]{1,0:T(8,128)(2,1)S(1)}, u32[]{:S(2)}, u32[]{:S(2)}) collective-permute-start(bf16[2112,128]{1,0:T(8,128)(2,1)S(1)} %collective-permute-done.7.refs_9_.refs_3_), channel_id=1, source_target_pairs={{0,16},{1,17},{2,18},{3,19},{4,20},{5,21},{6,22},{7,23},{8,24},{9,... | collective-permute-start | bytes 1622024 | tf_op jit(solution)/shard_map/ppermute | solution.py:53
  55.7 8.9 %collective-permute-start.22 = (bf16[2112,128]{1,0:T(8,128)(2,1)S(1)}, bf16[2112,128]{1,0:T(8,128)(2,1)S(1)}, u32[]{:S(2)}, u32[]{:S(2)}) collective-permute-start(bf16[2112,128]{1,0:T(8,128)(2,1)S(1)} %collective-permute-done.3.refs_10_.refs_4_), channel_id=1, source_target_pairs={{0,16},{1,17},{2,18},{3,19},{4,20},{5,21},{6,22},{7,23},{8,24},{9,... | collective-permute-start | bytes 1622024 | tf_op jit(solution)/shard_map/ppermute | solution.py:53
  60.3 5.2 %collective-permute-start.26 = (bf16[2112,128]{1,0:T(8,128)(2,1)S(1)}, bf16[2112,128]{1,0:T(8,128)(2,1)S(1)}, u32[]{:S(2)}, u32[]{:S(2)}) collective-permute-start(bf16[2112,128]{1,0:T(8,128)(2,1)S(1)} %collective-permute-done.11.refs_14_.refs_8_), channel_id=1, source_target_pairs={{0,16},{1,17},{2,18},{3,19},{4,20},{5,21},{6,22},{7,23},{8,24},{9,... | collective-permute-start | bytes 1622024 | tf_op jit(solution)/shard_map/ppermute | solution.py:53
  61.5 5.1 %collective-permute-start.30 = (bf16[2112,128]{1,0:T(8,128)(2,1)}, bf16[2112,128]{1,0:T(8,128)(2,1)S(1)}, u32[]{:S(2)}, u32[]{:S(2)}) collective-permute-start(bf16[2112,128]{1,0:T(8,128)(2,1)} %collective-permute-done.15.refs_18_.refs_12_), channel_id=1, source_target_pairs={{0,16},{1,17},{2,18},{3,19},{4,20},{5,21},{6,22},{7,23},{8,24},{9,... | collective-permute-start | bytes 1622024 | tf_op jit(solution)/shard_map/ppermute | solution.py:53
  61.5 8.8 %collective-permute-start.10 = (bf16[2112,128]{1,0:T(8,128)(2,1)S(1)}, bf16[2112,128]{1,0:T(8,128)(2,1)S(1)}, u32[]{:S(2)}, u32[]{:S(2)}) collective-permute-start(bf16[2112,128]{1,0:T(8,128)(2,1)S(1)} %collective-permute-done.9.refs_13_.refs_7_), channel_id=1, source_target_pairs={{0,12},{1,13},{2,14},{3,15},{4,0},{5,1},{6,2},{7,3},{8,4},{9,5},{1... | collective-permute-start | bytes 1622024 | tf_op jit(solution)/shard_map/ppermute | solution.py:53
  64.1 12.1 %collective-permute-start.14 = (bf16[2112,128]{1,0:T(8,128)(2,1)S(1)}, bf16[2112,128]{1,0:T(8,128)(2,1)S(1)}, u32[]{:S(2)}, u32[]{:S(2)}) collective-permute-start(bf16[2112,128]{1,0:T(8,128)(2,1)S(1)} %collective-permute-done.13.refs_17_.refs_11_), channel_id=1, source_target_pairs={{0,12},{1,13},{2,14},{3,15},{4,0},{5,1},{6,2},{7,3},{8,4},{9,5},{1... | collective-permute-start | bytes 1622024 | tf_op jit(solution)/shard_map/ppermute | solution.py:53
  64.6 12.6 %collective-permute-start.17 = (bf16[2112,128]{1,0:T(8,128)(2,1)S(1)}, bf16[2112,128]{1,0:T(8,128)(2,1)S(1)}, u32[]{:S(2)}, u32[]{:S(2)}) collective-permute-start(bf16[2112,128]{1,0:T(8,128)(2,1)S(1)} %collective-permute-done.16.refs_19_.refs_13_), channel_id=1, source_target_pairs={{0,4},{1,5},{2,6},{3,7},{4,8},{5,9},{6,10},{7,11},{8,12},{9,13},{1... | collective-permute-start | bytes 1622024 | tf_op jit(solution)/shard_map/ppermute | solution.py:53
  65.5 11.7 %collective-permute-start.20 = (bf16[2112,128]{1,0:T(8,128)(2,1)S(1)}, bf16[2112,128]{1,0:T(8,128)(2,1)S(1)}, u32[]{:S(2)}, u32[]{:S(2)}) collective-permute-start(bf16[2112,128]{1,0:T(8,128)(2,1)S(1)} %collective-permute-done.6.refs_8_.refs_2_), channel_id=1, source_target_pairs={{0,16},{1,17},{2,18},{3,19},{4,20},{5,21},{6,22},{7,23},{8,24},{9,... | collective-permute-start | bytes 1622024 | tf_op jit(solution)/shard_map/ppermute | solution.py:53
  66.6 11.1 %collective-permute-start.23 = (bf16[2112,128]{1,0:T(8,128)(2,1)S(1)}, bf16[2112,128]{1,0:T(8,128)(2,1)S(1)}, u32[]{:S(2)}, u32[]{:S(2)}) collective-permute-start(bf16[2112,128]{1,0:T(8,128)(2,1)S(1)} %collective-permute-done.8.refs_11_.refs_5_), channel_id=1, source_target_pairs={{0,16},{1,17},{2,18},{3,19},{4,20},{5,21},{6,22},{7,23},{8,24},{9,... | collective-permute-start | bytes 1622024 | tf_op jit(solution)/shard_map/ppermute | solution.py:53
  70.4 7.4 %collective-permute-start.25 = (bf16[2112,128]{1,0:T(8,128)(2,1)S(1)}, bf16[2112,128]{1,0:T(8,128)(2,1)S(1)}, u32[]{:S(2)}, u32[]{:S(2)}) collective-permute-start(bf16[2112,128]{1,0:T(8,128)(2,1)S(1)} %collective-permute-done.9.refs_13_.refs_7_), channel_id=1, source_target_pairs={{0,16},{1,17},{2,18},{3,19},{4,20},{5,21},{6,22},{7,23},{8,24},{9,... | collective-permute-start | bytes 1622024 | tf_op jit(solution)/shard_map/ppermute | solution.py:53
  77.8 4.0 %collective-permute-start.24 = (bf16[2112,128]{1,0:T(8,128)(2,1)S(1)}, bf16[2112,128]{1,0:T(8,128)(2,1)S(1)}, u32[]{:S(2)}, u32[]{:S(2)}) collective-permute-start(bf16[2112,128]{1,0:T(8,128)(2,1)S(1)} %collective-permute-done.10.refs_12_.refs_6_), channel_id=1, source_target_pairs={{0,16},{1,17},{2,18},{3,19},{4,20},{5,21},{6,22},{7,23},{8,24},{9,... | collective-permute-start | bytes 1622024 | tf_op jit(solution)/shard_map/ppermute | solution.py:53
  90.6 27.9 %collective-permute-start.34 = (bf16[2048,128]{1,0:T(8,128)(2,1)S(1)}, bf16[2048,128]{1,0:T(8,128)(2,1)S(1)}, u32[]{:S(2)}, u32[]{:S(2)}) collective-permute-start(bf16[2048,128]{1,0:T(8,128)(2,1)S(1)} %get-tuple-element.75), channel_id=1, source_target_pairs={{0,64},{1,65},{2,66},{3,67},{4,68},{5,69},{6,70},{7,71},{8,72},{9,... | collective-permute-start | bytes 1572872 | tf_op jit(solution)/shard_map/ppermute | solution.py:53
  92.1 37.5 %collective-permute-start.35 = (bf16[2048,128]{1,0:T(8,128)(2,1)S(1)}, bf16[2048,128]{1,0:T(8,128)(2,1)S(1)}, u32[]{:S(2)}, u32[]{:S(2)}) collective-permute-start(bf16[2048,128]{1,0:T(8,128)(2,1)S(1)} %get-tuple-element.76), channel_id=1, source_target_pairs={{0,32},{1,33},{2,34},{3,35},{4,36},{5,37},{6,38},{7,39},{8,40},{9,... | collective-permute-start | bytes 1572872 | tf_op jit(solution)/shard_map/ppermute | solution.py:53
  92.1 37.5 %collective-permute-start.36 = (bf16[2048,128]{1,0:T(8,128)(2,1)S(1)}, bf16[2048,128]{1,0:T(8,128)(2,1)S(1)}, u32[]{:S(2)}, u32[]{:S(2)}) collective-permute-start(bf16[2048,128]{1,0:T(8,128)(2,1)S(1)} %get-tuple-element.77), channel_id=1, source_target_pairs={{0,96},{1,97},{2,98},{3,99},{4,100},{5,101},{6,102},{7,103},{8,104... | collective-permute-start | bytes 1572872 | tf_op jit(solution)/shard_map/ppermute | solution.py:53
  106.4 28.6 %collective-permute-start.37 = (bf16[2048,128]{1,0:T(8,128)(2,1)S(1)}, bf16[2048,128]{1,0:T(8,128)(2,1)S(1)}, u32[]{:S(2)}, u32[]{:S(2)}) collective-permute-start(bf16[2048,128]{1,0:T(8,128)(2,1)S(1)} %get-tuple-element.82), channel_id=1, source_target_pairs={{0,64},{1,65},{2,66},{3,67},{4,68},{5,69},{6,70},{7,71},{8,72},{9,... | collective-permute-start | bytes 1572872 | tf_op jit(solution)/shard_map/ppermute | solution.py:53
  117.8 22.0 %collective-permute-start.38 = (bf16[2048,128]{1,0:T(8,128)(2,1)S(1)}, bf16[2048,128]{1,0:T(8,128)(2,1)S(1)}, u32[]{:S(2)}, u32[]{:S(2)}) collective-permute-start(bf16[2048,128]{1,0:T(8,128)(2,1)S(1)} %get-tuple-element.83), channel_id=1, source_target_pairs={{0,32},{1,33},{2,34},{3,35},{4,36},{5,37},{6,38},{7,39},{8,40},{9,... | collective-permute-start | bytes 1572872 | tf_op jit(solution)/shard_map/ppermute | solution.py:53
  118.5 21.2 %collective-permute-start.39 = (bf16[2048,128]{1,0:T(8,128)(2,1)S(1)}, bf16[2048,128]{1,0:T(8,128)(2,1)S(1)}, u32[]{:S(2)}, u32[]{:S(2)}) collective-permute-start(bf16[2048,128]{1,0:T(8,128)(2,1)S(1)} %get-tuple-element.84), channel_id=1, source_target_pairs={{0,96},{1,97},{2,98},{3,99},{4,100},{5,101},{6,102},{7,103},{8,104... | collective-permute-start | bytes 1572872 | tf_op jit(solution)/shard_map/ppermute | solution.py:53
  (21 other events, 219.3 us)
